TPU v7x, 32 devices: a whole 2x2x4 slice. The times are simulated.
32 devices in a mesh: dp: 8 (over z, x), row: 2 (over core), col: 2 (over y).
Axes of the slice: x: 2, y: 2, z: 4, core: 2. Of those that a mesh axis runs over, the one named last changes fastest.
Arguments:
- tokens: bfloat16 [8192, 2048], P('dp', ('row', 'col')), may hold values from -6 to 6
- teacher: bfloat16 [8192, 2048], P('dp', ('row', 'col')), may hold values from -6 to 6
- segments: int32 [8192], P('dp'), may hold values from 0 to 17, as said below
- valid_mask: int32 [8192], P('dp'), may hold values from 0 to 1, as said below
- query_weight: bfloat16 [2048, 2048], P('row', 'col'), may hold values from -0.1875 to 0.1875
- key_weight: bfloat16 [2048, 2048], P('row', 'col'), may hold values from -0.1875 to 0.1875
- value_weight: bfloat16 [2048, 2048], P('row', 'col'), may hold values from -0.125 to 0.125
- output_weight: bfloat16 [2048, 2048], P('col', 'row'), may hold values from -0.5 to 0.5
- gate_weight: bfloat16 [2048, 8192], P('row', 'col'), may hold values from -0.125 to 0.125
- up_weight: bfloat16 [2048, 8192], P('row', 'col'), may hold values from -0.125 to 0.125
- down_weight: bfloat16 [8192, 2048], P('col', 'row'), may hold values from -0.09375 to 0.09375
Outputs:
- output: bfloat16 [8192, 2048], P('dp', ('row', 'col'))
- loss: float32 [], replicated
- grad_tokens: float32 [8192, 2048], P('dp', ('row', 'col'))
- grad_query: float32 [2048, 2048], P('row', 'col')
- grad_key: float32 [2048, 2048], P('row', 'col')
- grad_value: float32 [2048, 2048], P('row', 'col')
- grad_output: float32 [2048, 2048], P('col', 'row')
- grad_gate: float32 [2048, 8192], P('row', 'col')
- grad_up: float32 [2048, 8192], P('row', 'col')
- grad_down: float32 [8192, 2048], P('col', 'row')
Inputs may be any that keep to these rules, and one draw needn't show every extreme that they name: `segments`: within each sequence of 1024 tokens the segment numbers start at 0 and never fall; every segment but the last is a document of 60 to 800 tokens, and documents of exactly 60 and of exactly 800 tokens occur in every draw; the last segment of each sequence is padding of one or more tokens; some sequence in every draw reaches the largest segment number. `valid_mask`: 1 on the documents' tokens, 0 on each sequence's padding segment.
All inputs are finite; a program needn't handle non-finite values.
Results may differ from a plain program's by a relative error of at most 0.0095.
The roundings to bfloat16 on the way count: a program that leaves them out, or rounds other values in their place, can miss the bound.
Values may be sent and summed in bfloat16 or wider, within the bound.
A program may use at most 384 MiB of HBM per device.

v0:
```python
import math

import jax
import jax.numpy as jnp
from jax import lax
from jax.sharding import PartitionSpec as P

D = 2048
HEAD = 128
LEN = 1024


EPS = 1e-05
THETA = 10000.0
NEG = -1e30


def rope_tables(local_rows):
    half_width = HEAD // 2
    places = (jnp.arange(local_rows) % LEN).astype(jnp.float32)
    frequency = jnp.exp(
        jnp.arange(half_width).astype(jnp.float32) * (-2.0 * math.log(THETA) / HEAD)
    )
    angles = places[:, None] * frequency[None, :]
    return (jnp.cos(angles), jnp.sin(angles))


def rotate(operand, cosine, sine_table):
    half_width = operand.shape[-1] // 2
    front_half = operand[..., :half_width]
    back_half = operand[..., half_width:]
    cosine = cosine[:, None, :]
    sine_table = sine_table[:, None, :]
    return jnp.concatenate(
        [
            front_half * cosine - back_half * sine_table,
            back_half * cosine + front_half * sine_table,
        ],
        axis=-1,
    )


def contract_rows(left, right):
    return lax.dot_general(
        left, right, (((0,), (0,)), ((), ())), preferred_element_type=jnp.float32
    )


def contract_cols(left, right):
    return lax.dot_general(
        left, right, (((1,), (1,)), ((), ())), preferred_element_type=jnp.float32
    )


def block_scores(queries, key_heads, segments, offset, block_rows):
    anchor = offset // LEN * LEN
    query_block = lax.dynamic_slice_in_dim(queries, offset, block_rows, 0)
    query_segs = lax.dynamic_slice_in_dim(segments, offset, block_rows, 0)
    query_places = offset - anchor + jnp.arange(block_rows, dtype=jnp.int32)
    key_places = jnp.arange(LEN, dtype=jnp.int32)
    scores = jnp.einsum(
        "qhd,khd->hqk", query_block, key_heads, preferred_element_type=jnp.float32
    ) * (1.0 / math.sqrt(HEAD))
    allowed = (query_segs[:, None] == segments[None, :]) & (
        key_places[None, :] <= query_places[:, None]
    )
    return (jnp.where(allowed[None], scores, NEG), anchor, query_block, key_heads)


def attention_forward(queries, key_heads, value_heads, segments):
    local_rows = queries.shape[0]
    block_rows = min(512, LEN)
    block_total = local_rows // block_rows

    def one_block(block_index):
        offset = block_index * block_rows
        scores, anchor, query_block, key_block = block_scores(
            queries, key_heads, segments, offset, block_rows
        )
        row_max = jnp.max(scores, axis=-1, keepdims=True)
        shares = jnp.exp(scores - row_max)
        totals = jnp.sum(shares, axis=-1, keepdims=True)
        shares = shares / totals
        attended = jnp.einsum(
            "hqk,khd->qhd",
            shares.astype(jnp.bfloat16),
            value_heads,
            preferred_element_type=jnp.float32,
        )
        return (attended, (row_max + jnp.log(totals))[..., 0])

    attended, logsum = lax.map(one_block, jnp.arange(block_total, dtype=jnp.int32))
    return (attended.reshape(local_rows, queries.shape[1] * queries.shape[2]), logsum)


def attention_backward(queries, key_heads, value_heads, grad_attended, logsum, segments):
    local_rows = queries.shape[0]
    block_rows = min(512, LEN)
    block_total = local_rows // block_rows
    factor = 1.0 / math.sqrt(HEAD)
    zeros = jnp.zeros(queries.shape, jnp.float32)

    def one_block(block_index, carried):
        grad_query, grad_key, grad_value = carried
        offset = block_index * block_rows
        scores, anchor, query_block, key_block = block_scores(
            queries, key_heads, segments, offset, block_rows
        )
        grad_block = lax.dynamic_slice_in_dim(grad_attended, offset, block_rows, 0)
        shares = jnp.exp(scores - logsum[block_index][:, :, None])
        grad_shares = jnp.einsum(
            "qhd,khd->hqk", grad_block, value_heads, preferred_element_type=jnp.float32
        )
        centre = jnp.sum(shares * grad_shares, axis=-1, keepdims=True)
        grad_scores = (shares * (grad_shares - centre)).astype(jnp.bfloat16)
        query_part = (
            jnp.einsum("hqk,khd->qhd", grad_scores, key_block, preferred_element_type=jnp.float32)
            * factor
        )
        key_part = (
            jnp.einsum("hqk,qhd->khd", grad_scores, query_block, preferred_element_type=jnp.float32)
            * factor
        )
        value_part = jnp.einsum(
            "hqk,qhd->khd",
            shares.astype(jnp.bfloat16),
            grad_block,
            preferred_element_type=jnp.float32,
        )
        grad_query = lax.dynamic_update_slice_in_dim(grad_query, query_part, offset, 0)
        grad_key = grad_key + key_part
        grad_value = grad_value + value_part
        return (grad_query, grad_key, grad_value)

    return lax.fori_loop(0, block_total, one_block, (zeros, zeros, zeros))


def body(
    tokens,
    teacher,
    segments,
    valid_mask,
    query_weight,
    key_weight,
    value_weight,
    output_weight,
    gate_weight,
    up_weight,
    down_weight,
):
    local_rows = tokens.shape[0]
    total_rows = local_rows * lax.axis_size("dp")
    validity = valid_mask.astype(jnp.float32)
    token_total = lax.psum(jnp.sum(validity), "dp")

    def feature_sums(front_term, back_term):
        return lax.psum((jnp.sum(front_term, axis=1), jnp.sum(back_term, axis=1)), ("row", "col"))

    def normalize_with(operand, summing):
        summed, squares = summing(operand, operand * operand)
        average = summed / D
        factor = lax.rsqrt(squares / D - average * average + EPS)
        return ((operand - average[:, None]) * factor[:, None], factor)

    def normalize_back_with(gradient, normed, factor, summing):
        summed, crossed = summing(gradient, gradient * normed)
        return factor[:, None] * (gradient - summed[:, None] / D - normed * (crossed[:, None] / D))

    def gather_cols(operand):
        return lax.all_gather(operand, "col", axis=1, tiled=True)

    def sum_cols(operand):
        return lax.psum_scatter(operand, "col", scatter_dimension=1, tiled=True)

    def sum_rows(operand):
        return lax.psum_scatter(operand, "row", scatter_dimension=1, tiled=True)

    def gather_rows(operand):
        return lax.all_gather(operand, "row", axis=1, tiled=True)

    tokens_f = tokens.astype(jnp.float32)
    teacher_f = teacher.astype(jnp.float32)
    normed, factor_one = normalize_with(tokens_f, feature_sums)
    normed_cols = gather_cols(normed.astype(jnp.bfloat16))
    queries, key_heads, value_heads = (
        lax.psum_scatter(
            jnp.dot(normed_cols, query_weight, preferred_element_type=jnp.float32),
            "row",
            scatter_dimension=1,
            tiled=True,
        ),
        lax.psum_scatter(
            jnp.dot(normed_cols, key_weight, preferred_element_type=jnp.float32),
            "row",
            scatter_dimension=1,
            tiled=True,
        ),
        lax.psum_scatter(
            jnp.dot(normed_cols, value_weight, preferred_element_type=jnp.float32),
            "row",
            scatter_dimension=1,
            tiled=True,
        ),
    )
    local_heads = queries.shape[1] // HEAD
    cosine, sine_table = rope_tables(local_rows)
    query_low = rotate(queries.reshape(local_rows, local_heads, HEAD), cosine, sine_table).astype(
        jnp.bfloat16
    )
    key_low = rotate(key_heads.reshape(local_rows, local_heads, HEAD), cosine, sine_table).astype(
        jnp.bfloat16
    )
    value_low = value_heads.reshape(local_rows, local_heads, HEAD).astype(jnp.bfloat16)
    attended, logsum = attention_forward(query_low, key_low, value_low, segments)
    attended_rows = gather_rows(attended.astype(jnp.bfloat16))
    branch_part = jnp.dot(attended_rows, output_weight, preferred_element_type=jnp.float32)
    hidden = tokens_f + sum_cols(branch_part)
    normed_two, factor_two = normalize_with(hidden, feature_sums)
    hidden_cols = gather_cols(normed_two.astype(jnp.bfloat16))
    gate_out, up_out = (
        lax.psum_scatter(
            jnp.dot(hidden_cols, gate_weight, preferred_element_type=jnp.float32),
            "row",
            scatter_dimension=1,
            tiled=True,
        ),
        lax.psum_scatter(
            jnp.dot(hidden_cols, up_weight, preferred_element_type=jnp.float32),
            "row",
            scatter_dimension=1,
            tiled=True,
        ),
    )
    sigmoid_gate = jax.nn.sigmoid(gate_out)
    activated = gate_out * sigmoid_gate
    act_rows = gather_rows((activated * up_out).astype(jnp.bfloat16))
    down_part = jnp.dot(act_rows, down_weight, preferred_element_type=jnp.float32)
    result = hidden + sum_cols(down_part)
    error_term = result - teacher_f
    loss_value = (
        lax.psum(0.5 * jnp.sum(validity[:, None] * error_term * error_term), ("dp", "row", "col"))
        / token_total
    )
    scale = total_rows / token_total
    grad_result = scale * validity[:, None] * error_term
    result_cols = gather_cols(grad_result.astype(jnp.bfloat16))
    grad_down = contract_rows(act_rows, result_cols)
    grad_act = sum_rows(contract_cols(result_cols, down_weight))
    gate_back = (grad_act * up_out * sigmoid_gate * (1.0 + gate_out * (1.0 - sigmoid_gate))).astype(
        jnp.bfloat16
    )
    up_back = (grad_act * activated).astype(jnp.bfloat16)
    gate_rows, up_rows = (
        lax.all_gather(gate_back, "row", axis=1, tiled=True),
        lax.all_gather(up_back, "row", axis=1, tiled=True),
    )
    grad_gate = contract_rows(hidden_cols, gate_rows)
    grad_up = contract_rows(hidden_cols, up_rows)
    normed_two_part = contract_cols(gate_rows, gate_weight) + contract_cols(up_rows, up_weight)
    grad_normed_two = sum_cols(normed_two_part)
    grad_hidden = grad_result + normalize_back_with(
        grad_normed_two, normed_two, factor_two, feature_sums
    )
    hidden_grad_cols = gather_cols(grad_hidden.astype(jnp.bfloat16))
    grad_output = contract_rows(attended_rows, hidden_grad_cols)
    grad_attended = sum_rows(contract_cols(hidden_grad_cols, output_weight)).astype(jnp.bfloat16)
    grad_query_rot, grad_key_rot, grad_value_heads = attention_backward(
        query_low,
        key_low,
        value_low,
        grad_attended.reshape(local_rows, local_heads, HEAD),
        logsum,
        segments,
    )
    query_back = (
        rotate(grad_query_rot, cosine, -sine_table).reshape(local_rows, -1).astype(jnp.bfloat16)
    )
    key_back = (
        rotate(grad_key_rot, cosine, -sine_table).reshape(local_rows, -1).astype(jnp.bfloat16)
    )
    value_back = grad_value_heads.reshape(local_rows, -1).astype(jnp.bfloat16)
    query_rows, key_rows, value_rows = (
        lax.all_gather(query_back, "row", axis=1, tiled=True),
        lax.all_gather(key_back, "row", axis=1, tiled=True),
        lax.all_gather(value_back, "row", axis=1, tiled=True),
    )
    grad_query = contract_rows(normed_cols, query_rows)
    grad_key = contract_rows(normed_cols, key_rows)
    grad_value = contract_rows(normed_cols, value_rows)
    grad_normed = sum_cols(
        contract_cols(query_rows, query_weight)
        + contract_cols(key_rows, key_weight)
        + contract_cols(value_rows, value_weight)
    )
    grad_tokens = grad_hidden + normalize_back_with(grad_normed, normed, factor_one, feature_sums)
    grad_query, grad_key, grad_value, grad_output, grad_gate, grad_up, grad_down = lax.psum(
        (grad_query, grad_key, grad_value, grad_output, grad_gate, grad_up, grad_down), "dp"
    )
    return (
        result.astype(jnp.bfloat16),
        loss_value,
        grad_tokens,
        grad_query,
        grad_key,
        grad_value,
        grad_output,
        grad_gate,
        grad_up,
        grad_down,
    )


def solution(mesh):
    in_specs = (
        P("dp", ("row", "col")),
        P("dp", ("row", "col")),
        P("dp"),
        P("dp"),
        P("row", "col"),
        P("row", "col"),
        P("row", "col"),
        P("col", "row"),
        P("row", "col"),
        P("row", "col"),
        P("col", "row"),
    )
    out_specs = (
        P("dp", ("row", "col")),
        P(),
        P("dp", ("row", "col")),
        P("row", "col"),
        P("row", "col"),
        P("row", "col"),
        P("col", "row"),
        P("row", "col"),
        P("row", "col"),
        P("col", "row"),
    )
    return jax.shard_map(body, mesh=mesh, in_specs=in_specs, out_specs=out_specs, check_vma=False)
```

profile of v0, /device:TPU:0, one launch (start us, length us, event | category | flops | bytes accessed | tf_op | source)
XLA Modules:
  0.0 2929.7 jit_solution(9221369113226071031)
XLA Ops:
  9.0 9.1 all-reduce.4
  21.3 34.1 %all-gather.12.cloned.1.call-done = bf16[1024,1024]{1,0:T(8,128)(2,1)} async-done(((bf16[1024,512]{1,0:T(8,128)(2,1)}), bf16[1024,1024]{1,0:T(8,128)(2,1)}) %all-gather.12.cloned.1.call-update) | async-done | bytes 2097168 | tf_op jit(solution)/shard_map/all_gather | solution.py:170
  55.3 6.6 fusion.54
  62.0 6.6 fusion.53
  68.7 7.0 fusion.55
  80.7 9.8 reduce-scatter.12.cloned.1.call-done
  100.3 6.2 reduce-scatter.16.cloned.1.call-done
  109.2 23.2 while.34
  136.1 12.0 all-gather.14.cloned.1.call-done
  154.1 55.6 %reduce-scatter.18.cloned.1.call-done = f32[1024,512]{1,0:T(8,128)} async-done(((f32[1024,1024]{1,0:T(8,128)}), f32[1024,512]{1,0:T(8,128)}) %reduce-scatter.18.cloned.1.call-update) | async-done | bytes 2097168 | tf_op jit(solution)/shard_map/reduce_scatter | solution.py:173
  212.7 6.4 all-reduce.3
  223.0 34.7 %all-gather.16.cloned.1.call-done = bf16[1024,1024]{1,0:T(8,128)(2,1)} async-done(((bf16[1024,512]{1,0:T(8,128)(2,1)}), bf16[1024,1024]{1,0:T(8,128)(2,1)}) %all-gather.16.cloned.1.call-update) | async-done | bytes 2097168 | tf_op jit(solution)/shard_map/all_gather | solution.py:170
  257.7 16.1 fusion.58
  273.9 18.3 fusion.57
  292.3 8.1 reduce-scatter.22.cloned.1.call-done
  300.3 30.6 %reduce-scatter.20.cloned.1.call-done = f32[1024,2048]{1,0:T(8,128)} async-done(((f32[1024,4096]{1,0:T(8,128)}), f32[1024,2048]{1,0:T(8,128)}) %reduce-scatter.20.cloned.1.call-update) | async-done | bytes 8388624 | tf_op jit(solution)/shard_map/reduce_scatter | solution.py:221
  330.9 8.7 multiply_convert_fusion.3
  339.7 21.2 all-gather.18.cloned.1.call-done
  360.9 15.0 fusion.59
  377.1 22.2 psum.124
  400.0 31.4 %reduce-scatter.24.cloned.1.call-done = f32[1024,512]{1,0:T(8,128)} async-done(((f32[1024,1024]{1,0:T(8,128)}), f32[1024,512]{1,0:T(8,128)}) %reduce-scatter.24.cloned.1.call-update) | async-done | bytes 2097168 | tf_op jit(solution)/shard_map/reduce_scatter | solution.py:173
  435.5 32.8 %all-gather.20.cloned.1.call-done = bf16[1024,1024]{1,0:T(8,128)(2,1)} async-done(((bf16[1024,512]{1,0:T(8,128)(2,1)}), bf16[1024,1024]{1,0:T(8,128)(2,1)}) %all-gather.20.cloned.1.call-update) | async-done | bytes 2097168 | tf_op jit(solution)/shard_map/all_gather | solution.py:170
  468.3 16.2 fusion.60
  484.6 26.4 reduce-scatter.26.cloned.1.call-done
  511.0 12.9 multiply_convert_fusion.1
  524.7 20.4 all-gather.22.cloned.1.call-done
  545.1 15.0 fusion.61
  560.2 8.0 all-gather.24.cloned.1.call-done
  568.1 15.7 convolution_add_fusion
  583.9 55.6 %reduce-scatter.28.cloned.1.call-done = f32[1024,512]{1,0:T(8,128)} async-done(((f32[1024,1024]{1,0:T(8,128)}), f32[1024,512]{1,0:T(8,128)}) %reduce-scatter.28.cloned.1.call-update) | async-done | bytes 2097168 | tf_op jit(solution)/shard_map/reduce_scatter | solution.py:173
  643.7 6.4 all-reduce.2
  655.0 35.0 %all-gather.26.cloned.1.call-done = bf16[1024,1024]{1,0:T(8,128)(2,1)} async-done(((bf16[1024,512]{1,0:T(8,128)(2,1)}), bf16[1024,1024]{1,0:T(8,128)(2,1)}) %all-gather.26.cloned.1.call-update) | async-done | bytes 2097168 | tf_op jit(solution)/shard_map/all_gather | solution.py:170
  696.3 11.9 reduce-scatter.30.cloned.1.call-done
  714.7 46.0 %while.35 = (s32[]{:T(128)}, f32[1024,4,128]{0,2,1:T(8,128)}, f32[1024,4,128]{0,2,1:T(8,128)S(1)}, f32[1024,4,128]{0,2,1:T(8,128)}, s32[1024]{0:T(1024)S(1)}, /*...) while((s32[]{:T(128)}, f32[1024,4,128]{0,2,1:T(8,128)}, ...), condition=%wide.region_32.33_spmd.clone, body=%wide.region_30.32_spmd.clone.sunk | while | flops 2720266752 | bytes 93395416 | solution.py:135
  768.6 7.5 all-gather.28.cloned.1.call-done
  782.0 7.8 all-gather.30.cloned.1.call-done
  789.8 6.6 fusion.64
  796.4 7.3 all-gather.32.cloned.1.call-done
  803.7 8.5 add_add_fusion
  812.4 16.4 fusion.71
  828.8 14.8 fusion.70
  843.6 15.2 fusion.69
  877.4 46.7 %psum.123 = f32[]{:T(128)} all-reduce(f32[]{:T(128)S(6)} %mul_shard_map.3), channel_id=1, replica_groups=mesh['dp'=8,'row'=2,'col'=2] {'dp','row','col'}, use_global_device_ids=true, to_apply=%region_20.21 | all-reduce | flops 1 | bytes 8 | tf_op jit(solution)/shard_map/psum | solution.py:241
  928.1 8.8 all-reduce.1
  940.4 1933.7 %all-reduce.7.cloned.1.call-done = (f32[1024,1024]{1,0:T(8,128)}, f32[1024,1024]{1,0:T(8,128)}, f32[1024,1024]{1,0:T(8,128)}, f32[1024,1024]{1,0:T(8,128)}, f32[...) async-done(((f32[1024,1024]{1,0:T(8,128)}, f32[1024,1024]{1,0:T(8,128)}, f32[1024,1024]{1,0:T(8,128)}, f32[1024,1024]{1,0:T(8,128)}, ...) | async-done | bytes 67108880 | tf_op jit(solution)/shard_map/psum | solution.py:296
  2888.6 14.0 copy.121
  2904.6 8.5 copy.122
  2915.5 6.3 copy.123
  (249 shorter events, 191.8 us)
Async XLA Ops:
  7.2 140.9 %copy-start = (bf16[1024,1024]{1,0:T(8,128)(2,1)S(1)}, bf16[1024,1024]{1,0:T(8,128)(2,1)}, u32[]{:S(2)}) copy-start(bf16[1024,1024]{1,0:T(8,128)(2,1)} %param.22) | copy-start | bytes 6291460
  7.2 48.2 %all-gather.12.cloned.1.call-start = ((), (), s32[]{:S(2)}) async-start(), calls=%async_computation.11 | async-start | bytes 3145728 | tf_op jit(solution)/shard_map/all_gather | solution.py:170
  21.2 56.5 %reduce-scatter.14.cloned.1.call-start = ((), (), s32[]{:S(2)}) async-start(), calls=%async_computation.13 | async-start | bytes 6291456 | tf_op jit(solution)/shard_map/reduce_scatter | solution.py:192
  61.9 28.5 reduce-scatter.12.cloned.1.call-start
  68.7 37.9 %reduce-scatter.16.cloned.1.call-start = ((), (), s32[]{:S(2)}) async-start(), calls=%async_computation.14 | async-start | bytes 6291456 | tf_op jit(solution)/shard_map/reduce_scatter | solution.py:198
  75.7 72.4 %all-gather.14.cloned.1.call-start = ((), (), s32[]{:S(2)}) async-start(), calls=%async_computation.15 | async-start | bytes 3145728 | tf_op jit(solution)/shard_map/all_gather | solution.py:179
  77.7 15.6 copy-start.13
  100.3 8.9 copy-start.17
  136.0 73.6 %reduce-scatter.18.cloned.1.call-start = ((), (), s32[]{:S(2)}) async-start(), calls=%async_computation.16 | async-start | bytes 6291456 | tf_op jit(solution)/shard_map/reduce_scatter | solution.py:173
  154.0 55.6 %copy-start.7 = (bf16[1024,512]{1,0:T(8,128)(2,1)S(1)}, bf16[1024,512]{1,0:T(8,128)(2,1)}, u32[]{:S(2)}) copy-start(bf16[1024,512]{1,0:T(8,128)(2,1)} %param.15) | copy-start | bytes 3145732
  154.0 103.7 %all-gather.16.cloned.1.call-start = ((), (), s32[]{:S(2)}) async-start(), calls=%async_computation.17 | async-start | bytes 3145728 | tf_op jit(solution)/shard_map/all_gather | solution.py:170
  222.7 77.6 %reduce-scatter.22.cloned.1.call-start = ((), (), s32[]{:S(2)}) async-start(), calls=%async_computation.19 | async-start | bytes 25165824 | tf_op jit(solution)/shard_map/reduce_scatter | solution.py:227
  273.9 57.0 %reduce-scatter.20.cloned.1.call-start = ((), (), s32[]{:S(2)}) async-start(), calls=%async_computation.18 | async-start | bytes 25165824 | tf_op jit(solution)/shard_map/reduce_scatter | solution.py:221
  292.2 68.7 %all-gather.18.cloned.1.call-start = ((), (), s32[]{:S(2)}) async-start(), calls=%async_computation.20 | async-start | bytes 12582912 | tf_op jit(solution)/shard_map/all_gather | solution.py:179
  339.6 91.8 %reduce-scatter.24.cloned.1.call-start = ((), (), s32[]{:S(2)}) async-start(), calls=%async_computation.21 | async-start | bytes 6291456 | tf_op jit(solution)/shard_map/reduce_scatter | solution.py:173
  375.8 55.6 %copy-start.9 = (bf16[1024,512]{1,0:T(8,128)(2,1)S(1)}, bf16[1024,512]{1,0:T(8,128)(2,1)}, u32[]{:S(2)}) copy-start(bf16[1024,512]{1,0:T(8,128)(2,1)} %param.16) | copy-start | bytes 3145732
  375.9 92.4 %all-gather.20.cloned.1.call-start = ((), (), s32[]{:S(2)}) async-start(), calls=%async_computation.22 | async-start | bytes 3145728 | tf_op jit(solution)/shard_map/all_gather | solution.py:170
  435.0 76.0 %reduce-scatter.26.cloned.1.call-start = ((), (), s32[]{:S(2)}) async-start(), calls=%async_computation.23 | async-start | bytes 25165824 | tf_op jit(solution)/shard_map/reduce_scatter | solution.py:176
  484.5 60.6 %all-gather.22.cloned.1.call-start = ((), (), s32[]{:S(2)}) async-start(), calls=%async_computation.24 | async-start | bytes 12582912 | tf_op jit(solution)/shard_map/all_gather | solution.py:254
  523.9 44.3 %all-gather.24.cloned.1.call-start = ((), (), s32[]{:S(2)}) async-start(), calls=%async_computation.25 | async-start | bytes 12582912 | tf_op jit(solution)/shard_map/all_gather | solution.py:255
  524.5 115.0 %reduce-scatter.28.cloned.1.call-start = ((), (), s32[]{:S(2)}) async-start(), calls=%async_computation.26 | async-start | bytes 6291456 | tf_op jit(solution)/shard_map/reduce_scatter | solution.py:173
  583.8 55.7 %copy-start.26 = (f32[1024]{0:T(1024)S(1)}, f32[1024]{0:T(1024)}, u32[]{:S(2)}) copy-start(f32[1024]{0:T(1024)} %copy-done.25) | copy-start | bytes 12292
  583.8 55.7 %copy-start.28 = (f32[1024]{0:T(1024)S(1)}, f32[1024]{0:T(1024)}, u32[]{:S(2)}) copy-start(f32[1024]{0:T(1024)} %copy-done.27) | copy-start | bytes 12292
  583.8 106.2 %all-gather.26.cloned.1.call-start = ((), (), s32[]{:S(2)}) async-start(), calls=%async_computation.27 | async-start | bytes 3145728 | tf_op jit(solution)/shard_map/all_gather | solution.py:170
  655.0 53.2 %reduce-scatter.30.cloned.1.call-start = ((), (), s32[]{:S(2)}) async-start(), calls=%async_computation.28 | async-start | bytes 6291456 | tf_op jit(solution)/shard_map/reduce_scatter | solution.py:176
  696.0 80.1 %all-gather.28.cloned.1.call-start = ((), (), s32[]{:S(2)}) async-start(), calls=%async_computation.29 | async-start | bytes 3145728 | tf_op jit(solution)/shard_map/all_gather | solution.py:283
  714.7 46.0 %copy-start.14 = (f32[1024,64]{0,1:T(8,128)S(1)}, f32[1024,64]{0,1:T(8,128)}, u32[]{:S(2)}) copy-start(f32[1024,64]{0,1:T(8,128)} %copy-done.13) | copy-start | bytes 786436
  764.0 25.8 all-gather.30.cloned.1.call-start
  765.1 38.6 %all-gather.32.cloned.1.call-start = ((), (), s32[]{:S(2)}) async-start(), calls=%async_computation.31 | async-start | bytes 3145728 | tf_op jit(solution)/shard_map/all_gather | solution.py:285
  765.2 10.9 copy-start.30
  768.1 157.4 %reduce-scatter.32.cloned.1.call-start = ((), (), s32[]{:S(2)}) async-start(), calls=%async_computation.32 | async-start | bytes 6291456 | tf_op jit(solution)/shard_map/reduce_scatter | solution.py:173
  782.0 21.7 copy-start.31
  812.2 16.6 copy-start.34
  812.2 2061.9 %all-reduce.7.cloned.1.call-start = ((), (), s32[]{:S(2)}) async-start(), calls=%async_computation.33 | async-start | bytes 134217728 | tf_op jit(solution)/shard_map/psum | solution.py:296
  843.6 15.2 copy-start.33
  843.6 15.2 copy-start.35
  876.6 48.8 %copy-start.8 = (bf16[1024,512]{1,0:T(8,128)(2,1)S(1)}, bf16[1024,512]{1,0:T(8,128)(2,1)}, u32[]{:S(2)}) copy-start(bf16[1024,512]{1,0:T(8,128)(2,1)} %param.15) | copy-start | bytes 3145732
  876.6 48.8 %copy-start.22 = (f32[1024]{0:T(1024)S(1)}, f32[1024]{0:T(1024)}, u32[]{:S(2)}) copy-start(f32[1024]{0:T(1024)} %copy-done.21) | copy-start | bytes 12292
  876.6 48.9 %copy-start.24 = (f32[1024]{0:T(1024)S(1)}, f32[1024]{0:T(1024)}, u32[]{:S(2)}) copy-start(f32[1024]{0:T(1024)} %copy-done.23) | copy-start | bytes 12292
  2886.5 16.1 slice-start.4
  2888.6 14.0 slice-start.5
  2888.6 14.1 slice-start.6
  2888.6 16.0 slice-start.7
  2888.6 24.5 slice-start
  2888.6 24.5 slice-start.1
  2904.6 9.6 slice-start.2
  2904.6 10.9 slice-start.3
  2915.5 6.3 copy-start.1
  (27 other events, 76.9 us)
Sparse Core Ops, SparseCore 0:
  21.3 33.9 all-gather.11
  62.1 12.0 reduce-scatter.13
  77.1 13.3 reduce-scatter.11
  93.2 13.3 reduce-scatter.15
  136.2 11.8 all-gather.13
  154.1 55.4 reduce-scatter.17
  222.8 34.8 all-gather.15
  274.0 26.2 reduce-scatter.21
  303.3 27.5 reduce-scatter.19
  339.8 21.0 all-gather.17
  376.0 55.4 reduce-scatter.23
  435.1 33.1 all-gather.19
  484.7 26.2 reduce-scatter.25
  524.0 21.0 all-gather.21
  547.1 21.0 all-gather.23
  583.9 55.4 reduce-scatter.27
  655.1 34.8 all-gather.25
  696.1 12.0 reduce-scatter.29
  764.1 11.8 all-gather.27
  778.0 11.7 all-gather.29
  791.9 11.7 all-gather.31
  812.3 55.4 reduce-scatter.31
  876.8 1997.2 all-reduce.6
where the time goes:
time: 2940 us; the launch traced here: 2930 us
  waiting for transfers between devices  2390 us (81%)
  matrix products  254 us (9%)
  blocking collectives  99.6 us (3%)
  other arithmetic  81.6 us (3%)
  local copies, waits for them, and re-layouts  81.2 us (3%)
    psum x1, waiting for transfers between devices, body(): lax.psum((grad_query, grad_key, grad_value, grad_output, grad_gate, grad_...  1930 us
    reduce_scatter x4, waiting for transfers between devices, sum_cols(): return lax.psum_scatter(operand, 'col', scatter_dimension=1, tiled=True)  143 us
    all_gather x4, waiting for transfers between devices, gather_cols(): return lax.all_gather(operand, 'col', axis=1, tiled=True)  137 us
    dot_general x7, matrix products, contract_cols(): lax.dot_general(left, right, (((1,), (1,)), ((), ())), preferred_element_...  73.9 us
    dot_general x7, matrix products, contract_rows(): lax.dot_general(left, right, (((0,), (0,)), ((), ())), preferred_element_...  64.1 us
  transfers between devices with their start and end apart: 23, of which 21 were waited for; matrix products, arithmetic and copies ran while one was open for 5% of the time, Pallas kernels for 0%

commit v1 on v0

v1 whole, which is shorter than its diff:
```python
import functools
import math

import jax
import jax.numpy as jnp
from jax import lax
from jax.experimental import pallas as pl
from jax.experimental.pallas import tpu as pltpu
from jax.sharding import PartitionSpec as P

D = 2048
HEAD = 128
LEN = 1024
EPS = 1e-05
THETA = 10000.0
NEG = -1e30
CHUNKS = 2

BF = jnp.bfloat16
F32 = jnp.float32


def rope_tables(places):
    half_width = HEAD // 2
    frequency = jnp.exp(
        jnp.arange(half_width).astype(F32) * (-2.0 * math.log(THETA) / HEAD)
    )
    angles = places.astype(F32)[:, None] * frequency[None, :]
    return (jnp.cos(angles), jnp.sin(angles))


def rotate(operand, cosine, sine_table):
    half_width = operand.shape[-1] // 2
    front_half = operand[..., :half_width]
    back_half = operand[..., half_width:]
    cosine = cosine[:, None, :]
    sine_table = sine_table[:, None, :]
    return jnp.concatenate(
        [
            front_half * cosine - back_half * sine_table,
            back_half * cosine + front_half * sine_table,
        ],
        axis=-1,
    )


def dot(left, right):
    return jnp.dot(left, right, preferred_element_type=F32)


def contract_rows(left, right):
    return lax.dot_general(left, right, (((0,), (0,)), ((), ())), preferred_element_type=F32)


def contract_cols(left, right):
    return lax.dot_general(left, right, (((1,), (1,)), ((), ())), preferred_element_type=F32)


def take(operand, index, size, axis):
    return lax.dynamic_slice_in_dim(operand, index * size, size, axis)


def swap_halves(operand, axis):
    half = operand.shape[axis] // 2
    return jnp.concatenate(
        [
            lax.slice_in_dim(operand, half, 2 * half, axis=axis),
            lax.slice_in_dim(operand, 0, half, axis=axis),
        ],
        axis=axis,
    )


def ordered(first, mine, other, axis):
    return jnp.concatenate(
        [jnp.where(first, mine, other), jnp.where(first, other, mine)], axis=axis
    )


def add_low(left, right):
    return (left.astype(F32) + right.astype(F32)).astype(BF)


MESH = pl.DeviceIdType.MESH


def line_kernel(sizes, spots, chunk, lag, ahead, deep, *refs):
    count = len(sizes)
    pieces = refs[:count]
    out = refs[count]
    held, got_in, got_mid, load, send_in, send_mid, send_out, send_side, in_sem, mid_sem, out_sem, side_sem, keep = refs[count + 1:]
    places = lax.axis_size("dp") // 2
    dp = lax.axis_index("dp")
    row = lax.axis_index("row")
    col = lax.axis_index("col")
    place, side = dp // 2, dp % 2
    half = places // 2
    low = place < half
    depth = jnp.where(low, place, places - 1 - place)
    is_mid = depth == half - 1
    is_end = depth == 0
    to_in = jnp.where(low, place + 1, place - 1)
    to_out = jnp.where(low, place - 1, place + 1)
    inner = (to_in * 2 + side, row, col)
    outer = (jnp.clip(to_out, 0, places - 1) * 2 + side, row, col)
    other = (dp + 1 - 2 * side, row, col)
    total_rows = held.shape[0]
    steps = total_rows // chunk

    loads = []
    for i in range(count):
        rows = sizes[i]
        at = pl.multiple_of(spots[i](row), 16)
        loads.append(pltpu.make_async_copy(pieces[i], held.at[pl.ds(at, rows)], load.at[i]))
        loads[-1].start()

    barrier = pltpu.get_barrier_semaphore()
    pl.semaphore_signal(barrier, inc=1, device_id=inner, device_id_type=MESH)
    pl.semaphore_signal(barrier, inc=1, device_id=other, device_id_type=MESH)

    @pl.when(jnp.logical_not(is_end))
    def _():
        pl.semaphore_signal(barrier, inc=1, device_id=outer, device_id_type=MESH)
        pl.semaphore_wait(barrier, 3)

    @pl.when(is_end)
    def _():
        pl.semaphore_wait(barrier, 2)

    for copy in loads:
        copy.wait()

    def at(t):
        return pl.ds(pl.multiple_of(t * chunk, chunk), chunk)

    def inward(t):
        return pltpu.make_async_remote_copy(
            src_ref=held.at[at(t)], dst_ref=got_in.at[at(t)], send_sem=send_in.at[t],
            recv_sem=in_sem.at[t], device_id=inner, device_id_type=MESH)

    def middle(t):
        return pltpu.make_async_remote_copy(
            src_ref=held.at[at(t)], dst_ref=got_mid.at[at(t)], send_sem=send_mid.at[t],
            recv_sem=mid_sem.at[t], device_id=inner, device_id_type=MESH)

    def outward(t, source):
        return pltpu.make_async_remote_copy(
            src_ref=source, dst_ref=out.at[side, at(t)], send_sem=send_out.at[t],
            recv_sem=out_sem.at[t], device_id=outer, device_id_type=MESH)

    def across(t, source):
        return pltpu.make_async_remote_copy(
            src_ref=source, dst_ref=out.at[side, at(t)], send_sem=send_side.at[t],
            recv_sem=side_sem.at[t], device_id=other, device_id_type=MESH)

    def store(t):
        return pltpu.make_async_copy(got_in.at[at(t)], out.at[side, at(t)], keep.at[t])

    def mid_loop(t, _):
        @pl.when(t < steps)
        def _():
            @pl.when(jnp.logical_not(is_end))
            def _():
                inward(t).wait_recv()
                held[at(t)] = (held[at(t)].astype(F32) + got_in[at(t)].astype(F32)).astype(BF)
            @pl.when(t >= deep)
            def _():
                middle(t - deep).wait_send()
            middle(t).start()

        @pl.when(t >= ahead)
        def _():
            u = t - ahead
            middle(u).wait_recv()
            got_in[at(u)] = (held[at(u)].astype(F32) + got_mid[at(u)].astype(F32)).astype(BF)
            store(u).start()
            @pl.when(u >= deep)
            def _():
                @pl.when(jnp.logical_not(is_end))
                def _():
                    outward(u - deep, got_in.at[at(u)]).wait_send()
                across(u - deep, got_in.at[at(u)]).wait_send()
            @pl.when(jnp.logical_not(is_end))
            def _():
                outward(u, got_in.at[at(u)]).start()
            across(u, got_in.at[at(u)]).start()
        return 0

    def far_loop(t, _):
        @pl.when(t < steps)
        def _():
            @pl.when(jnp.logical_not(is_end))
            def _():
                inward(t).wait_recv()
                held[at(t)] = (held[at(t)].astype(F32) + got_in[at(t)].astype(F32)).astype(BF)
            @pl.when(t >= deep)
            def _():
                inward(t - deep).wait_send()
            inward(t).start()

        @pl.when(t >= lag)
        def _():
            u = t - lag
            outward(u, out.at[side, at(u)]).wait_recv()
            @pl.when(u >= deep)
            def _():
                @pl.when(jnp.logical_not(is_end))
                def _():
                    outward(u - deep, out.at[side, at(u)]).wait_send()
                across(u - deep, out.at[side, at(u)]).wait_send()
            @pl.when(jnp.logical_not(is_end))
            def _():
                outward(u, out.at[side, at(u)]).start()
            across(u, out.at[side, at(u)]).start()
        return 0

    @pl.when(is_mid)
    def _():
        lax.fori_loop(0, steps + ahead, mid_loop, 0)
        def finish(t, _):
            store(t).wait()
            across(t, got_in.at[at(t)]).wait_recv()
            @pl.when(t >= steps - deep)
            def _():
                middle(t).wait_send()
                across(t, got_in.at[at(t)]).wait_send()
                @pl.when(jnp.logical_not(is_end))
                def _():
                    outward(t, got_in.at[at(t)]).wait_send()
            return 0
        lax.fori_loop(0, steps, finish, 0)

    @pl.when(jnp.logical_not(is_mid))
    def _():
        lax.fori_loop(0, steps + lag, far_loop, 0)
        def finish(t, _):
            across(t, out.at[side, at(t)]).wait_recv()
            @pl.when(t >= steps - deep)
            def _():
                inward(t).wait_send()
                across(t, out.at[side, at(t)]).wait_send()
                @pl.when(jnp.logical_not(is_end))
                def _():
                    outward(t, out.at[side, at(t)]).wait_send()
            return 0
        lax.fori_loop(0, steps, finish, 0)


def line_sum(pieces, spots, chunk, lag=8, ahead=2, deep=2):
    sizes = [p.shape[0] for p in pieces]
    rows, width = sum(sizes), pieces[0].shape[1]
    steps = rows // chunk
    dma = pltpu.SemaphoreType.DMA
    return pl.pallas_call(
        functools.partial(line_kernel, sizes, spots, chunk, lag, ahead, deep),
        out_shape=jax.ShapeDtypeStruct((2, rows, width), BF),
        in_specs=[pl.BlockSpec(memory_space=pl.ANY)] * len(pieces),
        out_specs=pl.BlockSpec(memory_space=pl.ANY),
        scratch_shapes=[pltpu.VMEM((rows, width), BF)] * 3 + [dma((len(pieces),))] + [dma((steps,))] * 9,
        compiler_params=pltpu.CompilerParams(collective_id=0, has_side_effects=True, vmem_limit_bytes=56 * 2**20),
        name="line_sum",
    )(*pieces)


def pack(operand, width):
    rows, columns = operand.shape
    if columns == width:
        return operand
    if columns > width:
        return jnp.concatenate(
            [operand[:, i : i + width] for i in range(0, columns, width)], axis=0
        )
    times = width // columns
    step = rows // times
    return jnp.concatenate([operand[i * step : (i + 1) * step] for i in range(times)], axis=1)


def unpack(operand, columns):
    rows, width = operand.shape
    if columns == width:
        return operand
    if columns > width:
        step = rows * width // columns
        return jnp.concatenate(
            [operand[i * step : (i + 1) * step] for i in range(columns // width)], axis=1
        )
    return jnp.concatenate(
        [operand[:, i : i + columns] for i in range(0, width, columns)], axis=0
    )


def butterfly(operand, axis):
    size = lax.axis_size(axis)
    step = 1
    while step < size:
        operand = operand + lax.ppermute(operand, axis, [(i, i ^ step) for i in range(size)])
        step *= 2
    return operand


def allowed_pairs(query_segs, query_places, key_segs, key_places):
    return (query_segs[:, None] == key_segs[None, :]) & (
        key_places[None, :] <= query_places[:, None]
    )


def attend(queries, key_heads, value_heads, allowed):
    scores = jnp.einsum("qhd,khd->hqk", queries, key_heads, preferred_element_type=F32)
    scores = jnp.where(allowed[None], scores * (1.0 / math.sqrt(HEAD)), NEG)
    row_max = jnp.max(scores, axis=-1, keepdims=True)
    shares = jnp.exp(scores - row_max)
    totals = jnp.sum(shares, axis=-1, keepdims=True)
    shares = (shares / totals).astype(BF)
    attended = jnp.einsum("hqk,khd->qhd", shares, value_heads, preferred_element_type=F32)
    return attended.astype(BF), row_max + jnp.log(totals)


def attend_back(queries, key_heads, value_heads, allowed, logsum, gradient):
    factor = 1.0 / math.sqrt(HEAD)
    scores = jnp.einsum("qhd,khd->hqk", queries, key_heads, preferred_element_type=F32)
    scores = jnp.where(allowed[None], scores * factor, NEG)
    shares = jnp.exp(scores - logsum)
    grad_shares = jnp.einsum("qhd,khd->hqk", gradient, value_heads, preferred_element_type=F32)
    centre = jnp.sum(shares * grad_shares, axis=-1, keepdims=True)
    grad_scores = (shares * (grad_shares - centre)).astype(BF)
    grad_q = jnp.einsum("hqk,khd->qhd", grad_scores, key_heads, preferred_element_type=F32)
    grad_k = jnp.einsum("hqk,qhd->khd", grad_scores, queries, preferred_element_type=F32)
    grad_v = jnp.einsum("hqk,qhd->khd", shares.astype(BF), gradient, preferred_element_type=F32)
    return grad_q * factor, grad_k * factor, grad_v


def moments(operand):
    average = jnp.mean(operand, axis=-1, keepdims=True)
    centre = operand - average
    factor = lax.rsqrt(jnp.mean(centre * centre, axis=-1, keepdims=True) + EPS)
    return average, factor


def normalize_back(gradient, normed, factor):
    mean = jnp.mean(gradient, axis=-1, keepdims=True)
    crossed = jnp.mean(gradient * normed, axis=-1, keepdims=True)
    return factor * (gradient - mean - normed * crossed)


def body(
    tokens,
    teacher,
    segments,
    valid_mask,
    query_weight,
    key_weight,
    value_weight,
    output_weight,
    gate_weight,
    up_weight,
    down_weight,
):
    rows = tokens.shape[0]
    cols = lax.axis_size("col")
    row = lax.axis_index("row")
    col = lax.axis_index("col")
    block = tokens.shape[1]
    half_width = block * cols
    wide = query_weight.shape[1] // 2
    hidden_units = gate_weight.shape[1] // 2
    local_heads = wide // HEAD
    span = rows // CHUNKS
    own = span // 2
    first_row = row == 0
    side = lax.axis_index("dp") % 2
    sides = [(i, i ^ 1) for i in range(lax.axis_size("dp"))]
    part_units = hidden_units // 2
    part_wide = wide // 2

    def swap(operand):
        return lax.ppermute(operand, "row", [(0, 1), (1, 0)])

    def own_columns(weight, size):
        kept, sent = take(weight, row, size, 1), take(weight, 1 - row, size, 1)
        return jnp.concatenate([kept, swap(sent)], axis=0)

    def own_rows(weight, size):
        kept, sent = take(weight, row, size, 0), take(weight, 1 - row, size, 0)
        return jnp.concatenate([kept, swap(sent)], axis=1)

    def cross(operand):
        return lax.ppermute(operand, "dp", sides)

    def gather_blocks(operand):
        if cols == 2:
            got = lax.ppermute(operand, "col", [(0, 1), (1, 0)])
            return ordered(col == 0, operand, got, 1)
        return lax.all_gather(operand, "col", axis=1, tiled=True)

    def sum_chips(mine, sent):
        if cols == 2:
            return mine + lax.ppermute(sent.astype(BF), "col", [(0, 1), (1, 0)]).astype(F32)
        return mine + (lax.psum(sent, "col") - sent)

    def both_cores(kept):
        return jnp.concatenate([kept, swap(swap_halves(kept, 1))], axis=0)

    def sum_cores(part):
        sent = swap_halves(part[own:], 1).astype(BF)
        return part[:own] + swap(sent).astype(F32)

    def local_order(vector):
        pieces = []
        for j in range(CHUNKS):
            piece = vector[j * span : (j + 1) * span]
            pieces.append(ordered(first_row, piece[:own], piece[own:], 0))
        return pieces

    validity = valid_mask.astype(F32)
    token_total = butterfly(jnp.sum(validity).reshape(1, 1), "dp")
    scale = (rows * lax.axis_size("dp")) / token_total
    segs = local_order(segments)
    places = local_order(jnp.arange(rows, dtype=jnp.int32))
    valids = [v[:own, None] for v in local_order(validity)]

    qkv_weight = own_columns(
        jnp.concatenate(
            [
                jnp.concatenate(
                    [
                        lax.slice_in_dim(w, h * wide, (h + 1) * wide, axis=1)
                        for w in (query_weight, key_weight, value_weight)
                    ],
                    axis=1,
                )
                for h in range(2)
            ],
            axis=1,
        ),
        3 * wide,
    )
    out_weight = own_rows(output_weight, wide)
    gates = own_columns(gate_weight, hidden_units)
    ups = own_columns(up_weight, hidden_units)
    downs = own_rows(down_weight, hidden_units)

    inputs, first_stats, low_first = [], [], []
    for j in range(CHUNKS):
        piece = tokens[j * span : (j + 1) * span]
        piece = ordered(first_row, piece[:own], piece[own:], 0)
        half = gather_blocks(piece)
        whole = jnp.concatenate([half, swap(swap_halves(half, 0))], axis=1)
        whole_f = whole.astype(F32)
        average, factor = moments(whole_f)
        inputs.append(whole[:own])
        first_stats.append((average[:own], factor[:own]))
        low_first.append(((whole_f - average) * factor).astype(BF))

    tables = [rope_tables(p) for p in places]
    query_heads, key_heads, value_heads = [], [], []
    attended, logsums = [], []
    hidden, second_stats, low_second = [], [], []
    for j in range(CHUNKS):
        raw = dot(low_first[j], qkv_weight).reshape(span, 3, local_heads, HEAD)
        query_heads.append(rotate(raw[:, 0], *tables[j]).astype(BF))
        key_heads.append(rotate(raw[:, 1], *tables[j]).astype(BF))
        value_heads.append(raw[:, 2].astype(BF))

    def keys_to(j):
        return (
            jnp.concatenate(key_heads[: j + 1], axis=0),
            jnp.concatenate(value_heads[: j + 1], axis=0),
            allowed_pairs(
                segs[j],
                places[j],
                jnp.concatenate(segs[: j + 1]),
                jnp.concatenate(places[: j + 1]),
            ),
        )

    for j in range(CHUNKS):
        keys, values, allowed = keys_to(j)
        heads, logsum = attend(query_heads[j], keys, values, allowed)
        attended.append(heads.reshape(span, wide))
        logsums.append(logsum)
        part = sum_cores(dot(attended[j], out_weight))
        hidden.append(inputs[j].astype(F32) + sum_chips(part, part))
        average, factor = moments(hidden[j])
        second_stats.append((average, factor))
        low_second.append(both_cores(((hidden[j] - average) * factor).astype(BF)))

    gate_outs, up_outs, acts = [], [], []
    outputs, grad_results, low_results = [], [], []
    error_sum = jnp.zeros((), F32)
    for j in range(CHUNKS):
        gate_outs.append(dot(low_second[j], gates))
        up_outs.append(dot(low_second[j], ups))
        acts.append((jax.nn.silu(gate_outs[j]) * up_outs[j]).astype(BF))
        part = sum_cores(dot(acts[j], downs))

        piece = teacher[j * span : (j + 1) * span]
        piece = ordered(first_row, piece[:own], piece[own:], 0)
        near, far = piece[:own].astype(F32), swap(piece[own:]).astype(F32)
        blocks = [jnp.where(col == b, near, 0.0) for b in range(cols)]
        blocks += [jnp.where(col == b, far, 0.0) for b in range(cols)]
        part = part - jnp.concatenate(blocks, axis=1)
        error = hidden[j] + sum_chips(part, part)

        near_error, far_error = take(error[:, :half_width], col, block, 1), take(
            error[:, half_width:], col, block, 1
        )
        near_out, far_out = near_error + near, far_error + far
        outputs.append(
            ordered(first_row, near_out.astype(BF), swap(far_out.astype(BF)), 0)
        )
        error_sum = error_sum + 0.5 * jnp.sum(
            valids[j] * (near_error * near_error + far_error * far_error)
        )
        grad_results.append(scale * valids[j] * error)
        low_results.append(both_cores(grad_results[j].astype(BF)))
    output = jnp.concatenate(outputs, axis=0)

    def with_side(mine, other):
        return jnp.concatenate([*mine, *other], axis=0)

    def split_rows(full):
        half = full.shape[0] // 2
        return full[:half], swap(full[half:])

    def split_cols(full):
        half = full.shape[1] // 2
        return full[:, :half], swap(full[:, half:])

    results = with_side(low_results, [cross(g) for g in low_results])
    act = with_side(
        [take(a, side, part_units, 1) for a in acts],
        [cross(take(a, 1 - side, part_units, 1)) for a in acts],
    )
    twos = with_side(low_second, [cross(a) for a in low_second])
    down_pair = split_cols(contract_rows(act, results).astype(BF))

    gate_backs, up_backs = [], []
    for j in range(CHUNKS):
        grad_act = contract_cols(low_results[j], downs)
        sigmoid = jax.nn.sigmoid(gate_outs[j])
        gate_backs.append(
            (
                grad_act * up_outs[j] * sigmoid * (1.0 + gate_outs[j] * (1.0 - sigmoid))
            ).astype(BF)
        )
        up_backs.append((grad_act * gate_outs[j] * sigmoid).astype(BF))

    def input_pair(lefts, rights, size):
        right = with_side(
            [take(g, side, size, 1) for g in rights],
            [cross(take(g, 1 - side, size, 1)) for g in rights],
        )
        return split_rows(contract_rows(lefts, right).astype(BF))

    gate_pair = input_pair(twos, gate_backs, part_units)
    up_pair = input_pair(twos, up_backs, part_units)

    grad_hiddens, low_hiddens = [], []
    for j in range(CHUNKS):
        part = sum_cores(contract_cols(gate_backs[j], gates) + contract_cols(up_backs[j], ups))
        gradient = sum_chips(part, part)
        average, factor = second_stats[j]
        normed = (hidden[j] - average) * factor
        grad_hiddens.append(grad_results[j] + normalize_back(gradient, normed, factor))
        low_hiddens.append(both_cores(grad_hiddens[j].astype(BF)))
    low_hidden = jnp.concatenate(low_hiddens, axis=0)

    grad_out = contract_rows(jnp.concatenate(attended, axis=0), low_hidden).astype(BF)
    grad_out = add_low(
        take(grad_out, side, part_wide, 0), cross(take(grad_out, 1 - side, part_wide, 0))
    )
    out_pair = split_cols(grad_out)
    grad_attended = contract_cols(low_hidden, out_weight).astype(BF)
    grad_attended = grad_attended.reshape(rows, local_heads, HEAD)
    grad_q, grad_k, grad_v = [], [], []
    for j in range(CHUNKS):
        keys, values, allowed = keys_to(j)
        parts = attend_back(
            query_heads[j],
            keys,
            values,
            allowed,
            logsums[j],
            grad_attended[j * span : (j + 1) * span],
        )
        grad_q.append(parts[0])
        for i in range(j + 1):
            at = slice(i * span, (i + 1) * span)
            if i == j:
                grad_k.append(parts[1][at])
                grad_v.append(parts[2][at])
            else:
                grad_k[i] = grad_k[i] + parts[1][at]
                grad_v[i] = grad_v[i] + parts[2][at]
    backs = []
    for j in range(CHUNKS):
        cosine, sine_table = tables[j]
        backs.append(
            jnp.concatenate(
                [
                    rotate(grad_q[j], cosine, -sine_table).reshape(span, wide),
                    rotate(grad_k[j], cosine, -sine_table).reshape(span, wide),
                    grad_v[j].reshape(span, wide),
                ],
                axis=1,
            ).astype(BF)
        )
    ones = with_side(low_first, [cross(a) for a in low_first])
    backs_wide = []
    for which in range(2):
        chosen = side if which == 0 else 1 - side
        backs_wide.append(
            [
                jnp.concatenate(
                    [
                        take(g[:, i * wide : (i + 1) * wide], chosen, part_wide, 1)
                        for i in range(3)
                    ],
                    axis=1,
                )
                for g in backs
            ]
        )
    qkv_pair = split_rows(
        contract_rows(
            ones, with_side(backs_wide[0], [cross(g) for g in backs_wide[1]])
        ).astype(BF)
    )
    three = [
        ordered(
            first_row,
            qkv_pair[0][:, i * part_wide : (i + 1) * part_wide],
            qkv_pair[1][:, i * part_wide : (i + 1) * part_wide],
            1,
        )
        for i in range(3)
    ]
    pieces, spots, starts = [], [], []
    total = 0
    for pair in (down_pair, gate_pair, up_pair, out_pair):
        packed = [pack(p, half_width) for p in pair]
        size = packed[0].shape[0]
        pieces += packed
        spots += [
            lambda r, total=total, size=size: total + r * size,
            lambda r, total=total, size=size: total + (1 - r) * size,
        ]
        starts.append((total, size))
        total += 2 * size
    for item in (jnp.concatenate(three[:2], axis=1), three[2]):
        packed = pack(item, half_width)
        size = packed.shape[0]
        pieces.append(packed)
        spots.append(lambda r, total=total: total + 0 * r)
        starts.append((total, size))
        total += size
    sums = line_sum(pieces, spots, chunk=min(256, total // 8))

    def blocks_of(which, columns):
        start, size = starts[which]
        return [
            unpack(sums[x, start + s * size : start + (s + 1) * size], columns)
            for s in range(2)
            for x in range(2)
        ]

    grad_down = jnp.concatenate(blocks_of(0, half_width), axis=0).astype(F32)
    grad_gate = jnp.concatenate(blocks_of(1, part_units), axis=1).astype(F32)
    grad_up = jnp.concatenate(blocks_of(2, part_units), axis=1).astype(F32)
    grad_output = jnp.concatenate(blocks_of(3, half_width), axis=0).astype(F32)
    three = [[], [], []]
    qk = [unpack(sums[x, starts[4][0] : starts[4][0] + starts[4][1]], 4 * part_wide) for x in range(2)]
    v = [unpack(sums[x, starts[5][0] : starts[5][0] + starts[5][1]], 2 * part_wide) for x in range(2)]
    for s in range(2):
        for x in range(2):
            at = s * part_wide
            three[0].append(qk[x][:, at : at + part_wide])
            three[1].append(qk[x][:, 2 * part_wide + at : 2 * part_wide + at + part_wide])
            three[2].append(v[x][:, at : at + part_wide])
    grad_query, grad_key, grad_value = (
        jnp.concatenate(t, axis=1).astype(F32) for t in three
    )
    grad_tokens = []
    for j in range(CHUNKS):
        part = sum_cores(contract_cols(backs[j], qkv_weight))
        gradient = sum_chips(part, part)
        average, factor = first_stats[j]
        normed = (inputs[j].astype(F32) - average) * factor
        grads = grad_hiddens[j] + normalize_back(gradient, normed, factor)
        near = take(grads[:, :half_width], col, block, 1)
        far = take(grads[:, half_width:], col, block, 1)
        grad_tokens.append(ordered(first_row, near, swap(far), 0))
    error_sum = error_sum.reshape(1, 1)
    for axis in ("row", "col", "dp"):
        error_sum = butterfly(error_sum, axis)
    loss_value = (error_sum / token_total)[0, 0]
    return (
        output,
        loss_value,
        jnp.concatenate(grad_tokens, axis=0),
        grad_query,
        grad_key,
        grad_value,
        grad_output,
        grad_gate,
        grad_up,
        grad_down,
    )


def solution(mesh):
    features = P("dp", ("row", "col"))
    into, back = P("row", "col"), P("col", "row")
    in_specs = (features, features, P("dp"), P("dp"), into, into, into, back, into, into, back)
    out_specs = (features, P(), features, into, into, into, back, into, into, back)
    return jax.shard_map(body, mesh=mesh, in_specs=in_specs, out_specs=out_specs, check_vma=False)
```

time: 2940 us -> 1310 us (0.45)
  waiting for transfers between devices: 2390 us -> 253 us
  Pallas kernels: 0 us -> 450 us
  blocking collectives: 99.6 us -> 0 us
  local copies, waits for them, and re-layouts: 81.2 us -> 167 us
  other arithmetic: 81.6 us -> 140 us
  starting transfers between devices: 2.7 us -> 57 us
    psum x1 -> x0, waiting for transfers between devices: 1930 us -> none  [body(): lax.psum((grad_query, grad_key, grad_value, grad_output, grad_gate, grad_...]
    pallas_call x0 -> x1, Pallas kernels: none -> 450 us  [line_sum(): pl.pallas_call(functools.partial(line_kernel, sizes, spots, chunk, lag, a...]
    ppermute x0 -> x65, waiting for transfers between devices: none -> 253 us  [the longest x15 148 us: cross(): return lax.ppermute(operand, 'dp', sides)]
    reduce_scatter x11 -> x0, waiting for transfers between devices: 235 us -> none  [the longest x4 143 us: sum_cols(): return lax.psum_scatter(operand, 'col', scatter_dimension=1, tiled=True)]
    all_gather x11 -> x0, waiting for transfers between devices: 221 us -> none  [the longest x4 137 us: gather_cols(): return lax.all_gather(operand, 'col', axis=1, tiled=True)]
    psum x6 -> x0, blocking collectives: 99.6 us -> none  [the longest x1 46.7 us: body(): lax.psum(0.5 * jnp.sum(validity[:, None] * error_term * error_term), ('dp...]
    ppermute x0 -> x65, starting transfers between devices: none -> 57 us  [the longest x8 22.6 us: butterfly(): lax.ppermute(operand, axis, [(i, i ^ step) for i in range(size)])]
    dynamic_slice x8 -> x20, local copies, waits for them, and re-layouts: 3.93 us -> 50.9 us  [take(): return lax.dynamic_slice_in_dim(operand, index * size, size, axis)]
  transfers between devices with their start and end apart: 23 -> 65, of which waited for: 21 -> 19; matrix products, arithmetic and copies ran while one was open for 5% -> 39% of each run, Pallas kernels for 0% -> 34%
where the time goes in v1:
time: 1310 us
  Pallas kernels  450 us (34%)
  waiting for transfers between devices  253 us (19%)
  matrix products  229 us (17%)
  local copies, waits for them, and re-layouts  167 us (13%)
  other arithmetic  140 us (11%)
  starting transfers between devices  57 us (4%)
    pallas_call x1, Pallas kernels, line_sum(): pl.pallas_call(functools.partial(line_kernel, sizes, spots, chunk, lag, a...  450 us
    ppermute x15, waiting for transfers between devices, cross(): return lax.ppermute(operand, 'dp', sides)  148 us
    ppermute x8, waiting for transfers between devices, sum_chips(): lax.ppermute(sent.astype(BF), 'col', [(0, 1), (1, 0)]).astype(F32)  98 us
    dot_general x9, matrix products, contract_cols(): lax.dot_general(left, right, (((1,), (1,)), ((), ())), preferred_element_...  82.4 us
    dot_general x10, matrix products, dot(): return jnp.dot(left, right, preferred_element_type=F32)  70 us
    dot_general x5, matrix products, contract_rows(): lax.dot_general(left, right, (((0,), (0,)), ((), ())), preferred_element_...  52.3 us
    dynamic_slice x20, local copies, waits for them, and re-layouts, take(): return lax.dynamic_slice_in_dim(operand, index * size, size, axis)  50.9 us
    unnamed x368, local copies, waits for them, and re-layouts  48.6 us
  transfers between devices with their start and end apart: 65, of which 19 were waited for; matrix products, arithmetic and copies ran while one was open for 39% of the time, Pallas kernels for 34%

profile of v1, /device:TPU:0, one launch (start us, length us, event | category | flops | bytes accessed | tf_op | source)
XLA Modules:
  0.0 1307.4 jit_solution(2408690604608717764)
XLA Ops:
  23.4 6.0 constant_dynamic-slice_fusion.36
  36.4 8.7 constant_dynamic-slice_fusion.32
  46.4 4.2 constant_dynamic-slice_fusion.30
  55.1 8.0 constant_dynamic-slice_fusion.28
  69.8 4.0 collective-permute-start.30
  86.4 6.0 fusion.183
  95.8 7.6 fusion.184
  103.4 4.8 reshape.509
  155.3 18.4 %collective-permute-done.5 = bf16[256,2048]{1,0:T(8,128)(2,1)S(1)} collective-permute-done((bf16[256,2048]{1,0:T(8,128)(2,1)S(1)}, bf16[256,2048]{1,0:T(8,128)(2,1)S(1)}, u32[]{:S(2)}, u32[]{:S(2)}) %collective-permute-start.5) | collective-permute-done | bytes 1048608 | tf_op jit(solution)/shard_map/ppermute | solution.py:397
  177.4 21.2 %collective-permute-done.17 = bf16[256,2048]{1,0:T(8,128)(2,1)S(1)} collective-permute-done((bf16[256,2048]{1,0:T(8,128)(2,1)S(1)}, bf16[256,2048]{1,0:T(8,128)(2,1)S(1)}, u32[]{:S(2)}, u32[]{:S(2)}) %collective-permute-start.17) | collective-permute-done | bytes 1048608 | tf_op jit(solution)/shard_map/ppermute | solution.py:397
  206.3 8.9 fusion.194
  215.1 8.7 multiply_convert_fusion.7
  223.8 8.0 fusion.240
  243.7 8.7 fusion.193
  252.4 8.7 multiply_convert_fusion.6
  261.1 8.0 fusion.243
  281.1 13.9 %collective-permute-done.50 = bf16[512,2048]{1,0:T(8,128)(2,1)} collective-permute-done((bf16[512,2048]{1,0:T(8,128)(2,1)}, bf16[512,2048]{1,0:T(8,128)(2,1)}, u32[]{:S(2)}, u32[]{:S(2)}) %collective-permute-start.50) | collective-permute-done | bytes 2097184 | tf_op jit(solution)/shard_map/ppermute | solution.py:387
  300.6 11.3 multiply_convert_fusion.5
  314.7 9.2 collective-permute-done.21
  335.8 10.7 fusion.190
  346.5 9.3 fusion.245
  378.3 4.0 collective-permute-start.27
  385.3 10.5 multiply_convert_fusion.3
  402.1 8.7 fusion.189
  410.9 11.1 fusion.244
  432.9 12.7 fusion.52
  445.5 10.9 collective-permute-done.33
  462.1 20.4 %collective-permute-done.56 = bf16[512,1024]{1,0:T(8,128)(2,1)S(1)} collective-permute-done((bf16[512,1024]{1,0:T(8,128)(2,1)S(1)}, bf16[512,1024]{1,0:T(8,128)(2,1)S(1)}, u32[]{:S(2)}, u32[]{:S(2)}) %collective-permute-start.56) | collective-permute-done | bytes 1048608 | tf_op jit(solution)/shard_map/ppermute | solution.py:387
  484.1 13.6 %fusion.49 = bf16[2048,1024]{1,0:T(8,128)(2,1)} fusion(bf16[2048,2048]{1,0:T(8,128)(2,1)} %constant_dynamic-update-slice_fusion.6, bf16[512,1024]{1,0:T(8,128)(2,1)} %copy-done.168, bf16[512,1024]{1,0:T(8,128)(2,1)} %collective-permute-done.55, bf16[512,1024]{1,0:T(8,128)(2,1)S(1)} %copy-done.120, bf16[512,1024]{1,0:T(8,128)(2,1)S(1)} %copy-done.118), kind=kOutput, calls=%fused_computation.83 | convolution fusion | flops 8608808960 | bytes 16777216 | tf_op jit(solution)/shard_map/dot_general | solution.py:52
  506.6 41.4 %collective-permute-done.47 = bf16[512,2048]{1,0:T(8,128)(2,1)} collective-permute-done((bf16[512,2048]{1,0:T(8,128)(2,1)}, bf16[512,2048]{1,0:T(8,128)(2,1)}, u32[]{:S(2)}, u32[]{:S(2)}) %collective-permute-start.47) | collective-permute-done | bytes 2097184 | tf_op jit(solution)/shard_map/ppermute | solution.py:387
  555.4 3.7 fusion.204
  559.3 56.9 %collective-permute-done.48 = bf16[512,2048]{1,0:T(8,128)(2,1)S(1)} collective-permute-done((bf16[512,2048]{1,0:T(8,128)(2,1)S(1)}, bf16[512,2048]{1,0:T(8,128)(2,1)S(1)}, u32[]{:S(2)}, u32[]{:S(2)}) %collective-permute-start.48) | collective-permute-done | bytes 2097184 | tf_op jit(solution)/shard_map/ppermute | solution.py:387
  617.9 10.4 fusion.55
  631.1 4.8 convolution_convert_fusion.1
  646.4 3.6 fusion.128
  681.1 7.9 fusion.247
  691.8 8.1 fusion.246
  705.0 11.1 collective-permute-done.63
  717.0 13.1 %fusion.59 = bf16[2048,768]{1,0:T(8,128)(2,1)} fusion(bf16[512,2048]{1,0:T(8,128)(2,1)} %collective-permute-done.61, bf16[512,2048]{1,0:T(8,128)(2,1)} %collective-permute-done.60, bf16[512,2048]{1,0:T(8,128)(2,1)} %fusion.15, bf16[512,2048]{1,0:T(8,128)(2,1)} %fusion.17, bf16[512,768]{0,1:T(8,128)(2,1)} %copy-done.170, bf16[512,768]{0,1:T(8,128)(2,1)} %copy-done.169, ...), kind=kOutput, calls=%fused_computation.87 | convolution fusion | flops 6502744064 | bytes 14680064 | tf_op jit(solution)/shard_map/dot_general | solution.py:52
  733.9 3.8 collective-permute-done.58
  742.4 19.6 %collective-permute-done.43 = bf16[256,2048]{1,0:T(8,128)(2,1)S(1)} collective-permute-done((bf16[256,2048]{1,0:T(8,128)(2,1)S(1)}, bf16[256,2048]{1,0:T(8,128)(2,1)S(1)}, u32[]{:S(2)}, u32[]{:S(2)}) %collective-permute-start.43) | collective-permute-done | bytes 1048608 | tf_op jit(solution)/shard_map/ppermute | solution.py:397
  766.7 18.6 %collective-permute-done.40 = bf16[256,2048]{1,0:T(8,128)(2,1)S(1)} collective-permute-done((bf16[256,2048]{1,0:T(8,128)(2,1)S(1)}, bf16[256,2048]{1,0:T(8,128)(2,1)S(1)}, u32[]{:S(2)}, u32[]{:S(2)}) %collective-permute-start.40) | collective-permute-done | bytes 1048608 | tf_op jit(solution)/shard_map/ppermute | solution.py:397
  795.2 449.9 %line_sum.1 = bf16[2,8192,1024]{2,1,0:T(8,128)(2,1)} custom-call(bf16[1024,1024]{1,0:T(8,128)(2,1)} %get-tuple-element.95.refs_0_, bf16[1024,1024]{1,0:T(8,128)(2,1)} %collective-permute-done.49.refs_1_, bf16[1024,1024]{1,0:T(8,128)(2,1)} %get-tuple-element.93.refs_2_, bf16[1024,1024]{1,0:T(8,128)(2,1)} %copy-done.83, ...), custom_call_target="tpu_custom_call" | custom-call | tf_op jit(solution)/shard_map/line_sum/pallas_call | solution.py:254
  1250.6 16.8 %slice_bitcast_fusion.3 = (bf16[1024,1024]{1,0:T(8,128)(2,1)}, bf16[1024,1024]{1,0:T(8,128)(2,1)}, bf16[1024,1024]{1,0:T(8,128)(2,1)}, bf16[1024,1024]{1,0:T(8,1...) fusion(bf16[2,8192,1024]{2,1,0:T(8,128)(2,1)} %line_sum.1), kind=kLoop, calls=%fused_computation.158 | loop fusion | bytes 58720256 | tf_op jit(solution)/shard_map/squeeze | solution.py:662
  1270.3 4.7 fusion.99
  1275.1 6.5 maximum_convert_fusion.2
  1281.6 6.4 maximum_convert_fusion.1
  1288.0 6.4 maximum_convert_fusion
  (693 shorter events, 316.0 us)
Async XLA Ops:
  1.9 62.3 %collective-permute-start.28 = (f32[1,1]{1,0:T(1,128)}, f32[1,1]{1,0:T(1,128)}, u32[]{:S(2)}, u32[]{:S(2)}) collective-permute-start(f32[1,1]{1,0:T(1,128)} %bitcast.12), channel_id=1, source_target_pairs={{0,4},{4,0},{8,12},{12,8},{16,20},{20,16},{24,28},{28,24},{1,5},{5... | collective-permute-start | bytes 20 | tf_op jit(solution)/shard_map/ppermute | solution.py:296
  6.9 143.9 %collective-permute-start.11 = (bf16[256,512]{1,0:T(8,128)(2,1)}, bf16[256,512]{1,0:T(8,128)(2,1)}, u32[]{:S(2)}, u32[]{:S(2)}) collective-permute-start(bf16[256,512]{1,0:T(8,128)(2,1)} %get-tuple-element.198), channel_id=1, source_target_pairs={{0,2},{2,0},{1,3},{3,1},{4,6},{6,4},{5,7},{7,5},{8,10},{10,8},{9,1... | collective-permute-start | bytes 786440 | tf_op jit(solution)/shard_map/ppermute | solution.py:376
  9.0 41.6 %collective-permute-start = (bf16[512,512]{1,0:T(8,128)(2,1)}, bf16[512,512]{1,0:T(8,128)(2,1)S(1)}, u32[]{:S(2)}, u32[]{:S(2)}) collective-permute-start(bf16[512,512]{1,0:T(8,128)(2,1)} %pad_maximum_fusion.42), channel_id=1, source_target_pairs={{0,1},{1,0},{2,3},{3,2},{4,5},{5,4},{6,7},{7,6},{8,9},{9,8},{10,11... | collective-permute-start | bytes 1572872 | tf_op jit(solution)/shard_map/ppermute | solution.py:391
  11.3 40.8 %collective-permute-start.14 = (bf16[512,512]{1,0:T(8,128)(2,1)}, bf16[512,512]{1,0:T(8,128)(2,1)S(1)}, u32[]{:S(2)}, u32[]{:S(2)}) collective-permute-start(bf16[512,512]{1,0:T(8,128)(2,1)} %pad_maximum_fusion.45), channel_id=1, source_target_pairs={{0,1},{1,0},{2,3},{3,2},{4,5},{5,4},{6,7},{7,6},{8,9},{9,8},{10,11... | collective-permute-start | bytes 1572872 | tf_op jit(solution)/shard_map/ppermute | solution.py:391
  29.4 56.5 %collective-permute-start.2 = (bf16[1024,1536]{1,0:T(8,128)(2,1)}, bf16[1024,1536]{1,0:T(8,128)(2,1)}, u32[]{:S(2)}, u32[]{:S(2)}) collective-permute-start(bf16[1024,1536]{1,0:T(8,128)(2,1)} %get-tuple-element.83), channel_id=1, source_target_pairs={{0,2},{2,0},{1,3},{3,1},{4,6},{6,4},{5,7},{7,5},{8,10},{10,8},{9,1... | collective-permute-start | bytes 9437192 | tf_op jit(solution)/shard_map/ppermute | solution.py:376
  53.5 22.2 %collective-permute-start.15 = (bf16[512,1024]{1,0:T(8,128)(2,1)}, bf16[512,1024]{1,0:T(8,128)(2,1)}, u32[]{:S(2)}, u32[]{:S(2)}) collective-permute-start(bf16[512,1024]{1,0:T(8,128)(2,1)} %fusion.144), channel_id=1, source_target_pairs={{0,2},{2,0},{1,3},{3,1},{4,6},{6,4},{5,7},{7,5},{8,10},{10,8},{9,1... | collective-permute-start | bytes 3145736 | tf_op jit(solution)/shard_map/ppermute | solution.py:376
  54.0 23.8 %collective-permute-start.1 = (bf16[512,1024]{1,0:T(8,128)(2,1)}, bf16[512,1024]{1,0:T(8,128)(2,1)S(1)}, u32[]{:S(2)}, u32[]{:S(2)}) collective-permute-start(bf16[512,1024]{1,0:T(8,128)(2,1)} %fusion.145), channel_id=1, source_target_pairs={{0,2},{2,0},{1,3},{3,1},{4,6},{6,4},{5,7},{7,5},{8,10},{10,8},{9,1... | collective-permute-start | bytes 3145736 | tf_op jit(solution)/shard_map/ppermute | solution.py:376
  74.5 73.7 %collective-permute-start.20 = (bf16[256,512]{1,0:T(8,128)(2,1)}, bf16[256,512]{1,0:T(8,128)(2,1)}, u32[]{:S(2)}, u32[]{:S(2)}) collective-permute-start(bf16[256,512]{1,0:T(8,128)(2,1)} %get-tuple-element.199), channel_id=1, source_target_pairs={{0,2},{2,0},{1,3},{3,1},{4,6},{6,4},{5,7},{7,5},{8,10},{10,8},{9,1... | collective-permute-start | bytes 786440 | tf_op jit(solution)/shard_map/ppermute | solution.py:376
  75.7 55.7 %collective-permute-start.3 = (bf16[512,1024]{1,0:T(8,128)(2,1)}, bf16[512,1024]{1,0:T(8,128)(2,1)}, u32[]{:S(2)}, u32[]{:S(2)}) collective-permute-start(bf16[512,1024]{1,0:T(8,128)(2,1)} %get-tuple-element.147), channel_id=1, source_target_pairs={{0,2},{2,0},{1,3},{3,1},{4,6},{6,4},{5,7},{7,5},{8,10},{10,8},{9,1... | collective-permute-start | bytes 3145736 | tf_op jit(solution)/shard_map/ppermute | solution.py:376
  78.8 123.6 %collective-permute-start.7 = (bf16[1024,2048]{1,0:T(8,128)(2,1)}, bf16[1024,2048]{1,0:T(8,128)(2,1)}, u32[]{:S(2)}, u32[]{:S(2)}) collective-permute-start(bf16[1024,2048]{1,0:T(8,128)(2,1)} %get-tuple-element.79), channel_id=1, source_target_pairs={{0,2},{2,0},{1,3},{3,1},{4,6},{6,4},{5,7},{7,5},{8,10},{10,8},{9,1... | collective-permute-start | bytes 12582920 | tf_op jit(solution)/shard_map/ppermute | solution.py:376
  85.9 129.3 %collective-permute-start.8 = (bf16[1024,2048]{1,0:T(8,128)(2,1)}, bf16[1024,2048]{1,0:T(8,128)(2,1)}, u32[]{:S(2)}, u32[]{:S(2)}) collective-permute-start(bf16[1024,2048]{1,0:T(8,128)(2,1)} %get-tuple-element.81), channel_id=1, source_target_pairs={{0,2},{2,0},{1,3},{3,1},{4,6},{6,4},{5,7},{7,5},{8,10},{10,8},{9,1... | collective-permute-start | bytes 12582920 | tf_op jit(solution)/shard_map/ppermute | solution.py:376
  148.2 25.6 %collective-permute-start.5 = (bf16[256,2048]{1,0:T(8,128)(2,1)S(1)}, bf16[256,2048]{1,0:T(8,128)(2,1)S(1)}, u32[]{:S(2)}, u32[]{:S(2)}) collective-permute-start(bf16[256,2048]{1,0:T(8,128)(2,1)S(1)} %fusion.132), channel_id=1, source_target_pairs={{0,1},{1,0},{2,3},{3,2},{4,5},{5,4},{6,7},{7,6},{8,9},{9,8},{10,11... | collective-permute-start | bytes 3145736 | tf_op jit(solution)/shard_map/ppermute | solution.py:397
  150.8 73.0 %collective-permute-start.9 = (bf16[2048,1024]{1,0:T(8,128)(2,1)}, bf16[2048,1024]{1,0:T(8,128)(2,1)}, u32[]{:S(2)}, u32[]{:S(2)}) collective-permute-start(bf16[2048,1024]{1,0:T(8,128)(2,1)} %get-tuple-element.77), channel_id=1, source_target_pairs={{0,2},{2,0},{1,3},{3,1},{4,6},{6,4},{5,7},{7,5},{8,10},{10,8},{9,1... | collective-permute-start | bytes 12582920 | tf_op jit(solution)/shard_map/ppermute | solution.py:376
  154.5 548.7 %collective-permute-start.61 = (bf16[512,2048]{1,0:T(8,128)(2,1)}, bf16[512,2048]{1,0:T(8,128)(2,1)}, u32[]{:S(2)}, u32[]{:S(2)}) collective-permute-start(bf16[512,2048]{1,0:T(8,128)(2,1)} %fusion.15), channel_id=1, source_target_pairs={{0,4},{4,0},{8,12},{12,8},{16,20},{20,16},{24,28},{28,24},{1,5},{5... | collective-permute-start | bytes 6291464 | tf_op jit(solution)/shard_map/ppermute | solution.py:387
  173.8 24.9 %collective-permute-start.17 = (bf16[256,2048]{1,0:T(8,128)(2,1)S(1)}, bf16[256,2048]{1,0:T(8,128)(2,1)S(1)}, u32[]{:S(2)}, u32[]{:S(2)}) collective-permute-start(bf16[256,2048]{1,0:T(8,128)(2,1)S(1)} %fusion.133), channel_id=1, source_target_pairs={{0,1},{1,0},{2,3},{3,2},{4,5},{5,4},{6,7},{7,6},{8,9},{9,8},{10,11... | collective-permute-start | bytes 3145736 | tf_op jit(solution)/shard_map/ppermute | solution.py:397
  201.3 501.9 %collective-permute-start.60 = (bf16[512,2048]{1,0:T(8,128)(2,1)}, bf16[512,2048]{1,0:T(8,128)(2,1)}, u32[]{:S(2)}, u32[]{:S(2)}) collective-permute-start(bf16[512,2048]{1,0:T(8,128)(2,1)} %fusion.17), channel_id=1, source_target_pairs={{0,4},{4,0},{8,12},{12,8},{16,20},{20,16},{24,28},{28,24},{1,5},{5... | collective-permute-start | bytes 6291464 | tf_op jit(solution)/shard_map/ppermute | solution.py:387
  202.4 36.1 %collective-permute-start.18 = (bf16[256,2048]{1,0:T(8,128)(2,1)S(1)}, bf16[256,2048]{1,0:T(8,128)(2,1)S(1)}, u32[]{:S(2)}, u32[]{:S(2)}) collective-permute-start(bf16[256,2048]{1,0:T(8,128)(2,1)S(1)} %pad_maximum_fusion.22), channel_id=1, source_target_pairs={{0,2},{2,0},{1,3},{3,1},{4,6},{6,4},{5,7},{7,5},{8,10},{10,8},{9,1... | collective-permute-start | bytes 3145736 | tf_op jit(solution)/shard_map/ppermute | solution.py:376
  235.3 59.7 %collective-permute-start.50 = (bf16[512,2048]{1,0:T(8,128)(2,1)}, bf16[512,2048]{1,0:T(8,128)(2,1)}, u32[]{:S(2)}, u32[]{:S(2)}) collective-permute-start(bf16[512,2048]{1,0:T(8,128)(2,1)} %pad_maximum_fusion.7), channel_id=1, source_target_pairs={{0,4},{4,0},{8,12},{12,8},{16,20},{20,16},{24,28},{28,24},{1,5},{5... | collective-permute-start | bytes 6291464 | tf_op jit(solution)/shard_map/ppermute | solution.py:387
  240.0 121.3 %collective-permute-start.51 = (bf16[512,2048]{1,0:T(8,128)(2,1)}, bf16[512,2048]{1,0:T(8,128)(2,1)}, u32[]{:S(2)}, u32[]{:S(2)}) collective-permute-start(bf16[512,2048]{1,0:T(8,128)(2,1)} %pad_maximum_fusion.9), channel_id=1, source_target_pairs={{0,4},{4,0},{8,12},{12,8},{16,20},{20,16},{24,28},{28,24},{1,5},{5... | collective-permute-start | bytes 6291464 | tf_op jit(solution)/shard_map/ppermute | solution.py:387
  242.0 29.8 %collective-permute-start.12 = (bf16[256,2048]{1,0:T(8,128)(2,1)}, bf16[256,2048]{1,0:T(8,128)(2,1)S(1)}, u32[]{:S(2)}, u32[]{:S(2)}) collective-permute-start(bf16[256,2048]{1,0:T(8,128)(2,1)} %fusion.195), channel_id=1, source_target_pairs={{0,1},{1,0},{2,3},{3,2},{4,5},{5,4},{6,7},{7,6},{8,9},{9,8},{10,11... | collective-permute-start | bytes 3145736 | tf_op jit(solution)/shard_map/ppermute | solution.py:397
  275.7 24.9 %collective-permute-start.31 = (bf16[256,2048]{1,0:T(8,128)(2,1)S(1)}, bf16[256,2048]{1,0:T(8,128)(2,1)S(1)}, u32[]{:S(2)}, u32[]{:S(2)}) collective-permute-start(bf16[256,2048]{1,0:T(8,128)(2,1)S(1)} %pad_maximum_fusion.25), channel_id=1, source_target_pairs={{0,2},{2,0},{1,3},{3,1},{4,6},{6,4},{5,7},{7,5},{8,10},{10,8},{9,1... | collective-permute-start | bytes 3145736 | tf_op jit(solution)/shard_map/ppermute | solution.py:376
  298.2 25.8 %collective-permute-start.21 = (bf16[256,2048]{1,0:T(8,128)(2,1)}, bf16[256,2048]{1,0:T(8,128)(2,1)S(1)}, u32[]{:S(2)}, u32[]{:S(2)}) collective-permute-start(bf16[256,2048]{1,0:T(8,128)(2,1)} %fusion.196), channel_id=1, source_target_pairs={{0,1},{1,0},{2,3},{3,2},{4,5},{5,4},{6,7},{7,6},{8,9},{9,8},{10,11... | collective-permute-start | bytes 3145736 | tf_op jit(solution)/shard_map/ppermute | solution.py:397
  329.5 55.8 %collective-permute-start.35 = (bf16[256,2048]{1,0:T(8,128)(2,1)}, bf16[256,2048]{1,0:T(8,128)(2,1)}, u32[]{:S(2)}, u32[]{:S(2)}) collective-permute-start(bf16[256,2048]{1,0:T(8,128)(2,1)} %pad_maximum_fusion.28), channel_id=1, source_target_pairs={{0,2},{2,0},{1,3},{3,1},{4,6},{6,4},{5,7},{7,5},{8,10},{10,8},{9,1... | collective-permute-start | bytes 3145736 | tf_op jit(solution)/shard_map/ppermute | solution.py:376
  334.5 30.4 %collective-permute-start.23 = (f32[1,1]{1,0:T(1,128)}, f32[1,1]{1,0:T(1,128)}, u32[]{:S(2)}, u32[]{:S(2)}) collective-permute-start(f32[1,1]{1,0:T(1,128)} %bitcast.11), channel_id=1, source_target_pairs={{0,2},{2,0},{1,3},{3,1},{4,6},{6,4},{5,7},{7,5},{8,10},{10,8},{9,1... | collective-permute-start | bytes 20 | tf_op jit(solution)/shard_map/ppermute | solution.py:296
  361.4 22.6 %collective-permute-start.22 = (bf16[256,512]{1,0:T(8,128)(2,1)S(1)}, bf16[256,512]{1,0:T(8,128)(2,1)S(1)}, u32[]{:S(2)}, u32[]{:S(2)}) collective-permute-start(bf16[256,512]{1,0:T(8,128)(2,1)S(1)} %copy-done.141), channel_id=1, source_target_pairs={{0,2},{2,0},{1,3},{3,1},{4,6},{6,4},{5,7},{7,5},{8,10},{10,8},{9,1... | collective-permute-start | bytes 786440 | tf_op jit(solution)/shard_map/ppermute | solution.py:376
  382.9 48.3 %collective-permute-start.52 = (bf16[512,1024]{1,0:T(8,128)(2,1)}, bf16[512,1024]{1,0:T(8,128)(2,1)}, u32[]{:S(2)}, u32[]{:S(2)}) collective-permute-start(bf16[512,1024]{1,0:T(8,128)(2,1)} %get-tuple-element.115), channel_id=1, source_target_pairs={{0,4},{4,0},{8,12},{12,8},{16,20},{20,16},{24,28},{28,24},{1,5},{5... | collective-permute-start | bytes 3145736 | tf_op jit(solution)/shard_map/ppermute | solution.py:387
  384.0 45.4 %collective-permute-start.32 = (bf16[256,2048]{1,0:T(8,128)(2,1)}, bf16[256,2048]{1,0:T(8,128)(2,1)S(1)}, u32[]{:S(2)}, u32[]{:S(2)}) collective-permute-start(bf16[256,2048]{1,0:T(8,128)(2,1)} %pad_maximum_fusion.26), channel_id=1, source_target_pairs={{0,2},{2,0},{1,3},{3,1},{4,6},{6,4},{5,7},{7,5},{8,10},{10,8},{9,1... | collective-permute-start | bytes 3145736 | tf_op jit(solution)/shard_map/ppermute | solution.py:376
  400.6 32.3 %collective-permute-start.53 = (bf16[512,1024]{1,0:T(8,128)(2,1)}, bf16[512,1024]{1,0:T(8,128)(2,1)}, u32[]{:S(2)}, u32[]{:S(2)}) collective-permute-start(bf16[512,1024]{1,0:T(8,128)(2,1)} %get-tuple-element.117), channel_id=1, source_target_pairs={{0,4},{4,0},{8,12},{12,8},{16,20},{20,16},{24,28},{28,24},{1,5},{5... | collective-permute-start | bytes 3145736 | tf_op jit(solution)/shard_map/ppermute | solution.py:387
  429.4 31.1 %collective-permute-start.55 = (bf16[512,1024]{1,0:T(8,128)(2,1)S(1)}, bf16[512,1024]{1,0:T(8,128)(2,1)}, u32[]{:S(2)}, u32[]{:S(2)}) collective-permute-start(bf16[512,1024]{1,0:T(8,128)(2,1)S(1)} %copy-done.119), channel_id=1, source_target_pairs={{0,4},{4,0},{8,12},{12,8},{16,20},{20,16},{24,28},{28,24},{1,5},{5... | collective-permute-start | bytes 3145736 | tf_op jit(solution)/shard_map/ppermute | solution.py:387
  431.2 25.2 %collective-permute-start.33 = (bf16[256,2048]{1,0:T(8,128)(2,1)}, bf16[256,2048]{1,0:T(8,128)(2,1)S(1)}, u32[]{:S(2)}, u32[]{:S(2)}) collective-permute-start(bf16[256,2048]{1,0:T(8,128)(2,1)} %fusion.134), channel_id=1, source_target_pairs={{0,1},{1,0},{2,3},{3,2},{4,5},{5,4},{6,7},{7,6},{8,9},{9,8},{10,11... | collective-permute-start | bytes 3145736 | tf_op jit(solution)/shard_map/ppermute | solution.py:397
  432.8 25.9 %collective-permute-start.36 = (bf16[256,2048]{1,0:T(8,128)(2,1)}, bf16[256,2048]{1,0:T(8,128)(2,1)S(1)}, u32[]{:S(2)}, u32[]{:S(2)}) collective-permute-start(bf16[256,2048]{1,0:T(8,128)(2,1)} %pad_maximum_fusion.29), channel_id=1, source_target_pairs={{0,2},{2,0},{1,3},{3,1},{4,6},{6,4},{5,7},{7,5},{8,10},{10,8},{9,1... | collective-permute-start | bytes 3145736 | tf_op jit(solution)/shard_map/ppermute | solution.py:376
  456.4 26.1 %collective-permute-start.56 = (bf16[512,1024]{1,0:T(8,128)(2,1)S(1)}, bf16[512,1024]{1,0:T(8,128)(2,1)S(1)}, u32[]{:S(2)}, u32[]{:S(2)}) collective-permute-start(bf16[512,1024]{1,0:T(8,128)(2,1)S(1)} %copy-done.121), channel_id=1, source_target_pairs={{0,4},{4,0},{8,12},{12,8},{16,20},{20,16},{24,28},{28,24},{1,5},{5... | collective-permute-start | bytes 3145736 | tf_op jit(solution)/shard_map/ppermute | solution.py:387
  458.7 157.6 %collective-permute-start.45 = (bf16[512,1024]{1,0:T(8,128)(2,1)}, bf16[512,1024]{1,0:T(8,128)(2,1)}, u32[]{:S(2)}, u32[]{:S(2)}) collective-permute-start(bf16[512,1024]{1,0:T(8,128)(2,1)} %get-tuple-element.119), channel_id=1, source_target_pairs={{0,4},{4,0},{8,12},{12,8},{16,20},{20,16},{24,28},{28,24},{1,5},{5... | collective-permute-start | bytes 3145736 | tf_op jit(solution)/shard_map/ppermute | solution.py:387
  460.5 87.6 %collective-permute-start.47 = (bf16[512,2048]{1,0:T(8,128)(2,1)}, bf16[512,2048]{1,0:T(8,128)(2,1)}, u32[]{:S(2)}, u32[]{:S(2)}) collective-permute-start(bf16[512,2048]{1,0:T(8,128)(2,1)} %pad_maximum_fusion.10), channel_id=1, source_target_pairs={{0,4},{4,0},{8,12},{12,8},{16,20},{20,16},{24,28},{28,24},{1,5},{5... | collective-permute-start | bytes 6291464 | tf_op jit(solution)/shard_map/ppermute | solution.py:387
  482.5 70.3 %collective-permute-start.37 = (bf16[256,2048]{1,0:T(8,128)(2,1)}, bf16[256,2048]{1,0:T(8,128)(2,1)}, u32[]{:S(2)}, u32[]{:S(2)}) collective-permute-start(bf16[256,2048]{1,0:T(8,128)(2,1)} %fusion.135), channel_id=1, source_target_pairs={{0,1},{1,0},{2,3},{3,2},{4,5},{5,4},{6,7},{7,6},{8,9},{9,8},{10,11... | collective-permute-start | bytes 3145736 | tf_op jit(solution)/shard_map/ppermute | solution.py:397
  548.0 68.9 %collective-permute-start.46 = (bf16[512,1024]{1,0:T(8,128)(2,1)S(1)}, bf16[512,1024]{1,0:T(8,128)(2,1)S(1)}, u32[]{:S(2)}, u32[]{:S(2)}) collective-permute-start(bf16[512,1024]{1,0:T(8,128)(2,1)S(1)} %copy-done.116), channel_id=1, source_target_pairs={{0,4},{4,0},{8,12},{12,8},{16,20},{20,16},{24,28},{28,24},{1,5},{5... | collective-permute-start | bytes 3145736 | tf_op jit(solution)/shard_map/ppermute | solution.py:387
  552.8 63.4 %collective-permute-start.48 = (bf16[512,2048]{1,0:T(8,128)(2,1)S(1)}, bf16[512,2048]{1,0:T(8,128)(2,1)S(1)}, u32[]{:S(2)}, u32[]{:S(2)}) collective-permute-start(bf16[512,2048]{1,0:T(8,128)(2,1)S(1)} %copy-done.105), channel_id=1, source_target_pairs={{0,4},{4,0},{8,12},{12,8},{16,20},{20,16},{24,28},{28,24},{1,5},{5... | collective-permute-start | bytes 6291464 | tf_op jit(solution)/shard_map/ppermute | solution.py:387
  616.4 177.2 %collective-permute-start.57 = (bf16[1024,1024]{1,0:T(8,128)(2,1)}, bf16[1024,1024]{1,0:T(8,128)(2,1)}, u32[]{:S(2)}, u32[]{:S(2)}) collective-permute-start(bf16[1024,1024]{1,0:T(8,128)(2,1)} %get-tuple-element.90), channel_id=1, source_target_pairs={{0,2},{2,0},{1,3},{3,1},{4,6},{6,4},{5,7},{7,5},{8,10},{10,8},{9,1... | collective-permute-start | bytes 6291464 | tf_op jit(solution)/shard_map/ppermute | solution.py:376
  678.8 24.9 %collective-permute-start.62 = (bf16[512,768]{0,1:T(8,128)(2,1)S(1)}, bf16[512,768]{0,1:T(8,128)(2,1)S(1)}, u32[]{:S(2)}, u32[]{:S(2)}) collective-permute-start(bf16[512,768]{0,1:T(8,128)(2,1)S(1)} %pad_maximum_fusion.33), channel_id=1, source_target_pairs={{0,4},{4,0},{8,12},{12,8},{16,20},{20,16},{24,28},{28,24},{1,5},{5... | collective-permute-start | bytes 2359304 | tf_op jit(solution)/shard_map/ppermute | solution.py:387
  680.5 35.6 %collective-permute-start.63 = (bf16[512,768]{0,1:T(8,128)(2,1)S(1)}, bf16[512,768]{0,1:T(8,128)(2,1)S(1)}, u32[]{:S(2)}, u32[]{:S(2)}) collective-permute-start(bf16[512,768]{0,1:T(8,128)(2,1)S(1)} %pad_maximum_fusion.34), channel_id=1, source_target_pairs={{0,4},{4,0},{8,12},{12,8},{16,20},{20,16},{24,28},{28,24},{1,5},{5... | collective-permute-start | bytes 2359304 | tf_op jit(solution)/shard_map/ppermute | solution.py:387
  703.2 90.5 %collective-permute-start.54 = (bf16[1024,1024]{1,0:T(8,128)(2,1)}, bf16[1024,1024]{1,0:T(8,128)(2,1)S(1)}, u32[]{:S(2)}, u32[]{:S(2)}) collective-permute-start(bf16[1024,1024]{1,0:T(8,128)(2,1)} %get-tuple-element.92), channel_id=1, source_target_pairs={{0,2},{2,0},{1,3},{3,1},{4,6},{6,4},{5,7},{7,5},{8,10},{10,8},{9,1... | collective-permute-start | bytes 6291464 | tf_op jit(solution)/shard_map/ppermute | solution.py:376
  703.2 90.5 %collective-permute-start.49 = (bf16[1024,1024]{1,0:T(8,128)(2,1)}, bf16[1024,1024]{1,0:T(8,128)(2,1)}, u32[]{:S(2)}, u32[]{:S(2)}) collective-permute-start(bf16[1024,1024]{1,0:T(8,128)(2,1)} %get-tuple-element.94), channel_id=1, source_target_pairs={{0,2},{2,0},{1,3},{3,1},{4,6},{6,4},{5,7},{7,5},{8,10},{10,8},{9,1... | collective-permute-start | bytes 6291464 | tf_op jit(solution)/shard_map/ppermute | solution.py:376
  703.7 34.0 %collective-permute-start.58 = (bf16[256,2048]{1,0:T(8,128)(2,1)}, bf16[256,2048]{1,0:T(8,128)(2,1)}, u32[]{:S(2)}, u32[]{:S(2)}) collective-permute-start(bf16[256,2048]{1,0:T(8,128)(2,1)} %constant_dynamic-slice_fusion.12), channel_id=1, source_target_pairs={{0,4},{4,0},{8,12},{12,8},{16,20},{20,16},{24,28},{28,24},{1,5},{5... | collective-permute-start | bytes 3145736 | tf_op jit(solution)/shard_map/ppermute | solution.py:387
  737.7 24.2 %collective-permute-start.43 = (bf16[256,2048]{1,0:T(8,128)(2,1)S(1)}, bf16[256,2048]{1,0:T(8,128)(2,1)S(1)}, u32[]{:S(2)}, u32[]{:S(2)}) collective-permute-start(bf16[256,2048]{1,0:T(8,128)(2,1)S(1)} %fusion.137), channel_id=1, source_target_pairs={{0,1},{1,0},{2,3},{3,2},{4,5},{5,4},{6,7},{7,6},{8,9},{9,8},{10,11... | collective-permute-start | bytes 3145736 | tf_op jit(solution)/shard_map/ppermute | solution.py:397
  742.1 48.0 %collective-permute-start.64 = (bf16[1024,768]{1,0:T(8,128)(2,1)S(1)}, bf16[1024,768]{1,0:T(8,128)(2,1)S(1)}, u32[]{:S(2)}, u32[]{:S(2)}) collective-permute-start(bf16[1024,768]{1,0:T(8,128)(2,1)S(1)} %slice.838), channel_id=1, source_target_pairs={{0,2},{2,0},{1,3},{3,1},{4,6},{6,4},{5,7},{7,5},{8,10},{10,8},{9,1... | collective-permute-start | bytes 4718600 | tf_op jit(solution)/shard_map/ppermute | solution.py:376
  762.0 23.3 %collective-permute-start.40 = (bf16[256,2048]{1,0:T(8,128)(2,1)S(1)}, bf16[256,2048]{1,0:T(8,128)(2,1)S(1)}, u32[]{:S(2)}, u32[]{:S(2)}) collective-permute-start(bf16[256,2048]{1,0:T(8,128)(2,1)S(1)} %fusion.136), channel_id=1, source_target_pairs={{0,1},{1,0},{2,3},{3,2},{4,5},{5,4},{6,7},{7,6},{8,9},{9,8},{10,11... | collective-permute-start | bytes 3145736 | tf_op jit(solution)/shard_map/ppermute | solution.py:397
  790.0 512.1 %collective-permute-start.44 = (f32[256,512]{1,0:T(8,128)}, f32[256,512]{1,0:T(8,128)}, u32[]{:S(2)}, u32[]{:S(2)}) collective-permute-start(f32[256,512]{1,0:T(8,128)} %constant_dynamic-slice_fusion.25), channel_id=1, source_target_pairs={{0,2},{2,0},{1,3},{3,1},{4,6},{6,4},{5,7},{7,5},{8,10},{10,8},{9,1... | collective-permute-start | bytes 1572872 | tf_op jit(solution)/shard_map/ppermute | solution.py:376
  793.5 509.8 %collective-permute-start.41 = (f32[256,512]{1,0:T(8,128)}, f32[256,512]{1,0:T(8,128)}, u32[]{:S(2)}, u32[]{:S(2)}) collective-permute-start(f32[256,512]{1,0:T(8,128)} %constant_dynamic-slice_fusion.26), channel_id=1, source_target_pairs={{0,2},{2,0},{1,3},{3,1},{4,6},{6,4},{5,7},{7,5},{8,10},{10,8},{9,1... | collective-permute-start | bytes 1572872 | tf_op jit(solution)/shard_map/ppermute | solution.py:376
  (194 other events, 2347.5 us)

commit v2 on v1

v2 whole, which is shorter than its diff:
```python
import functools
import math

import jax
import jax.numpy as jnp
from jax import lax
from jax.experimental import pallas as pl
from jax.experimental.pallas import tpu as pltpu
from jax.sharding import PartitionSpec as P

D = 2048
HEAD = 128
LEN = 1024
EPS = 1e-05
THETA = 10000.0
NEG = -1e30

BF = jnp.bfloat16
F32 = jnp.float32


def rope_tables(places):
    half_width = HEAD // 2
    frequency = jnp.exp(
        jnp.arange(half_width).astype(F32) * (-2.0 * math.log(THETA) / HEAD)
    )
    angles = places.astype(F32)[:, None] * frequency[None, :]
    cosine, sine_table = jnp.cos(angles), jnp.sin(angles)
    return (
        jnp.concatenate([cosine, cosine], axis=1),
        jnp.concatenate([-sine_table, sine_table], axis=1),
    )


def dot(left, right):
    return jnp.dot(left, right, preferred_element_type=F32)


def contract_rows(left, right):
    return lax.dot_general(left, right, (((0,), (0,)), ((), ())), preferred_element_type=F32)


def contract_cols(left, right):
    return lax.dot_general(left, right, (((1,), (1,)), ((), ())), preferred_element_type=F32)


def take(operand, index, size, axis):
    return lax.dynamic_slice_in_dim(operand, index * size, size, axis)


def swap_halves(operand, axis):
    half = operand.shape[axis] // 2
    return jnp.concatenate(
        [
            lax.slice_in_dim(operand, half, 2 * half, axis=axis),
            lax.slice_in_dim(operand, 0, half, axis=axis),
        ],
        axis=axis,
    )


def ordered(first, mine, other, axis):
    return jnp.concatenate(
        [jnp.where(first, mine, other), jnp.where(first, other, mine)], axis=axis
    )


def add_low(left, right):
    return (left.astype(F32) + right.astype(F32)).astype(BF)


MESH = pl.DeviceIdType.MESH


def line_kernel(sizes, spots, chunk, lag, ahead, deep, *refs):
    count = len(sizes)
    pieces = refs[:count]
    out = refs[count]
    held, got_in, got_mid, load, send_in, send_mid, send_out, send_side, in_sem, mid_sem, out_sem, side_sem, keep = refs[count + 1:]
    places = lax.axis_size("dp") // 2
    dp = lax.axis_index("dp")
    row = lax.axis_index("row")
    col = lax.axis_index("col")
    place, side = dp // 2, dp % 2
    half = places // 2
    low = place < half
    depth = jnp.where(low, place, places - 1 - place)
    is_mid = depth == half - 1
    is_end = depth == 0
    to_in = jnp.where(low, place + 1, place - 1)
    to_out = jnp.where(low, place - 1, place + 1)
    inner = (to_in * 2 + side, row, col)
    outer = (jnp.clip(to_out, 0, places - 1) * 2 + side, row, col)
    other = (dp + 1 - 2 * side, row, col)
    total_rows = held.shape[0]
    steps = total_rows // chunk

    loads = []
    for i in range(count):
        rows = sizes[i]
        at = pl.multiple_of(spots[i](row), 16)
        loads.append(pltpu.make_async_copy(pieces[i], held.at[pl.ds(at, rows)], load.at[i]))
        loads[-1].start()

    barrier = pltpu.get_barrier_semaphore()
    pl.semaphore_signal(barrier, inc=1, device_id=inner, device_id_type=MESH)
    pl.semaphore_signal(barrier, inc=1, device_id=other, device_id_type=MESH)

    @pl.when(jnp.logical_not(is_end))
    def _():
        pl.semaphore_signal(barrier, inc=1, device_id=outer, device_id_type=MESH)
        pl.semaphore_wait(barrier, 3)

    @pl.when(is_end)
    def _():
        pl.semaphore_wait(barrier, 2)

    for copy in loads:
        copy.wait()

    def at(t):
        return pl.ds(pl.multiple_of(t * chunk, chunk), chunk)

    def inward(t):
        return pltpu.make_async_remote_copy(
            src_ref=held.at[at(t)], dst_ref=got_in.at[at(t)], send_sem=send_in.at[t],
            recv_sem=in_sem.at[t], device_id=inner, device_id_type=MESH)

    def middle(t):
        return pltpu.make_async_remote_copy(
            src_ref=held.at[at(t)], dst_ref=got_mid.at[at(t)], send_sem=send_mid.at[t],
            recv_sem=mid_sem.at[t], device_id=inner, device_id_type=MESH)

    def outward(t, source):
        return pltpu.make_async_remote_copy(
            src_ref=source, dst_ref=out.at[side, at(t)], send_sem=send_out.at[t],
            recv_sem=out_sem.at[t], device_id=outer, device_id_type=MESH)

    def across(t, source):
        return pltpu.make_async_remote_copy(
            src_ref=source, dst_ref=out.at[side, at(t)], send_sem=send_side.at[t],
            recv_sem=side_sem.at[t], device_id=other, device_id_type=MESH)

    def store(t):
        return pltpu.make_async_copy(got_in.at[at(t)], out.at[side, at(t)], keep.at[t])

    def mid_loop(t, _):
        @pl.when(t < steps)
        def _():
            @pl.when(jnp.logical_not(is_end))
            def _():
                inward(t).wait_recv()
                held[at(t)] = (held[at(t)].astype(F32) + got_in[at(t)].astype(F32)).astype(BF)
            @pl.when(t >= deep)
            def _():
                middle(t - deep).wait_send()
            middle(t).start()

        @pl.when(t >= ahead)
        def _():
            u = t - ahead
            middle(u).wait_recv()
            got_in[at(u)] = (held[at(u)].astype(F32) + got_mid[at(u)].astype(F32)).astype(BF)
            store(u).start()
            @pl.when(u >= deep)
            def _():
                @pl.when(jnp.logical_not(is_end))
                def _():
                    outward(u - deep, got_in.at[at(u)]).wait_send()
                across(u - deep, got_in.at[at(u)]).wait_send()
            @pl.when(jnp.logical_not(is_end))
            def _():
                outward(u, got_in.at[at(u)]).start()
            across(u, got_in.at[at(u)]).start()
        return 0

    def far_loop(t, _):
        @pl.when(t < steps)
        def _():
            @pl.when(jnp.logical_not(is_end))
            def _():
                inward(t).wait_recv()
                held[at(t)] = (held[at(t)].astype(F32) + got_in[at(t)].astype(F32)).astype(BF)
            @pl.when(t >= deep)
            def _():
                inward(t - deep).wait_send()
            inward(t).start()

        @pl.when(t >= lag)
        def _():
            u = t - lag
            outward(u, out.at[side, at(u)]).wait_recv()
            @pl.when(u >= deep)
            def _():
                @pl.when(jnp.logical_not(is_end))
                def _():
                    outward(u - deep, out.at[side, at(u)]).wait_send()
                across(u - deep, out.at[side, at(u)]).wait_send()
            @pl.when(jnp.logical_not(is_end))
            def _():
                outward(u, out.at[side, at(u)]).start()
            across(u, out.at[side, at(u)]).start()
        return 0

    @pl.when(is_mid)
    def _():
        lax.fori_loop(0, steps + ahead, mid_loop, 0)
        def finish(t, _):
            store(t).wait()
            across(t, got_in.at[at(t)]).wait_recv()
            @pl.when(t >= steps - deep)
            def _():
                middle(t).wait_send()
                across(t, got_in.at[at(t)]).wait_send()
                @pl.when(jnp.logical_not(is_end))
                def _():
                    outward(t, got_in.at[at(t)]).wait_send()
            return 0
        lax.fori_loop(0, steps, finish, 0)

    @pl.when(jnp.logical_not(is_mid))
    def _():
        lax.fori_loop(0, steps + lag, far_loop, 0)
        def finish(t, _):
            across(t, out.at[side, at(t)]).wait_recv()
            @pl.when(t >= steps - deep)
            def _():
                inward(t).wait_send()
                across(t, out.at[side, at(t)]).wait_send()
                @pl.when(jnp.logical_not(is_end))
                def _():
                    outward(t, out.at[side, at(t)]).wait_send()
            return 0
        lax.fori_loop(0, steps, finish, 0)


def line_sum(pieces, spots, chunk, lag=8, ahead=2, deep=2):
    sizes = [p.shape[0] for p in pieces]
    rows, width = sum(sizes), pieces[0].shape[1]
    steps = rows // chunk
    dma = pltpu.SemaphoreType.DMA
    return pl.pallas_call(
        functools.partial(line_kernel, sizes, spots, chunk, lag, ahead, deep),
        out_shape=jax.ShapeDtypeStruct((2, rows, width), BF),
        in_specs=[pl.BlockSpec(memory_space=pl.ANY)] * len(pieces),
        out_specs=pl.BlockSpec(memory_space=pl.ANY),
        scratch_shapes=[pltpu.VMEM((rows, width), BF)] * 3 + [dma((len(pieces),))] + [dma((steps,))] * 9,
        compiler_params=pltpu.CompilerParams(collective_id=0, has_side_effects=True, vmem_limit_bytes=56 * 2**20),
        name="line_sum",
    )(*pieces)


def pack(operand, width):
    rows, columns = operand.shape
    if columns == width:
        return operand
    if columns > width:
        return jnp.concatenate(
            [operand[:, i : i + width] for i in range(0, columns, width)], axis=0
        )
    times = width // columns
    step = rows // times
    return jnp.concatenate([operand[i * step : (i + 1) * step] for i in range(times)], axis=1)


def unpack(operand, columns):
    rows, width = operand.shape
    if columns == width:
        return operand
    if columns > width:
        step = rows * width // columns
        return jnp.concatenate(
            [operand[i * step : (i + 1) * step] for i in range(columns // width)], axis=1
        )
    return jnp.concatenate(
        [operand[:, i : i + columns] for i in range(0, width, columns)], axis=0
    )


def butterfly(operand, axis):
    size = lax.axis_size(axis)
    step = 1
    while step < size:
        operand = operand + lax.ppermute(operand, axis, [(i, i ^ step) for i in range(size)])
        step *= 2
    return operand


def turned(operand, cosine, sine_table):
    return operand * cosine + pltpu.roll(operand, HEAD // 2, 1) * sine_table


def allowed_pairs(spot_col, spot_row):
    return (spot_col[:, 0:1] == spot_row[0:1, :]) & (spot_row[1:2, :] <= spot_col[:, 1:2])


def attention_kernel(
    x_ref, own_ref, got_ref, out_own, out_got, cos_ref, sin_ref, col_ref, row_ref, *refs
):
    earlier, (q_out, k_out, v_out, att_out, lse_out, kept, sent) = refs[:-7], refs[-7:]
    half = x_ref.shape[1] // 2
    wide = out_own.shape[0]
    own = kept.shape[0]
    near, far = x_ref[:, :half], x_ref[:, half:]
    cosine, sine_table = cos_ref[...], sin_ref[...]
    for which, out in enumerate((q_out, k_out, v_out)):
        at = slice(which * wide, (which + 1) * wide)
        raw = dot(near, own_ref[:, at]) + dot(far, got_ref[:, at])
        for h in range(wide // HEAD):
            head = slice(h * HEAD, (h + 1) * HEAD)
            value = raw[:, head]
            if which < 2:
                value = turned(value, cosine, sine_table)
            out[:, head] = value.astype(BF)
    allowed = allowed_pairs(col_ref[...], row_ref[...])
    for h in range(wide // HEAD):
        head = slice(h * HEAD, (h + 1) * HEAD)
        keys, values = k_out[:, head], v_out[:, head]
        if earlier:
            keys = jnp.concatenate([earlier[0][:, head], keys], axis=0)
            values = jnp.concatenate([earlier[1][:, head], values], axis=0)
        scores = contract_cols(q_out[:, head], keys) * (1.0 / math.sqrt(HEAD))
        scores = jnp.where(allowed, scores, NEG)
        row_max = jnp.max(scores, axis=-1, keepdims=True)
        shares = jnp.exp(scores - row_max)
        totals = jnp.sum(shares, axis=-1, keepdims=True)
        shares = (shares / totals).astype(BF)
        att_out[:, head] = dot(shares, values).astype(BF)
        lse_out[:, head] = jnp.broadcast_to(row_max + jnp.log(totals), (2 * own, HEAD))
    near, far = dot(att_out[...], out_own[...]), dot(att_out[...], out_got[...])
    kept[:, :half] = near[:own]
    kept[:, half:] = far[:own]
    sent[:, :half] = far[own:].astype(BF)
    sent[:, half:] = near[own:].astype(BF)


def attention_back_kernel(
    g_ref, out_own, out_got, cos_ref, sin_ref, col_ref, row_ref, lse_ref, q_ref, k_ref, v_ref, *refs
):
    span, wide = q_ref.shape
    half = g_ref.shape[1] // 2
    factor = 1.0 / math.sqrt(HEAD)
    cosine, sine_table = cos_ref[...], -sin_ref[...]
    grads = contract_cols(g_ref[:, :half], out_own[...])
    grads = (grads + contract_cols(g_ref[:, half:], out_got[...])).astype(BF)
    allowed = allowed_pairs(col_ref[...], row_ref[...])
    last = len(refs) > 3
    for h in range(wide // HEAD):
        head = slice(h * HEAD, (h + 1) * HEAD)
        queries, gradient = q_ref[:, head], grads[:, head]
        keys, values = k_ref[:, head], v_ref[:, head]
        if last:
            keys = jnp.concatenate([refs[0][:, head], keys], axis=0)
            values = jnp.concatenate([refs[1][:, head], values], axis=0)
        scores = jnp.where(allowed, contract_cols(queries, keys) * factor, NEG)
        shares = jnp.exp(scores - lse_ref[:, h * HEAD : h * HEAD + 1])
        grad_shares = contract_cols(gradient, values)
        centre = jnp.sum(shares * grad_shares, axis=-1, keepdims=True)
        grad_scores = (shares * (grad_shares - centre)).astype(BF)
        grad_q = turned(dot(grad_scores, keys) * factor, cosine, sine_table)
        grad_k = contract_rows(grad_scores, queries) * factor
        grad_v = contract_rows(shares.astype(BF), gradient)
        if not last:
            q_out, k_out, v_out = refs
            q_out[:, head] = grad_q.astype(BF)
            k_out[:, head] = grad_k
            v_out[:, head] = grad_v
        else:
            cos_first, sin_first, k_part, v_part, first_out, back_out = refs[2:]
            back_out[:, head] = grad_q.astype(BF)
            at = slice(wide + h * HEAD, wide + (h + 1) * HEAD)
            back_out[:, at] = turned(grad_k[span:], cosine, sine_table).astype(BF)
            first = grad_k[:span] + k_part[:, head]
            first_out[:, head] = turned(first, cos_first[...], -sin_first[...]).astype(BF)
            at = slice(2 * wide + h * HEAD, 2 * wide + (h + 1) * HEAD)
            back_out[:, at] = grad_v[span:].astype(BF)
            at = slice(wide + h * HEAD, wide + (h + 1) * HEAD)
            first_out[:, at] = (grad_v[:span] + v_part[:, head]).astype(BF)


def in_vmem(kernel, name, out_shape, operands):
    return pl.pallas_call(
        kernel,
        out_shape=out_shape,
        in_specs=[pl.BlockSpec(memory_space=pltpu.VMEM)] * len(operands),
        out_specs=[pl.BlockSpec(memory_space=pltpu.VMEM)] * len(out_shape),
        compiler_params=pltpu.CompilerParams(vmem_limit_bytes=52 * 2**20),
        cost_estimate=pl.CostEstimate(
            flops=8 * 10**9, bytes_accessed=2 * 10**7, transcendentals=2 * 10**6
        ),
        name=name,
    )(*operands)


def moments(operand):
    average = jnp.mean(operand, axis=-1, keepdims=True)
    centre = operand - average
    factor = lax.rsqrt(jnp.mean(centre * centre, axis=-1, keepdims=True) + EPS)
    return average, factor


def normalize_back(gradient, normed, factor):
    mean = jnp.mean(gradient, axis=-1, keepdims=True)
    crossed = jnp.mean(gradient * normed, axis=-1, keepdims=True)
    return factor * (gradient - mean - normed * crossed)


def feed_forward_kernel(
    r_ref, x_ref, gate_own, gate_got, up_own, up_got, down_own, down_got,
    gate_out, up_out, act_keep, act_give, kept, sent, total, *, side_steps,
):
    step, last = pl.program_id(0), pl.num_programs(0) - 1
    half = x_ref.shape[1] // 2
    own = kept.shape[0]
    near, far = x_ref[:, :half], x_ref[:, half:]
    gate = dot(near, gate_own[...]) + dot(far, gate_got[...])
    up = dot(near, up_own[...]) + dot(far, up_got[...])
    gate_out[...] = gate
    up_out[...] = up
    act = (gate * jax.nn.sigmoid(gate) * up).astype(BF)
    mine = step // side_steps == r_ref[1]

    @pl.when(mine)
    def _():
        act_keep[...] = act

    @pl.when(jnp.logical_not(mine))
    def _():
        act_give[...] = act

    near, far = dot(act, down_own[...]), dot(act, down_got[...])

    @pl.when(step == 0)
    def _():
        total[:, :half] = near
        total[:, half:] = far

    @pl.when(step > 0)
    def _():
        total[:, :half] += near
        total[:, half:] += far

    @pl.when(step == last)
    def _():
        kept[...] = total[:own]
        sent[:, :half] = total[own:, half:].astype(BF)
        sent[:, half:] = total[own:, :half].astype(BF)


def feed_forward_back_kernel(
    r_ref, g_ref, gate_ref, up_ref, gate_own, gate_got, up_own, up_got, down_own, down_got,
    gate_keep, gate_give, up_keep, up_give, kept, sent, total, *, side_steps,
):
    step, last = pl.program_id(0), pl.num_programs(0) - 1
    half = g_ref.shape[1] // 2
    own = kept.shape[0]
    grad = contract_cols(g_ref[:, :half], down_own[...]) + contract_cols(
        g_ref[:, half:], down_got[...]
    )
    gate, up = gate_ref[...], up_ref[...]
    sigmoid = jax.nn.sigmoid(gate)
    gate_back = (grad * up * sigmoid * (1.0 + gate * (1.0 - sigmoid))).astype(BF)
    up_back = (grad * gate * sigmoid).astype(BF)
    mine = step // side_steps == r_ref[1]

    @pl.when(mine)
    def _():
        gate_keep[...] = gate_back
        up_keep[...] = up_back

    @pl.when(jnp.logical_not(mine))
    def _():
        gate_give[...] = gate_back
        up_give[...] = up_back

    near = contract_cols(gate_back, gate_own[...]) + contract_cols(up_back, up_own[...])
    far = contract_cols(gate_back, gate_got[...]) + contract_cols(up_back, up_got[...])

    @pl.when(step == 0)
    def _():
        total[:, :half] = near
        total[:, half:] = far

    @pl.when(step > 0)
    def _():
        total[:, :half] += near
        total[:, half:] += far

    @pl.when(step == last)
    def _():
        kept[...] = total[:own]
        sent[:, :half] = total[own:, half:].astype(BF)
        sent[:, half:] = total[own:, :half].astype(BF)


def feed_forward(back, where, operand, saved, weights, got, units, tile):
    span, width = operand.shape
    half, own, steps = width // 2, span // 2, units // tile
    side_steps = steps // 2
    gate, up, down = weights
    gate_got, up_got, down_got = got

    def mine(i, r):
        return (0, jnp.clip(i - r[1] * side_steps, 0, side_steps - 1))

    def other(i, r):
        return (0, jnp.clip(i - (1 - r[1]) * side_steps, 0, side_steps - 1))

    whole = pl.BlockSpec((span, width), lambda i, r: (0, 0))
    wide = pl.BlockSpec((span, tile), lambda i, r: (0, i))
    into_own = pl.BlockSpec((half, tile), lambda i, r: (0, r[0] * steps + i))
    into_got = pl.BlockSpec((half, tile), lambda i, r: (0, i))
    back_own = pl.BlockSpec((tile, half), lambda i, r: (r[0] * steps + i, 0))
    back_got = pl.BlockSpec((tile, half), lambda i, r: (i, 0))
    weight_specs = [into_own, into_got, into_own, into_got, back_own, back_got]
    keep, give = pl.BlockSpec((span, tile), mine), pl.BlockSpec((span, tile), other)
    ends = [pl.BlockSpec((own, width), lambda i, r: (0, 0))] * 2
    part = jax.ShapeDtypeStruct((span, units // 2), BF)
    full = jax.ShapeDtypeStruct((span, units), F32)
    end_shapes = [
        jax.ShapeDtypeStruct((own, width), F32),
        jax.ShapeDtypeStruct((own, width), BF),
    ]
    if back:
        kernel = feed_forward_back_kernel
        in_specs = [whole, wide, wide] + weight_specs
        out_specs = [keep, give, keep, give] + ends
        out_shape = [part] * 4 + end_shapes
    else:
        kernel = feed_forward_kernel
        in_specs = [whole] + weight_specs
        out_specs = [wide, wide, keep, give] + ends
        out_shape = [full] * 2 + [part] * 2 + end_shapes
    return pl.pallas_call(
        functools.partial(kernel, side_steps=side_steps),
        out_shape=out_shape,
        grid_spec=pltpu.PrefetchScalarGridSpec(
            num_scalar_prefetch=1,
            grid=(steps,),
            in_specs=in_specs,
            out_specs=out_specs,
            scratch_shapes=[pltpu.VMEM((span, width), F32)],
        ),
        compiler_params=pltpu.CompilerParams(vmem_limit_bytes=52 * 2**20),
        cost_estimate=pl.CostEstimate(
            flops=6 * span * width * units,
            bytes_accessed=6 * width * units + 12 * span * units,
            transcendentals=span * units,
        ),
        name="feed_forward_back" if back else "feed_forward",
    )(where, operand, *saved, gate, gate_got, up, up_got, down, down_got)


def widen(sums, shape, block, spot):
    rows, columns = block

    def kernel(in_ref, out_ref):
        out_ref[...] = in_ref[0].astype(F32)

    return pl.pallas_call(
        kernel,
        out_shape=jax.ShapeDtypeStruct(shape, F32),
        grid=(shape[1] // columns, shape[0] // rows),
        in_specs=[pl.BlockSpec((1, rows, columns), spot)],
        out_specs=pl.BlockSpec((rows, columns), lambda j, i: (i, j)),
        compiler_params=pltpu.CompilerParams(vmem_limit_bytes=32 * 2**20),
        cost_estimate=pl.CostEstimate(
            flops=0, bytes_accessed=6 * shape[0] * shape[1], transcendentals=0
        ),
        name="widen",
    )(sums)


def widen_four(sums, shape, starts, part):
    rows, columns = shape
    qk, v, o = (start // part for start in starts)

    def kernel(qk_a, qk_b, v_a, v_b, o_ref, q_out, k_out, v_out, o_out):
        step = pl.program_id(0)
        o_out[...] = o_ref[0].astype(F32)
        for core in range(2):
            for pair, out, at in ((0, q_out, 0), (1, k_out, 2)):
                for x, ref in enumerate((qk_a, qk_b)):
                    spot = (2 * core + x) * part
                    source = (at + core) * part
                    out[:, spot : spot + part] = ref[0, :, source : source + part].astype(F32)
        for high in range(2):

            @pl.when(step // 2 == high)
            def _():
                for core in range(2):
                    for x, ref in enumerate((v_a, v_b)):
                        spot = (2 * core + x) * part
                        source = (2 * high + core) * part
                        v_out[:, spot : spot + part] = ref[0, :, source : source + part].astype(F32)

    block = (1, part, columns)
    return pl.pallas_call(
        kernel,
        out_shape=[jax.ShapeDtypeStruct(shape, F32)] * 4,
        grid=(rows // part,),
        in_specs=[
            pl.BlockSpec(block, lambda i: (0, qk + i, 0)),
            pl.BlockSpec(block, lambda i: (1, qk + i, 0)),
            pl.BlockSpec(block, lambda i: (0, v + i % 2, 0)),
            pl.BlockSpec(block, lambda i: (1, v + i % 2, 0)),
            pl.BlockSpec(block, lambda i: (i % 2, o + i // 2, 0)),
        ],
        out_specs=[pl.BlockSpec((part, columns), lambda i: (i, 0))] * 4,
        compiler_params=pltpu.CompilerParams(vmem_limit_bytes=32 * 2**20),
        name="widen_four",
    )(sums, sums, sums, sums, sums)


def body(
    tokens,
    teacher,
    segments,
    valid_mask,
    query_weight,
    key_weight,
    value_weight,
    output_weight,
    gate_weight,
    up_weight,
    down_weight,
):
    rows = tokens.shape[0]
    cols = lax.axis_size("col")
    row = lax.axis_index("row")
    col = lax.axis_index("col")
    side = lax.axis_index("dp") % 2
    sides = [(i, i ^ 1) for i in range(lax.axis_size("dp"))]
    block = tokens.shape[1]
    half_width = block * cols
    wide = query_weight.shape[1] // 2
    units = gate_weight.shape[1] // 2
    part_units = units // 2
    part_wide = wide // 2
    tile = min(512, part_units)
    span = rows // 2
    own = span // 2
    first_row = row == 0
    where = jnp.stack([row, side]).astype(jnp.int32)
    tie = lax.optimization_barrier

    def swap(operand):
        return lax.ppermute(operand, "row", [(0, 1), (1, 0)])

    def cross(operand):
        return lax.ppermute(operand, "dp", sides)

    def gather_blocks(operand):
        if cols == 2:
            got = lax.ppermute(operand, "col", [(0, 1), (1, 0)])
            return ordered(col == 0, operand, got, 1)
        return lax.all_gather(operand, "col", axis=1, tiled=True)

    def from_chips(sent):
        if cols == 2:
            return lax.ppermute(sent.astype(BF), "col", [(0, 1), (1, 0)])
        sent = sent.astype(F32)
        return lax.psum(sent, "col") - sent

    def both_cores(kept):
        return jnp.concatenate([kept, swap(swap_halves(kept, 1))], axis=0)

    def from_cores(first, second):
        other = swap(swap_halves(jnp.concatenate([first, second], axis=0), 1))
        return [first, other[:own], second, other[own:]]

    def sum_cores(near, far):
        sent = jnp.concatenate([far[own:], near[own:]], axis=1).astype(BF)
        return jnp.concatenate([near[:own], far[:own]], axis=1) + swap(sent).astype(F32)

    def local_order(vector):
        pieces = []
        for j in range(2):
            piece = vector[j * span : (j + 1) * span]
            pieces.append(ordered(first_row, piece[:own], piece[own:], 0))
        return pieces

    blocks = []
    for j in range(2):
        piece = tokens[j * span : (j + 1) * span]
        blocks.append(gather_blocks(ordered(first_row, piece[:own], piece[own:], 0)))

    def columns_of(core):
        return jnp.concatenate(
            [take(w, core, wide, 1) for w in (query_weight, key_weight, value_weight)], axis=1
        )

    qkv_own, qkv_got = columns_of(row), swap(columns_of(1 - row))
    out_own = take(output_weight, row, wide, 0)
    out_got = swap(take(output_weight, 1 - row, wide, 0))
    weights = (gate_weight, up_weight, down_weight)

    validity = valid_mask.astype(F32)
    token_total = butterfly(jnp.sum(validity).reshape(1, 1), "dp")
    scale = (rows * lax.axis_size("dp")) / token_total
    segs = local_order(segments)
    places = local_order(jnp.arange(rows, dtype=jnp.int32))
    valids = [v[:own, None] for v in local_order(validity)]
    tables = [rope_tables(p) for p in places]
    spot_cols = [jnp.stack([g, p], axis=1) for g, p in zip(segs, places)]
    spot_rows = [
        jnp.stack([jnp.concatenate(segs[: j + 1]), jnp.concatenate(places[: j + 1])])
        for j in range(2)
    ]

    inputs, first_stats, low_first = [], [], []
    query_heads, key_heads, value_heads = [], [], []
    attended, logsums = [], []

    def first_norm(j, half):
        whole = jnp.concatenate([half, swap(swap_halves(half, 0))], axis=1)
        whole_f = whole.astype(F32)
        average, factor = moments(whole_f)
        inputs.append(whole[:own])
        first_stats.append((average[:own], factor[:own]))
        low_first.append(((whole_f - average) * factor).astype(BF))
        return low_first[j]

    def attention(j, operand):
        out = jax.ShapeDtypeStruct((span, wide), BF)
        q, k, v, heads, logsum, kept, sent = in_vmem(
            attention_kernel,
            "attention",
            [out] * 4
            + [
                jax.ShapeDtypeStruct((span, wide), F32),
                jax.ShapeDtypeStruct((own, 2 * half_width), F32),
                jax.ShapeDtypeStruct((own, 2 * half_width), BF),
            ],
            [operand, qkv_own, qkv_got, out_own, out_got, *tables[j], spot_cols[j], spot_rows[j]]
            + [x for pair in zip(key_heads, value_heads) for x in pair],
        )
        query_heads.append(q)
        key_heads.append(k)
        value_heads.append(v)
        attended.append(heads)
        logsums.append(logsum)
        return kept, sent

    hidden, second_stats, low_second = [], [], []

    def second_norm(j, part, got):
        hidden.append(inputs[j].astype(F32) + (part + got.astype(F32)))
        average, factor = moments(hidden[j])
        second_stats.append((average, factor))
        low_second.append(both_cores(((hidden[j] - average) * factor).astype(BF)))
        return low_second[j]

    saved, acts, act_gives = [], [], []

    def forward(operand, received):
        return feed_forward(False, where, operand, (), weights, received, units, tile)

    def after_forward(j, raw):
        gate_out, up_out, act_keep, act_give, kept, sent = raw
        saved.append((gate_out, up_out))
        acts.append(act_keep)
        act_gives.append(act_give)
        piece = teacher[j * span : (j + 1) * span]
        piece = ordered(first_row, piece[:own], piece[own:], 0)
        near, far = piece[:own].astype(F32), swap(piece[own:]).astype(F32)
        minus = [jnp.where(col == b, near, 0.0) for b in range(cols)]
        minus += [jnp.where(col == b, far, 0.0) for b in range(cols)]
        part = kept + swap(sent).astype(F32) - jnp.concatenate(minus, axis=1)
        return part, (near, far)

    outputs, errors, grad_results, low_results = [], [], [], []

    def loss_of(j, part, got, targets):
        near, far = targets
        error = hidden[j] + (part + got.astype(F32))
        near_error = take(error[:, :half_width], col, block, 1)
        far_error = take(error[:, half_width:], col, block, 1)
        outputs.append(
            ordered(
                first_row,
                (near_error + near).astype(BF),
                swap((far_error + far).astype(BF)),
                0,
            )
        )
        errors.append(
            0.5 * jnp.sum(valids[j] * (near_error * near_error + far_error * far_error))
        )
        grad_results.append(scale * valids[j] * error)
        low_results.append(both_cores(grad_results[j].astype(BF)))
        return low_results[j]

    def backward(j, operand, received):
        return feed_forward(True, where, operand, saved[j], weights, received, units, tile)

    grad_hiddens, low_hiddens = [], []

    def second_norm_back(j, part, got):
        gradient = part + got.astype(F32)
        average, factor = second_stats[j]
        normed = (hidden[j] - average) * factor
        grad_hiddens.append(grad_results[j] + normalize_back(gradient, normed, factor))
        low_hiddens.append(both_cores(grad_hiddens[j].astype(BF)))
        return low_hiddens[j]

    def attention_back(j, operand, extra):
        first = jax.ShapeDtypeStruct((span, wide), F32)
        shapes = [jax.ShapeDtypeStruct((span, wide), BF), first, first]
        if j == 1:
            shapes = [jax.ShapeDtypeStruct((span, n * wide), BF) for n in (2, 3)]
        return in_vmem(
            attention_back_kernel,
            "attention_back",
            shapes,
            [
                operand,
                out_own,
                out_got,
                *tables[j],
                spot_cols[j],
                spot_rows[j],
                logsums[j],
                query_heads[j],
                key_heads[j],
                value_heads[j],
                *extra,
            ],
        )

    def joined(pair):
        return pair[0] + swap(pair[1]).astype(F32)

    part_a = joined(attention(0, first_norm(0, blocks[0])))
    operand = first_norm(1, blocks[1])
    operand, part_a, low, mine, scale = tie(
        (operand, part_a, part_a.astype(BF), low_first[0][:own], scale)
    )
    got_a, first_a = from_chips(low), cross(mine)
    pair = attention(1, operand)
    pair, got_a, first_a = tie((pair, got_a, first_a))
    received = (
        swap(take(gate_weight, 1 - row, units, 1)),
        swap(take(up_weight, 1 - row, units, 1)),
        swap(take(down_weight, 1 - row, units, 0)),
    )
    part_b = joined(pair)
    two_a = second_norm(0, part_a, got_a)
    two_a, part_b, low, mine, received = tie(
        (two_a, part_b, part_b.astype(BF), low_first[1][:own], received)
    )
    got_b, first_b = from_chips(low), cross(mine)
    raw = forward(two_a, received)
    raw, got_b, first_b = tie((raw, got_b, first_b))
    part_a, targets_a = after_forward(0, raw)
    two_b = second_norm(1, part_b, got_b)
    two_b, part_a, low, mine = tie((two_b, part_a, part_a.astype(BF), two_a[:own]))
    got_a, cross_two_a = from_chips(low), cross(mine)
    raw = forward(two_b, received)
    raw, got_a, cross_two_a = tie((raw, got_a, cross_two_a))
    part_b, targets_b = after_forward(1, raw)
    low_a = loss_of(0, part_a, got_a, targets_a)
    low_a, part_b, low, mine = tie((low_a, part_b, part_b.astype(BF), two_b[:own]))
    got_b, cross_two_b = from_chips(low), cross(mine)
    raw = backward(0, low_a, received)
    raw, got_b, cross_two_b = tie((raw, got_b, cross_two_b))
    ups_a, part_a = raw[:4], joined(raw[4:])
    low_b = loss_of(1, part_b, got_b, targets_b)
    low_b, part_a, low, mine = tie((low_b, part_a, part_a.astype(BF), act_gives[0]))
    got_a, cross_act_a = from_chips(low), cross(mine)
    raw = backward(1, low_b, received)
    raw, got_a, cross_act_a = tie((raw, got_a, cross_act_a))
    ups_b, part_b = raw[:4], joined(raw[4:])
    hidden_a = second_norm_back(0, part_a, got_a)
    hidden_a, part_b, low, mine = tie((hidden_a, part_b, part_b.astype(BF), low_a[:own]))
    got_b, cross_low_a = from_chips(low), cross(mine)
    parts = attention_back(0, hidden_a, [])
    parts, got_b, cross_low_a = tie((parts, got_b, cross_low_a))
    hidden_b = second_norm_back(1, part_b, got_b)
    hidden_b, parts, mine = tie((hidden_b, parts, low_b[:own]))
    cross_low_b = cross(mine)
    first_back, back_b = attention_back(
        1, hidden_b, [key_heads[0], value_heads[0], *tables[0], *parts[1:]]
    )
    first_back, back_b, cross_low_b = tie((first_back, back_b, cross_low_b))
    backs = [jnp.concatenate([parts[0], first_back], axis=1), back_b]
    gate_gives = [u[1] for u in (ups_a, ups_b)]
    up_gives = [u[3] for u in (ups_a, ups_b)]

    def half_columns(operand, which):
        return jnp.concatenate(
            [take(operand[:, i * wide : (i + 1) * wide], which, part_wide, 1) for i in range(3)],
            axis=1,
        )

    def split_rows(full):
        half = full.shape[0] // 2
        return full[:half], swap(full[half:])

    def split_cols(full):
        half = full.shape[1] // 2
        return full[:, :half], swap(full[:, half:])

    def together(lefts, rights):
        return jnp.concatenate(lefts, axis=0), jnp.concatenate(rights, axis=0)

    def product(lefts, rights):
        return contract_rows(lefts, rights).astype(BF)

    back_gives = [half_columns(g, 1 - side) for g in backs]
    hiddens = together(attended, [hidden_a, hidden_b])
    error_sum = (errors[0] + errors[1]).reshape(1, 1)
    hiddens, act_give, backs, back_gives = tie((hiddens, act_gives[1], backs, back_gives))
    cross_act_b = cross(act_give)
    last_parts = [
        sum_cores(contract_cols(g, qkv_own), contract_cols(g, qkv_got)) for g in backs
    ]
    grad_out = product(*hiddens)
    last_parts, grad_out, cross_act_b, error_sum = tie(
        (last_parts, grad_out, cross_act_b, error_sum)
    )
    downs = together(
        [*acts, cross_act_a, cross_act_b], [low_a, low_b, *from_cores(cross_low_a, cross_low_b)]
    )
    downs, gate_gives = tie((downs, gate_gives))
    cross_gates = [cross(g) for g in gate_gives]
    grad_down = product(*downs)
    error_sum = butterfly(error_sum, "row")
    cross_gates, grad_down, error_sum = tie((cross_gates, grad_down, error_sum))
    down_pair = split_cols(grad_down)
    twos = [two_a, two_b, *from_cores(cross_two_a, cross_two_b)]
    gates = together(twos, [ups_a[0], ups_b[0], *cross_gates])
    out_give = take(grad_out, 1 - side, part_wide, 0)
    gates, up_gives = tie((gates, up_gives))
    cross_ups = [cross(g) for g in up_gives]
    grad_gate = product(*gates)
    error_sum = butterfly(error_sum, "col")
    grad_gate, cross_ups, error_sum = tie((grad_gate, cross_ups, error_sum))
    gate_pair = split_rows(grad_gate)
    ups = together(twos, [ups_a[2], ups_b[2], *cross_ups])
    ups, out_give, back_gives = tie((ups, out_give, back_gives))
    grad_out_got = cross(out_give)
    cross_backs = [cross(g) for g in back_gives]
    grad_up = product(*ups)
    error_sum = butterfly(error_sum, "dp")
    grad_up, grad_out_got, cross_backs, error_sum = tie(
        (grad_up, grad_out_got, cross_backs, error_sum)
    )
    up_pair = split_rows(grad_up)
    out_pair = split_cols(add_low(take(grad_out, side, part_wide, 0), grad_out_got))
    qkv_pair = split_rows(
        product(
            *together(
                [*low_first, *from_cores(first_a, first_b)],
                [*[half_columns(g, side) for g in backs], *cross_backs],
            )
        )
    )
    three = [
        ordered(
            first_row,
            qkv_pair[0][:, i * part_wide : (i + 1) * part_wide],
            qkv_pair[1][:, i * part_wide : (i + 1) * part_wide],
            1,
        )
        for i in range(3)
    ]
    pieces, spots, starts = [], [], []
    total = 0
    for pair in (down_pair, gate_pair, up_pair, out_pair):
        packed = [pack(p, half_width) for p in pair]
        size = packed[0].shape[0]
        pieces += packed
        spots += [
            lambda r, total=total, size=size: total + r * size,
            lambda r, total=total, size=size: total + (1 - r) * size,
        ]
        starts.append((total, size))
        total += 2 * size
    for item in (jnp.concatenate(three[:2], axis=1), three[2]):
        packed = pack(item, half_width)
        size = packed.shape[0]
        pieces.append(packed)
        spots.append(lambda r, total=total: total + 0 * r)
        starts.append((total, size))
        total += size
    last_gots = [from_chips(p) for p in last_parts]
    sums = line_sum(pieces, spots, chunk=min(256, total // 8))
    sums, last_parts, last_gots = tie((sums, last_parts, last_gots))

    if cols == 2:
        tall = min(1024, starts[0][1])

        def rows_of(start, size, step):
            def spot(j, i):
                s, rest = i // (2 * step), i % (2 * step)
                return (rest // step, (start + s * size) // tall + rest % step, 0)

            return spot

        def columns_at(start):
            return lambda j, i: (j % 2, (start + (j // 2) * half_width) // tall + i, 0)

        grad_down = widen(
            sums,
            down_weight.shape,
            (tall, half_width),
            rows_of(*starts[0], part_units // tall),
        )
        grad_gate, grad_up = (
            widen(sums, gate_weight.shape, (tall, part_units), columns_at(starts[n][0]))
            for n in (1, 2)
        )
        grad_query, grad_key, grad_value, grad_output = widen_four(
            sums, query_weight.shape, [starts[n][0] for n in (4, 5, 3)], part_wide
        )
    else:

        def blocks_of(which, columns):
            start, size = starts[which]
            return [
                unpack(sums[x, start + s * size : start + (s + 1) * size], columns)
                for s in range(2)
                for x in range(2)
            ]

        grad_down = jnp.concatenate(blocks_of(0, half_width), axis=0).astype(F32)
        grad_gate = jnp.concatenate(blocks_of(1, part_units), axis=1).astype(F32)
        grad_up = jnp.concatenate(blocks_of(2, part_units), axis=1).astype(F32)
        grad_output = jnp.concatenate(blocks_of(3, half_width), axis=0).astype(F32)
        three = [[], [], []]
        qk, v = (
            [unpack(sums[x, starts[n][0] : starts[n][0] + starts[n][1]], k * part_wide) for x in range(2)]
            for n, k in ((4, 4), (5, 2))
        )
        for s in range(2):
            for x in range(2):
                at = s * part_wide
                three[0].append(qk[x][:, at : at + part_wide])
                three[1].append(qk[x][:, 2 * part_wide + at : 2 * part_wide + at + part_wide])
                three[2].append(v[x][:, at : at + part_wide])
        grad_query, grad_key, grad_value = (
            jnp.concatenate(t, axis=1).astype(F32) for t in three
        )

    grad_tokens = []
    for j in range(2):
        gradient = last_parts[j] + last_gots[j].astype(F32)
        average, factor = first_stats[j]
        normed = (inputs[j].astype(F32) - average) * factor
        grads = grad_hiddens[j] + normalize_back(gradient, normed, factor)
        near = take(grads[:, :half_width], col, block, 1)
        far = take(grads[:, half_width:], col, block, 1)
        grad_tokens.append(ordered(first_row, near, swap(far), 0))
    loss_value = (error_sum / token_total)[0, 0]
    return (
        jnp.concatenate(outputs, axis=0),
        loss_value,
        jnp.concatenate(grad_tokens, axis=0),
        grad_query,
        grad_key,
        grad_value,
        grad_output,
        grad_gate,
        grad_up,
        grad_down,
    )


def solution(mesh):
    features = P("dp", ("row", "col"))
    into, back = P("row", "col"), P("col", "row")
    in_specs = (features, features, P("dp"), P("dp"), into, into, into, back, into, into, back)
    out_specs = (features, P(), features, into, into, into, back, into, into, back)
    return jax.shard_map(body, mesh=mesh, in_specs=in_specs, out_specs=out_specs, check_vma=False)
```

time: 1310 us -> 1130 us (0.86)
  Pallas kernels: 450 us -> 645 us
  matrix products: 229 us -> 61.1 us
  waiting for transfers between devices: 253 us -> 105 us
  local copies, waits for them, and re-layouts: 167 us -> 104 us
  starting transfers between devices: 57 us -> 104 us
  other arithmetic: 140 us -> 95.2 us
    pallas_call x0 -> x12, Pallas kernels: none -> 195 us  [the longest x4 102 us: feed_forward(): pl.pallas_call(functools.partial(kernel, side_steps=side_steps), out_shap...]
    dot_general x22 -> x0, matrix products: 94.7 us -> none  [the longest x10 70 us: dot(): return jnp.dot(left, right, preferred_element_type=F32)]
    ppermute x8, waiting for transfers between devices: 98 us -> 14.1 us  [from_chips(): return lax.ppermute(sent.astype(BF), 'col', [(0, 1), (1, 0)])]
    dot_general x9 -> x4, matrix products: 82.4 us -> 12.6 us  [contract_cols(): lax.dot_general(left, right, (((1,), (1,)), ((), ())), preferred_element_...]
    ppermute x15, waiting for transfers between devices: 148 us -> 84.8 us  [cross(): return lax.ppermute(operand, 'dp', sides)]
    ppermute x8, starting transfers between devices: 22.6 us -> 72.3 us  [butterfly(): lax.ppermute(operand, axis, [(i, i ^ step) for i in range(size)])]
    dynamic_slice x20 -> x21, local copies, waits for them, and re-layouts: 50.9 us -> 23.6 us  [take(): return lax.dynamic_slice_in_dim(operand, index * size, size, axis)]
    convert_element_type x22 -> x14, other arithmetic: 53.4 us -> 26.8 us  [the longest x2 6.96 us: second_norm_back(): low_hiddens.append(both_cores(grad_hiddens[j].astype(BF)))]
  transfers between devices with their start and end apart: 65 -> 68, of which waited for: 19 -> 15; matrix products, arithmetic and copies ran while one was open for 39% -> 20% of each run, Pallas kernels for 34% -> 57%
where the time goes in v2:
time: 1130 us; the launch traced here: 1120 us
  Pallas kernels  645 us (57%)
  waiting for transfers between devices  105 us (9%)
  local copies, waits for them, and re-layouts  104 us (9%)
  starting transfers between devices  104 us (9%)
  other arithmetic  95.2 us (8%)
  matrix products  61.1 us (5%)
  between operations  11.5 us (1%)
    pallas_call x1, Pallas kernels, line_sum(): pl.pallas_call(functools.partial(line_kernel, sizes, spots, chunk, lag, a...  450 us
    pallas_call x4, Pallas kernels, feed_forward(): pl.pallas_call(functools.partial(kernel, side_steps=side_steps), out_shap...  102 us
    ppermute x15, waiting for transfers between devices, cross(): return lax.ppermute(operand, 'dp', sides)  84.8 us
    ppermute x8, starting transfers between devices, butterfly(): lax.ppermute(operand, axis, [(i, i ^ step) for i in range(size)])  72.3 us
    pallas_call x4, Pallas kernels, in_vmem(): pl.pallas_call(kernel, out_shape=out_shape, in_specs=[pl.BlockSpec(memory...  53.3 us
    unnamed x307, local copies, waits for them, and re-layouts  51.6 us
    dot_general x5, matrix products, contract_rows(): lax.dot_general(left, right, (((0,), (0,)), ((), ())), preferred_element_...  48.5 us
    pallas_call x3, Pallas kernels, widen(): pl.pallas_call(kernel, out_shape=jax.ShapeDtypeStruct(shape, F32), grid=(...  28.7 us
  transfers between devices with their start and end apart: 68, of which 15 were waited for; matrix products, arithmetic and copies ran while one was open for 20% of the time, Pallas kernels for 57%

profile of v2, /device:TPU:0, one launch (start us, length us, event | category | flops | bytes accessed | tf_op | source)
XLA Modules:
  0.0 1124.9 jit_solution(16026773506687585737)
XLA Ops:
  2.9 3.0 collective-permute-start
  18.6 4.9 constant_dynamic-slice_fusion.17
  23.5 4.9 constant_dynamic-slice_fusion.16
  32.8 4.7 constant_dynamic-slice_fusion.15
  43.7 2.9 collective-permute-start.8
  48.0 4.0 collective-permute-start.9
  59.5 3.1 collective-permute-done.3
  63.2 13.3 %attention.2 = (bf16[512,512]{1,0:T(8,128)(2,1)S(1)}, bf16[512,512]{1,0:T(8,128)(2,1)S(1)}, bf16[512,512]{1,0:T(8,128)(2,1)}, bf16[512,512]{1,0:T(8,128)(2,1)}, ...) custom-call(bf16[512,2048]{1,0:T(8,128)(2,1)} %copy-done.50, ...), custom_call_target="tpu_custom_call" | custom-call | flops 8000000000 | bytes 20000000 | tf_op jit(solution)/shard_map/attention/pallas_call | solution.py:382
  77.6 2.6 constant_dynamic-update-slice_fusion.16
  85.5 15.7 %attention.3 = (bf16[512,512]{1,0:T(8,128)(2,1)S(1)}, bf16[512,512]{1,0:T(8,128)(2,1)S(1)}, bf16[512,512]{1,0:T(8,128)(2,1)}, bf16[512,512]{1,0:T(8,128)(2,1)}, ...) custom-call(bf16[512,2048]{1,0:T(8,128)(2,1)} %get-tuple-element.180.x_ref, ...), custom_call_target="tpu_custom_call" | custom-call | flops 8000000000 | bytes 20000000 | tf_op jit(solution)/shard_map/attention/pallas_call | solution.py:382
  101.2 6.6 collective-permute-done.10
  127.1 24.7 %feed_forward.2 = (f32[512,2048]{1,0:T(8,128)}, f32[512,2048]{1,0:T(8,128)}, bf16[512,1024]{1,0:T(8,128)(2,1)S(1)}, bf16[512,1024]{1,0:T(8,128)(2,1)}, f32[256,2048]{1,0:T(8,128)}, /*index=5*/bf16[256,2048]{1,0:T(8,128)(2,1)}) custom-call(s32[2]{0:T(128)S(1)} %pad_add_fusion.10.r_ref, bf16[512,2048]{1,0:T(8,128)(2,1)} %copy-done.36, ...), custom_call_target="tpu_custom_call" | custom-call | flops 12884901888 | bytes 37748736 | tf_op jit(solution)/shard_map/feed_forward/pallas_call | solution.py:534
  167.1 24.2 %feed_forward.3 = (f32[512,2048]{1,0:T(8,128)}, f32[512,2048]{1,0:T(8,128)}, bf16[512,1024]{1,0:T(8,128)(2,1)S(1)}, bf16[512,1024]{1,0:T(8,128)(2,1)}, f32[256,2048]{1,0:T(8,128)}, /*index=5*/bf16[256,2048]{1,0:T(8,128)(2,1)}) custom-call(s32[2]{0:T(128)S(1)} %pad_add_fusion.10.r_ref, bf16[512,2048]{1,0:T(8,128)(2,1)} %copy-done.38, ...), custom_call_target="tpu_custom_call" | custom-call | flops 12884901888 | bytes 37748736 | tf_op jit(solution)/shard_map/feed_forward/pallas_call | solution.py:534
  208.5 26.4 %feed_forward_back.2 = (bf16[512,1024]{1,0:T(8,128)(2,1)S(1)}, bf16[512,1024]{1,0:T(8,128)(2,1)}, bf16[512,1024]{1,0:T(8,128)(2,1)}, bf16[512,1024]{1,0:T(8,128)...) custom-call(s32[2]{0:T(128)S(1)} %pad_add_fusion.10.r_ref, bf16[512,2048]{1,0:T(8,128)(2,1)} %pad_maximum_fusion.10.g_ref, ...), custom_call_target="tpu_custom_call" | custom-call | flops 12884901888 | bytes 37748736 | tf_op jit(solution)/shard_map/feed_forward_back/pallas_call | solution.py:534
  235.9 2.5 multiply_convert_fusion
  238.7 3.1 slice_dynamic-update-slice_fusion.1
  254.9 26.8 %feed_forward_back.3 = (bf16[512,1024]{1,0:T(8,128)(2,1)S(1)}, bf16[512,1024]{1,0:T(8,128)(2,1)}, bf16[512,1024]{1,0:T(8,128)(2,1)}, bf16[512,1024]{1,0:T(8,128)...) custom-call(s32[2]{0:T(128)S(1)} %pad_add_fusion.10.r_ref, bf16[512,2048]{1,0:T(8,128)(2,1)} %pad_maximum_fusion.12.g_ref, ...), custom_call_target="tpu_custom_call" | custom-call | flops 12884901888 | bytes 37748736 | tf_op jit(solution)/shard_map/feed_forward_back/pallas_call | solution.py:534
  285.6 3.5 fusion.64
  302.6 2.5 slice.413
  306.7 9.7 attention_back.2
  316.4 7.5 collective-permute-done.38
  326.5 3.5 fusion.62
  336.0 2.4 constant_dynamic-update-slice_fusion.7
  343.1 14.6 %attention_back.3 = (bf16[512,1024]{1,0:T(8,128)(2,1)}, bf16[512,1536]{1,0:T(8,128)(2,1)}) custom-call(bf16[512,2048]{1,0:T(8,128)(2,1)} %copy-done.45, bf16[512,1024]{1,0:T(8,128)(2,1)} %get-tuple-element.423.out_own, bf16[512,1024]{1,0:T(8,128)(2,1)} %collective-permute-done.5.out_got, f32[512,128]{1,0:T(8,128)S(1)} %copy-done.5, ...), custom_call_target="tpu_custom_call" | custom-call | flops 8000000000 | bytes 20000000 | tf_op jit(solution)/shard_map/attention_back/pallas_call | solution.py:382
  357.7 6.8 collective-permute-done.41
  371.4 4.4 fusion.95
  378.0 4.4 fusion.96
  391.1 2.4 convolution_convert_fusion.4
  395.4 14.4 %collective-permute-done.44 = bf16[512,1024]{1,0:T(8,128)(2,1)S(1)} collective-permute-done((bf16[512,1024]{1,0:T(8,128)(2,1)S(1)}, bf16[512,1024]{1,0:T(8,128)(2,1)S(1)}, u32[]{:S(2)}, u32[]{:S(2)}) %collective-permute-start.44) | collective-permute-done | bytes 1048608 | tf_op jit(solution)/shard_map/ppermute | solution.py:651
  413.2 2.5 constant_dynamic-update-slice_fusion.8
  418.7 11.7 %convolution_convert_fusion = bf16[1024,2048]{1,0:T(8,128)(2,1)S(1)} fusion(bf16[2048,1024]{1,0:T(8,128)(2,1)S(1)} %pad_maximum_fusion.1, bf16[2048,2048]{1,0:T(8,128)(2,1)} %slice_dynamic-update-slice_fusion.2), kind=kOutput, calls=%fused_computation.16 | convolution fusion | flops 8592031744 | bytes 16777216 | tf_op jit(solution)/shard_map/dot_general | solution.py:40
  430.5 12.2 %collective-permute-done.46 = bf16[512,1024]{1,0:T(8,128)(2,1)S(1)} collective-permute-done((bf16[512,1024]{1,0:T(8,128)(2,1)S(1)}, bf16[512,1024]{1,0:T(8,128)(2,1)S(1)}, u32[]{:S(2)}, u32[]{:S(2)}) %collective-permute-start.46) | collective-permute-done | bytes 1048608 | tf_op jit(solution)/shard_map/ppermute | solution.py:651
  442.7 22.1 %collective-permute-done.47 = bf16[512,1024]{1,0:T(8,128)(2,1)S(1)} collective-permute-done((bf16[512,1024]{1,0:T(8,128)(2,1)S(1)}, bf16[512,1024]{1,0:T(8,128)(2,1)S(1)}, u32[]{:S(2)}, u32[]{:S(2)}) %collective-permute-start.47) | collective-permute-done | bytes 1048608 | tf_op jit(solution)/shard_map/ppermute | solution.py:651
  467.4 2.5 collective-permute-start.51
  469.8 12.0 %convolution_convert_fusion.2 = bf16[2048,1024]{1,0:T(8,128)(2,1)S(1)} fusion(bf16[2048,2048]{1,0:T(8,128)(2,1)} %slice_dynamic-update-slice_fusion.4, bf16[2048,1024]{1,0:T(8,128)(2,1)S(1)} %pad_maximum_fusion.2), kind=kOutput, calls=%fused_computation.18 | convolution fusion | flops 8592031744 | bytes 16777216 | tf_op jit(solution)/shard_map/dot_general | solution.py:40
  481.9 2.5 fusion.76
  485.0 6.4 collective-permute-done.49
  491.4 21.2 %collective-permute-done.50 = bf16[512,1024]{1,0:T(8,128)(2,1)S(1)} collective-permute-done((bf16[512,1024]{1,0:T(8,128)(2,1)S(1)}, bf16[512,1024]{1,0:T(8,128)(2,1)S(1)}, u32[]{:S(2)}, u32[]{:S(2)}) %collective-permute-start.50) | collective-permute-done | bytes 1048608 | tf_op jit(solution)/shard_map/ppermute | solution.py:651
  515.8 53.1 %collective-permute-start.55 = (f32[1,1]{1,0:T(1,128)}, f32[1,1]{1,0:T(1,128)}, u32[]{:S(2)}, u32[]{:S(2)}) collective-permute-start(f32[1,1]{1,0:T(1,128)} %add.253), channel_id=1, source_target_pairs={{0,4},{4,0},{8,12},{12,8},{16,20},{20,16},{24,28},{28,24},{1,5},{5... | collective-permute-start | bytes 20 | tf_op jit(solution)/shard_map/ppermute | solution.py:284
  568.9 11.7 %convolution_convert_fusion.1 = bf16[2048,1024]{1,0:T(8,128)(2,1)S(1)} fusion(bf16[2048,2048]{1,0:T(8,128)(2,1)} %slice_dynamic-update-slice_fusion.4, bf16[2048,1024]{1,0:T(8,128)(2,1)S(1)} %pad_maximum_fusion.3), kind=kOutput, calls=%fused_computation.17 | convolution fusion | flops 8592031744 | bytes 16777216 | tf_op jit(solution)/shard_map/dot_general | solution.py:40
  583.1 2.9 collective-permute-start.56
  587.4 3.9 collective-permute-start.57
  594.5 10.6 convolution_convert_fusion.3
  622.4 450.4 %line_sum.1.qk_a.qk_b.v_a.v_b.o_ref.in_ref = bf16[2,8192,1024]{2,1,0:T(8,128)(2,1)} custom-call(bf16[1024,1024]{1,0:T(8,128)(2,1)} %get-tuple-element.407.refs_0_, bf16[1024,1024]{1,0:T(8,128)(2,1)} %copy-done.86, bf16[1024,1024]{1,0:T(8,128)(2,1)} %get-tuple-element.405.refs_2_, bf16[1024,1024]{1,0:T(8,128)(2,1)} %copy-done.87, ...), custom_call_target="tpu_custom_call" | custom-call | tf_op jit(solution)/shard_map/line_sum/pallas_call | solution.py:242
  1082.3 10.7 widen_four.1
  1093.0 9.6 widen.3
  1102.6 9.6 widen.4
  1112.1 9.6 widen.5
  (616 shorter events, 199.0 us)
Async XLA Ops:
  2.9 34.6 %collective-permute-start = (bf16[512,512]{1,0:T(8,128)(2,1)}, bf16[512,512]{1,0:T(8,128)(2,1)}, u32[]{:S(2)}, u32[]{:S(2)}) collective-permute-start(bf16[512,512]{1,0:T(8,128)(2,1)} %pad_maximum_fusion.35), channel_id=1, source_target_pairs={{0,1},{1,0},{2,3},{3,2},{4,5},{5,4},{6,7},{7,6},{8,9},{9,8},{10,11... | collective-permute-start | bytes 1572872 | tf_op jit(solution)/shard_map/ppermute | solution.py:655
  6.7 46.5 %collective-permute-start.2 = (bf16[512,512]{1,0:T(8,128)(2,1)}, bf16[512,512]{1,0:T(8,128)(2,1)}, u32[]{:S(2)}, u32[]{:S(2)}) collective-permute-start(bf16[512,512]{1,0:T(8,128)(2,1)} %pad_maximum_fusion.36), channel_id=1, source_target_pairs={{0,1},{1,0},{2,3},{3,2},{4,5},{5,4},{6,7},{7,6},{8,9},{9,8},{10,11... | collective-permute-start | bytes 1572872 | tf_op jit(solution)/shard_map/ppermute | solution.py:655
  13.2 50.0 %collective-permute-start.4 = (bf16[1024,1536]{1,0:T(8,128)(2,1)}, bf16[1024,1536]{1,0:T(8,128)(2,1)}, u32[]{:S(2)}, u32[]{:S(2)}) collective-permute-start(bf16[1024,1536]{1,0:T(8,128)(2,1)} %pad_maximum_fusion.5), channel_id=1, source_target_pairs={{0,2},{2,0},{1,3},{3,1},{4,6},{6,4},{5,7},{7,5},{8,10},{10,8},{9,1... | collective-permute-start | bytes 9437192 | tf_op jit(solution)/shard_map/ppermute | solution.py:648
  15.6 47.5 %collective-permute-start.5 = (bf16[512,1024]{1,0:T(8,128)(2,1)}, bf16[512,1024]{1,0:T(8,128)(2,1)}, u32[]{:S(2)}, u32[]{:S(2)}) collective-permute-start(bf16[512,1024]{1,0:T(8,128)(2,1)} %get-tuple-element.422), channel_id=1, source_target_pairs={{0,2},{2,0},{1,3},{3,1},{4,6},{6,4},{5,7},{7,5},{8,10},{10,8},{9,1... | collective-permute-start | bytes 3145736 | tf_op jit(solution)/shard_map/ppermute | solution.py:648
  16.2 26.3 %collective-permute-start.7 = (f32[1,1]{1,0:T(1,128)}, f32[1,1]{1,0:T(1,128)}, u32[]{:S(2)}, u32[]{:S(2)}) collective-permute-start(f32[1,1]{1,0:T(1,128)} %bitcast.4), channel_id=1, source_target_pairs={{0,4},{4,0},{8,12},{12,8},{16,20},{20,16},{24,28},{28,24},{1,5},{5... | collective-permute-start | bytes 20 | tf_op jit(solution)/shard_map/ppermute | solution.py:284
  39.0 16.2 %collective-permute-start.1 = (bf16[512,1024]{1,0:T(8,128)(2,1)S(1)}, bf16[512,1024]{1,0:T(8,128)(2,1)S(1)}, u32[]{:S(2)}, u32[]{:S(2)}) collective-permute-start(bf16[512,1024]{1,0:T(8,128)(2,1)S(1)} %fusion.41), channel_id=1, source_target_pairs={{0,2},{2,0},{1,3},{3,1},{4,6},{6,4},{5,7},{7,5},{8,10},{10,8},{9,1... | collective-permute-start | bytes 3145736 | tf_op jit(solution)/shard_map/ppermute | solution.py:648
  52.4 72.1 %collective-permute-start.14 = (bf16[1024,2048]{1,0:T(8,128)(2,1)}, bf16[1024,2048]{1,0:T(8,128)(2,1)}, u32[]{:S(2)}, u32[]{:S(2)}) collective-permute-start(bf16[1024,2048]{1,0:T(8,128)(2,1)} %constant_dynamic-slice_fusion.17), channel_id=1, source_target_pairs={{0,2},{2,0},{1,3},{3,1},{4,6},{6,4},{5,7},{7,5},{8,10},{10,8},{9,1... | collective-permute-start | bytes 12582920 | tf_op jit(solution)/shard_map/ppermute | solution.py:648
  53.2 71.3 %collective-permute-start.15 = (bf16[1024,2048]{1,0:T(8,128)(2,1)}, bf16[1024,2048]{1,0:T(8,128)(2,1)}, u32[]{:S(2)}, u32[]{:S(2)}) collective-permute-start(bf16[1024,2048]{1,0:T(8,128)(2,1)} %constant_dynamic-slice_fusion.16), channel_id=1, source_target_pairs={{0,2},{2,0},{1,3},{3,1},{4,6},{6,4},{5,7},{7,5},{8,10},{10,8},{9,1... | collective-permute-start | bytes 12582920 | tf_op jit(solution)/shard_map/ppermute | solution.py:648
  62.6 61.9 %collective-permute-start.16 = (bf16[2048,1024]{1,0:T(8,128)(2,1)}, bf16[2048,1024]{1,0:T(8,128)(2,1)}, u32[]{:S(2)}, u32[]{:S(2)}) collective-permute-start(bf16[2048,1024]{1,0:T(8,128)(2,1)} %constant_dynamic-slice_fusion.15), channel_id=1, source_target_pairs={{0,2},{2,0},{1,3},{3,1},{4,6},{6,4},{5,7},{7,5},{8,10},{10,8},{9,1... | collective-permute-start | bytes 12582920 | tf_op jit(solution)/shard_map/ppermute | solution.py:648
  82.3 25.5 %collective-permute-start.10 = (bf16[256,2048]{1,0:T(8,128)(2,1)}, bf16[256,2048]{1,0:T(8,128)(2,1)}, u32[]{:S(2)}, u32[]{:S(2)}) collective-permute-start(bf16[256,2048]{1,0:T(8,128)(2,1)} %get-tuple-element.185), channel_id=1, source_target_pairs={{0,1},{1,0},{2,3},{3,2},{4,5},{5,4},{6,7},{7,6},{8,9},{9,8},{10,11... | collective-permute-start | bytes 3145736 | tf_op jit(solution)/shard_map/ppermute | solution.py:661
  83.8 25.1 %collective-permute-start.11 = (bf16[256,2048]{1,0:T(8,128)(2,1)}, bf16[256,2048]{1,0:T(8,128)(2,1)S(1)}, u32[]{:S(2)}, u32[]{:S(2)}) collective-permute-start(bf16[256,2048]{1,0:T(8,128)(2,1)} %slice.471), channel_id=1, source_target_pairs={{0,4},{4,0},{8,12},{12,8},{16,20},{20,16},{24,28},{28,24},{1,5},{5... | collective-permute-start | bytes 3145736 | tf_op jit(solution)/shard_map/ppermute | solution.py:651
  124.5 27.3 %collective-permute-start.17 = (bf16[256,2048]{1,0:T(8,128)(2,1)S(1)}, bf16[256,2048]{1,0:T(8,128)(2,1)S(1)}, u32[]{:S(2)}, u32[]{:S(2)}) collective-permute-start(bf16[256,2048]{1,0:T(8,128)(2,1)S(1)} %get-tuple-element.201), channel_id=1, source_target_pairs={{0,1},{1,0},{2,3},{3,2},{4,5},{5,4},{6,7},{7,6},{8,9},{9,8},{10,11... | collective-permute-start | bytes 3145736 | tf_op jit(solution)/shard_map/ppermute | solution.py:661
  125.5 26.3 %collective-permute-start.18 = (bf16[256,2048]{1,0:T(8,128)(2,1)}, bf16[256,2048]{1,0:T(8,128)(2,1)S(1)}, u32[]{:S(2)}, u32[]{:S(2)}) collective-permute-start(bf16[256,2048]{1,0:T(8,128)(2,1)} %slice.475), channel_id=1, source_target_pairs={{0,4},{4,0},{8,12},{12,8},{16,20},{20,16},{24,28},{28,24},{1,5},{5... | collective-permute-start | bytes 3145736 | tf_op jit(solution)/shard_map/ppermute | solution.py:651
  158.1 80.5 %collective-permute-start.62 = (bf16[512,2048]{1,0:T(8,128)(2,1)}, bf16[512,2048]{1,0:T(8,128)(2,1)}, u32[]{:S(2)}, u32[]{:S(2)}) collective-permute-start(bf16[512,2048]{1,0:T(8,128)(2,1)} %pad_maximum_fusion.16), channel_id=1, source_target_pairs={{0,2},{2,0},{1,3},{3,1},{4,6},{6,4},{5,7},{7,5},{8,10},{10,8},{9,1... | collective-permute-start | bytes 6291464 | tf_op jit(solution)/shard_map/ppermute | solution.py:648
  163.3 28.0 %collective-permute-start.22 = (bf16[256,2048]{1,0:T(8,128)(2,1)}, bf16[256,2048]{1,0:T(8,128)(2,1)S(1)}, u32[]{:S(2)}, u32[]{:S(2)}) collective-permute-start(bf16[256,2048]{1,0:T(8,128)(2,1)} %get-tuple-element.214), channel_id=1, source_target_pairs={{0,1},{1,0},{2,3},{3,2},{4,5},{5,4},{6,7},{7,6},{8,9},{9,8},{10,11... | collective-permute-start | bytes 3145736 | tf_op jit(solution)/shard_map/ppermute | solution.py:661
  164.5 26.8 %collective-permute-start.23 = (bf16[256,2048]{1,0:T(8,128)(2,1)}, bf16[256,2048]{1,0:T(8,128)(2,1)S(1)}, u32[]{:S(2)}, u32[]{:S(2)}) collective-permute-start(bf16[256,2048]{1,0:T(8,128)(2,1)} %slice.388), channel_id=1, source_target_pairs={{0,4},{4,0},{8,12},{12,8},{16,20},{20,16},{24,28},{28,24},{1,5},{5... | collective-permute-start | bytes 3145736 | tf_op jit(solution)/shard_map/ppermute | solution.py:651
  199.8 407.8 %collective-permute-start.24 = (bf16[256,512]{1,0:T(8,128)(2,1)}, bf16[256,512]{1,0:T(8,128)(2,1)}, u32[]{:S(2)}, u32[]{:S(2)}) collective-permute-start(bf16[256,512]{1,0:T(8,128)(2,1)} %get-tuple-element.452), channel_id=1, source_target_pairs={{0,2},{2,0},{1,3},{3,1},{4,6},{6,4},{5,7},{7,5},{8,10},{10,8},{9,1... | collective-permute-start | bytes 786440 | tf_op jit(solution)/shard_map/ppermute | solution.py:648
  207.1 27.8 %collective-permute-start.28 = (bf16[256,2048]{1,0:T(8,128)(2,1)}, bf16[256,2048]{1,0:T(8,128)(2,1)S(1)}, u32[]{:S(2)}, u32[]{:S(2)}) collective-permute-start(bf16[256,2048]{1,0:T(8,128)(2,1)} %get-tuple-element.230), channel_id=1, source_target_pairs={{0,1},{1,0},{2,3},{3,2},{4,5},{5,4},{6,7},{7,6},{8,9},{9,8},{10,11... | collective-permute-start | bytes 3145736 | tf_op jit(solution)/shard_map/ppermute | solution.py:661
  208.0 27.0 %collective-permute-start.29 = (bf16[256,2048]{1,0:T(8,128)(2,1)S(1)}, bf16[256,2048]{1,0:T(8,128)(2,1)S(1)}, u32[]{:S(2)}, u32[]{:S(2)}) collective-permute-start(bf16[256,2048]{1,0:T(8,128)(2,1)S(1)} %copy-done.106), channel_id=1, source_target_pairs={{0,4},{4,0},{8,12},{12,8},{16,20},{20,16},{24,28},{28,24},{1,5},{5... | collective-permute-start | bytes 3145736 | tf_op jit(solution)/shard_map/ppermute | solution.py:651
  238.6 9.2 collective-permute-start.32
  252.2 29.4 %collective-permute-start.34 = (bf16[256,2048]{1,0:T(8,128)(2,1)}, bf16[256,2048]{1,0:T(8,128)(2,1)S(1)}, u32[]{:S(2)}, u32[]{:S(2)}) collective-permute-start(bf16[256,2048]{1,0:T(8,128)(2,1)} %get-tuple-element.248), channel_id=1, source_target_pairs={{0,1},{1,0},{2,3},{3,2},{4,5},{5,4},{6,7},{7,6},{8,9},{9,8},{10,11... | collective-permute-start | bytes 3145736 | tf_op jit(solution)/shard_map/ppermute | solution.py:661
  253.4 28.3 %collective-permute-start.35 = (bf16[512,1024]{1,0:T(8,128)(2,1)}, bf16[512,1024]{1,0:T(8,128)(2,1)S(1)}, u32[]{:S(2)}, u32[]{:S(2)}) collective-permute-start(bf16[512,1024]{1,0:T(8,128)(2,1)} %get-tuple-element.249), channel_id=1, source_target_pairs={{0,4},{4,0},{8,12},{12,8},{16,20},{20,16},{24,28},{28,24},{1,5},{5... | collective-permute-start | bytes 3145736 | tf_op jit(solution)/shard_map/ppermute | solution.py:651
  292.9 37.3 %collective-permute-start.31 = (bf16[512,2048]{1,0:T(8,128)(2,1)}, bf16[512,2048]{1,0:T(8,128)(2,1)}, u32[]{:S(2)}, u32[]{:S(2)}) collective-permute-start(bf16[512,2048]{1,0:T(8,128)(2,1)} %pad_maximum_fusion.11), channel_id=1, source_target_pairs={{0,2},{2,0},{1,3},{3,1},{4,6},{6,4},{5,7},{7,5},{8,10},{10,8},{9,1... | collective-permute-start | bytes 6291464 | tf_op jit(solution)/shard_map/ppermute | solution.py:648
  298.5 25.4 %collective-permute-start.38 = (bf16[256,2048]{1,0:T(8,128)(2,1)}, bf16[256,2048]{1,0:T(8,128)(2,1)}, u32[]{:S(2)}, u32[]{:S(2)}) collective-permute-start(bf16[256,2048]{1,0:T(8,128)(2,1)} %get-tuple-element.269), channel_id=1, source_target_pairs={{0,1},{1,0},{2,3},{3,2},{4,5},{5,4},{6,7},{7,6},{8,9},{9,8},{10,11... | collective-permute-start | bytes 3145736 | tf_op jit(solution)/shard_map/ppermute | solution.py:661
  299.3 25.1 %collective-permute-start.39 = (bf16[256,2048]{1,0:T(8,128)(2,1)}, bf16[256,2048]{1,0:T(8,128)(2,1)}, u32[]{:S(2)}, u32[]{:S(2)}) collective-permute-start(bf16[256,2048]{1,0:T(8,128)(2,1)} %slice.410), channel_id=1, source_target_pairs={{0,4},{4,0},{8,12},{12,8},{16,20},{20,16},{24,28},{28,24},{1,5},{5... | collective-permute-start | bytes 3145736 | tf_op jit(solution)/shard_map/ppermute | solution.py:651
  338.6 25.8 %collective-permute-start.41 = (bf16[256,2048]{1,0:T(8,128)(2,1)}, bf16[256,2048]{1,0:T(8,128)(2,1)}, u32[]{:S(2)}, u32[]{:S(2)}) collective-permute-start(bf16[256,2048]{1,0:T(8,128)(2,1)} %slice.413), channel_id=1, source_target_pairs={{0,4},{4,0},{8,12},{12,8},{16,20},{20,16},{24,28},{28,24},{1,5},{5... | collective-permute-start | bytes 3145736 | tf_op jit(solution)/shard_map/ppermute | solution.py:651
  384.0 9.6 collective-permute-start.42
  384.1 9.8 collective-permute-start.43
  385.1 24.7 %collective-permute-start.44 = (bf16[512,1024]{1,0:T(8,128)(2,1)S(1)}, bf16[512,1024]{1,0:T(8,128)(2,1)S(1)}, u32[]{:S(2)}, u32[]{:S(2)}) collective-permute-start(bf16[512,1024]{1,0:T(8,128)(2,1)S(1)} %copy-done.135), channel_id=1, source_target_pairs={{0,4},{4,0},{8,12},{12,8},{16,20},{20,16},{24,28},{28,24},{1,5},{5... | collective-permute-start | bytes 3145736 | tf_op jit(solution)/shard_map/ppermute | solution.py:651
  387.4 24.7 %collective-permute-start.45 = (bf16[512,2048]{1,0:T(8,128)(2,1)S(1)}, bf16[512,2048]{1,0:T(8,128)(2,1)S(1)}, u32[]{:S(2)}, u32[]{:S(2)}) collective-permute-start(bf16[512,2048]{1,0:T(8,128)(2,1)S(1)} %pad_maximum_fusion.15), channel_id=1, source_target_pairs={{0,2},{2,0},{1,3},{3,1},{4,6},{6,4},{5,7},{7,5},{8,10},{10,8},{9,1... | collective-permute-start | bytes 6291464 | tf_op jit(solution)/shard_map/ppermute | solution.py:648
  416.7 26.0 %collective-permute-start.46 = (bf16[512,1024]{1,0:T(8,128)(2,1)S(1)}, bf16[512,1024]{1,0:T(8,128)(2,1)S(1)}, u32[]{:S(2)}, u32[]{:S(2)}) collective-permute-start(bf16[512,1024]{1,0:T(8,128)(2,1)S(1)} %copy-done.137), channel_id=1, source_target_pairs={{0,4},{4,0},{8,12},{12,8},{16,20},{20,16},{24,28},{28,24},{1,5},{5... | collective-permute-start | bytes 3145736 | tf_op jit(solution)/shard_map/ppermute | solution.py:651
  417.3 47.5 %collective-permute-start.47 = (bf16[512,1024]{1,0:T(8,128)(2,1)S(1)}, bf16[512,1024]{1,0:T(8,128)(2,1)S(1)}, u32[]{:S(2)}, u32[]{:S(2)}) collective-permute-start(bf16[512,1024]{1,0:T(8,128)(2,1)S(1)} %copy-done.139), channel_id=1, source_target_pairs={{0,4},{4,0},{8,12},{12,8},{16,20},{20,16},{24,28},{28,24},{1,5},{5... | collective-permute-start | bytes 3145736 | tf_op jit(solution)/shard_map/ppermute | solution.py:651
  465.3 26.1 %collective-permute-start.49 = (bf16[512,1024]{1,0:T(8,128)(2,1)S(1)}, bf16[512,1024]{1,0:T(8,128)(2,1)S(1)}, u32[]{:S(2)}, u32[]{:S(2)}) collective-permute-start(bf16[512,1024]{1,0:T(8,128)(2,1)S(1)} %copy-done.136), channel_id=1, source_target_pairs={{0,4},{4,0},{8,12},{12,8},{16,20},{20,16},{24,28},{28,24},{1,5},{5... | collective-permute-start | bytes 3145736 | tf_op jit(solution)/shard_map/ppermute | solution.py:651
  465.9 46.7 %collective-permute-start.50 = (bf16[512,1024]{1,0:T(8,128)(2,1)S(1)}, bf16[512,1024]{1,0:T(8,128)(2,1)S(1)}, u32[]{:S(2)}, u32[]{:S(2)}) collective-permute-start(bf16[512,1024]{1,0:T(8,128)(2,1)S(1)} %copy-done.138), channel_id=1, source_target_pairs={{0,4},{4,0},{8,12},{12,8},{16,20},{20,16},{24,28},{28,24},{1,5},{5... | collective-permute-start | bytes 3145736 | tf_op jit(solution)/shard_map/ppermute | solution.py:651
  467.4 17.0 %collective-permute-start.51 = (f32[1,1]{1,0:T(1,128)}, f32[1,1]{1,0:T(1,128)}, u32[]{:S(2)}, u32[]{:S(2)}) collective-permute-start(f32[1,1]{1,0:T(1,128)} %add.252), channel_id=1, source_target_pairs={{0,1},{1,0},{2,3},{3,2},{4,5},{5,4},{6,7},{7,6},{8,9},{9,8},{10,11... | collective-permute-start | bytes 20 | tf_op jit(solution)/shard_map/ppermute | solution.py:284
  513.1 81.3 %collective-permute-start.52 = (bf16[256,2048]{1,0:T(8,128)(2,1)S(1)}, bf16[256,2048]{1,0:T(8,128)(2,1)}, u32[]{:S(2)}, u32[]{:S(2)}) collective-permute-start(bf16[256,2048]{1,0:T(8,128)(2,1)S(1)} %constant_dynamic-slice_fusion.8), channel_id=1, source_target_pairs={{0,4},{4,0},{8,12},{12,8},{16,20},{20,16},{24,28},{28,24},{1,5},{5... | collective-permute-start | bytes 3145736 | tf_op jit(solution)/shard_map/ppermute | solution.py:651
  513.8 78.9 %collective-permute-start.53 = (bf16[512,768]{1,0:T(8,128)(2,1)S(1)}, bf16[512,768]{1,0:T(8,128)(2,1)S(1)}, u32[]{:S(2)}, u32[]{:S(2)}) collective-permute-start(bf16[512,768]{1,0:T(8,128)(2,1)S(1)} %copy-done.117), channel_id=1, source_target_pairs={{0,4},{4,0},{8,12},{12,8},{16,20},{20,16},{24,28},{28,24},{1,5},{5... | collective-permute-start | bytes 2359304 | tf_op jit(solution)/shard_map/ppermute | solution.py:651
  515.2 78.1 %collective-permute-start.54 = (bf16[512,768]{1,0:T(8,128)(2,1)S(1)}, bf16[512,768]{1,0:T(8,128)(2,1)S(1)}, u32[]{:S(2)}, u32[]{:S(2)}) collective-permute-start(bf16[512,768]{1,0:T(8,128)(2,1)S(1)} %pad_maximum_fusion.34), channel_id=1, source_target_pairs={{0,4},{4,0},{8,12},{12,8},{16,20},{20,16},{24,28},{28,24},{1,5},{5... | collective-permute-start | bytes 2359304 | tf_op jit(solution)/shard_map/ppermute | solution.py:651
  515.8 66.7 %collective-permute-start.55 = (f32[1,1]{1,0:T(1,128)}, f32[1,1]{1,0:T(1,128)}, u32[]{:S(2)}, u32[]{:S(2)}) collective-permute-start(f32[1,1]{1,0:T(1,128)} %add.253), channel_id=1, source_target_pairs={{0,4},{4,0},{8,12},{12,8},{16,20},{20,16},{24,28},{28,24},{1,5},{5... | collective-permute-start | bytes 20 | tf_op jit(solution)/shard_map/ppermute | solution.py:284
  592.0 17.5 %collective-permute-start.30 = (bf16[256,512]{1,0:T(8,128)(2,1)S(1)}, bf16[256,512]{1,0:T(8,128)(2,1)S(1)}, u32[]{:S(2)}, u32[]{:S(2)}) collective-permute-start(bf16[256,512]{1,0:T(8,128)(2,1)S(1)} %copy-done.126), channel_id=1, source_target_pairs={{0,2},{2,0},{1,3},{3,1},{4,6},{6,4},{5,7},{7,5},{8,10},{10,8},{9,1... | collective-permute-start | bytes 786440 | tf_op jit(solution)/shard_map/ppermute | solution.py:648
  592.7 21.2 %collective-permute-start.58 = (bf16[1024,1024]{1,0:T(8,128)(2,1)}, bf16[1024,1024]{1,0:T(8,128)(2,1)S(1)}, u32[]{:S(2)}, u32[]{:S(2)}) collective-permute-start(bf16[1024,1024]{1,0:T(8,128)(2,1)} %get-tuple-element.406), channel_id=1, source_target_pairs={{0,2},{2,0},{1,3},{3,1},{4,6},{6,4},{5,7},{7,5},{8,10},{10,8},{9,1... | collective-permute-start | bytes 6291464 | tf_op jit(solution)/shard_map/ppermute | solution.py:648
  593.6 26.7 %collective-permute-start.59 = (bf16[1024,1024]{1,0:T(8,128)(2,1)S(1)}, bf16[1024,1024]{1,0:T(8,128)(2,1)S(1)}, u32[]{:S(2)}, u32[]{:S(2)}) collective-permute-start(bf16[1024,1024]{1,0:T(8,128)(2,1)S(1)} %get-tuple-element.404), channel_id=1, source_target_pairs={{0,2},{2,0},{1,3},{3,1},{4,6},{6,4},{5,7},{7,5},{8,10},{10,8},{9,1... | collective-permute-start | bytes 6291464 | tf_op jit(solution)/shard_map/ppermute | solution.py:648
  605.2 12.0 %collective-permute-start.63 = (bf16[1024,768]{1,0:T(8,128)(2,1)S(1)}, bf16[1024,768]{1,0:T(8,128)(2,1)S(1)}, u32[]{:S(2)}, u32[]{:S(2)}) collective-permute-start(bf16[1024,768]{1,0:T(8,128)(2,1)S(1)} %slice.513), channel_id=1, source_target_pairs={{0,2},{2,0},{1,3},{3,1},{4,6},{6,4},{5,7},{7,5},{8,10},{10,8},{9,1... | collective-permute-start | bytes 4718600 | tf_op jit(solution)/shard_map/ppermute | solution.py:648
  607.6 12.7 %collective-permute-start.60 = (bf16[1024,1024]{1,0:T(8,128)(2,1)S(1)}, bf16[1024,1024]{1,0:T(8,128)(2,1)S(1)}, u32[]{:S(2)}, u32[]{:S(2)}) collective-permute-start(bf16[1024,1024]{1,0:T(8,128)(2,1)S(1)} %get-tuple-element.402), channel_id=1, source_target_pairs={{0,2},{2,0},{1,3},{3,1},{4,6},{6,4},{5,7},{7,5},{8,10},{10,8},{9,1... | collective-permute-start | bytes 6291464 | tf_op jit(solution)/shard_map/ppermute | solution.py:648
  611.6 461.3 %collective-permute-start.64 = (bf16[256,2048]{1,0:T(8,128)(2,1)}, bf16[256,2048]{1,0:T(8,128)(2,1)S(1)}, u32[]{:S(2)}, u32[]{:S(2)}) collective-permute-start(bf16[256,2048]{1,0:T(8,128)(2,1)} %convert_element_type.239), channel_id=1, source_target_pairs={{0,1},{1,0},{2,3},{3,2},{4,5},{5,4},{6,7},{7,6},{8,9},{9,8},{10,11... | collective-permute-start | bytes 3145736 | tf_op jit(solution)/shard_map/ppermute | solution.py:661
  613.9 459.0 %collective-permute-start.65 = (bf16[256,2048]{1,0:T(8,128)(2,1)}, bf16[256,2048]{1,0:T(8,128)(2,1)}, u32[]{:S(2)}, u32[]{:S(2)}) collective-permute-start(bf16[256,2048]{1,0:T(8,128)(2,1)} %convert_element_type.240), channel_id=1, source_target_pairs={{0,1},{1,0},{2,3},{3,2},{4,5},{5,4},{6,7},{7,6},{8,9},{9,8},{10,11... | collective-permute-start | bytes 3145736 | tf_op jit(solution)/shard_map/ppermute | solution.py:661
  1077.2 44.5 %collective-permute-start.67 = (f32[256,512]{1,0:T(8,128)S(1)}, f32[256,512]{1,0:T(8,128)S(1)}, u32[]{:S(2)}, u32[]{:S(2)}) collective-permute-start(f32[256,512]{1,0:T(8,128)S(1)} %constant_dynamic-slice_fusion), channel_id=1, source_target_pairs={{0,2},{2,0},{1,3},{3,1},{4,6},{6,4},{5,7},{7,5},{8,10},{10,8},{9,1... | collective-permute-start | bytes 1572872 | tf_op jit(solution)/shard_map/ppermute | solution.py:648
  1080.4 41.5 %collective-permute-start.66 = (f32[256,512]{1,0:T(8,128)S(1)}, f32[256,512]{1,0:T(8,128)S(1)}, u32[]{:S(2)}, u32[]{:S(2)}) collective-permute-start(f32[256,512]{1,0:T(8,128)S(1)} %constant_dynamic-slice_fusion.1), channel_id=1, source_target_pairs={{0,2},{2,0},{1,3},{3,1},{4,6},{6,4},{5,7},{7,5},{8,10},{10,8},{9,1... | collective-permute-start | bytes 1572872 | tf_op jit(solution)/shard_map/ppermute | solution.py:648
  (171 other events, 3346.0 us)

commit v3 on v2

--- a/solution.py
+++ b/solution.py
@@ -72,11 +72,11 @@
 MESH = pl.DeviceIdType.MESH
 
 
-def line_kernel(sizes, spots, chunk, lag, ahead, deep, *refs):
+def line_kernel(sizes, spots, given, chunk, lag, ahead, deep, *refs):
     count = len(sizes)
-    pieces = refs[:count]
-    out = refs[count]
-    held, got_in, got_mid, load, send_in, send_mid, send_out, send_side, in_sem, mid_sem, out_sem, side_sem, keep = refs[count + 1:]
+    pieces, gives = refs[:count], refs[count : count + given]
+    out = refs[count + given]
+    held, got_in, got_mid, got_give, load, send_in, send_mid, send_out, send_side, in_sem, mid_sem, out_sem, side_sem, keep, send_give, give_sem = refs[count + given + 1:]
     places = lax.axis_size("dp") // 2
     dp = lax.axis_index("dp")
     row = lax.axis_index("row")
@@ -94,6 +94,8 @@
     other = (dp + 1 - 2 * side, row, col)
     total_rows = held.shape[0]
     steps = total_rows // chunk
+    base = total_rows - sum(sizes[count - given :])
+    first = base // chunk
 
     loads = []
     for i in range(count):
@@ -115,8 +117,29 @@
     def _():
         pl.semaphore_wait(barrier, 2)
 
+    given_copies = []
+    for i in range(given):
+        spot = pl.multiple_of(spots[count - given + i](row) - base, 16)
+        given_copies.append(
+            pltpu.make_async_remote_copy(
+                src_ref=gives[i], dst_ref=got_give.at[pl.ds(spot, sizes[count - given + i])],
+                send_sem=send_give.at[i], recv_sem=give_sem.at[i],
+                device_id=other, device_id_type=MESH))
+        given_copies[-1].start()
     for copy in loads:
         copy.wait()
+
+    def add_given(t):
+        @pl.when(t == first)
+        def _():
+            for copy in given_copies:
+                copy.wait()
+
+        @pl.when(t >= first)
+        def _():
+            held[at(t)] = (
+                held[at(t)].astype(F32) + got_give[at(t - first)].astype(F32)
+            ).astype(BF)
 
     def at(t):
         return pl.ds(pl.multiple_of(t * chunk, chunk), chunk)
@@ -147,6 +170,8 @@
     def mid_loop(t, _):
         @pl.when(t < steps)
         def _():
+            add_given(t)
+
             @pl.when(jnp.logical_not(is_end))
             def _():
                 inward(t).wait_recv()
@@ -177,6 +202,8 @@
     def far_loop(t, _):
         @pl.when(t < steps)
         def _():
+            add_given(t)
+
             @pl.when(jnp.logical_not(is_end))
             def _():
                 inward(t).wait_recv()
@@ -234,20 +261,27 @@
         lax.fori_loop(0, steps, finish, 0)
 
 
-def line_sum(pieces, spots, chunk, lag=8, ahead=2, deep=2):
+def line_sum(pieces, spots, gives, chunk, lag=8, ahead=2, deep=2):
     sizes = [p.shape[0] for p in pieces]
     rows, width = sum(sizes), pieces[0].shape[1]
     steps = rows // chunk
+    given_rows = sum(g.shape[0] for g in gives)
     dma = pltpu.SemaphoreType.DMA
     return pl.pallas_call(
-        functools.partial(line_kernel, sizes, spots, chunk, lag, ahead, deep),
+        functools.partial(line_kernel, sizes, spots, len(gives), chunk, lag, ahead, deep),
         out_shape=jax.ShapeDtypeStruct((2, rows, width), BF),
-        in_specs=[pl.BlockSpec(memory_space=pl.ANY)] * len(pieces),
+        in_specs=[pl.BlockSpec(memory_space=pl.ANY)] * (len(pieces) + len(gives)),
         out_specs=pl.BlockSpec(memory_space=pl.ANY),
-        scratch_shapes=[pltpu.VMEM((rows, width), BF)] * 3 + [dma((len(pieces),))] + [dma((steps,))] * 9,
-        compiler_params=pltpu.CompilerParams(collective_id=0, has_side_effects=True, vmem_limit_bytes=56 * 2**20),
+        scratch_shapes=[pltpu.VMEM((rows, width), BF)] * 3
+        + [pltpu.VMEM((given_rows, width), BF)]
+        + [dma((len(pieces),))]
+        + [dma((steps,))] * 9
+        + [dma((len(gives),))] * 2,
+        compiler_params=pltpu.CompilerParams(
+            collective_id=0, has_side_effects=True, vmem_limit_bytes=58 * 2**20
+        ),
         name="line_sum",
-    )(*pieces)
+    )(*pieces, *gives)
 
 
 def pack(operand, width):
@@ -277,13 +311,9 @@
     )
 
 
-def butterfly(operand, axis):
+def hop(operand, axis, step):
     size = lax.axis_size(axis)
-    step = 1
-    while step < size:
-        operand = operand + lax.ppermute(operand, axis, [(i, i ^ step) for i in range(size)])
-        step *= 2
-    return operand
+    return operand + lax.ppermute(operand, axis, [(i, i ^ step) for i in range(size)])
 
 
 def turned(operand, cosine, sine_table):
@@ -376,6 +406,17 @@
             back_out[:, at] = grad_v[span:].astype(BF)
             at = slice(wide + h * HEAD, wide + (h + 1) * HEAD)
             first_out[:, at] = (grad_v[:span] + v_part[:, head]).astype(BF)
+
+
+def last_kernel(a_ref, b_ref, own_ref, got_ref, kept_a, sent_a, kept_b, sent_b):
+    half = own_ref.shape[0]
+    own = kept_a.shape[0]
+    for ref, kept, sent in ((a_ref, kept_a, sent_a), (b_ref, kept_b, sent_b)):
+        near, far = contract_cols(ref[...], own_ref[...]), contract_cols(ref[...], got_ref[...])
+        kept[:, :half] = near[:own]
+        kept[:, half:] = far[:own]
+        sent[:, :half] = far[own:].astype(BF)
+        sent[:, half:] = near[own:].astype(BF)
 
 
 def in_vmem(kernel, name, out_shape, operands):
@@ -551,23 +592,27 @@
     )(where, operand, *saved, gate, gate_got, up, up_got, down, down_got)
 
 
-def widen(sums, shape, block, spot):
-    rows, columns = block
-
-    def kernel(in_ref, out_ref):
-        out_ref[...] = in_ref[0].astype(F32)
+def widen_three(sums, down_shape, into_shape, size):
+    def kernel(in_ref, *outs):
+        for n, out in enumerate(outs):
+
+            @pl.when(pl.program_id(0) // 4 == n)
+            def _():
+                out[...] = in_ref[0].astype(F32)
+
+    def spot(n):
+        if n == 0:
+            return lambda t: (jnp.clip(t, 0, 3), 0)
+        return lambda t: (0, jnp.clip(t - 4 * n, 0, 3))
 
     return pl.pallas_call(
         kernel,
-        out_shape=jax.ShapeDtypeStruct(shape, F32),
-        grid=(shape[1] // columns, shape[0] // rows),
-        in_specs=[pl.BlockSpec((1, rows, columns), spot)],
-        out_specs=pl.BlockSpec((rows, columns), lambda j, i: (i, j)),
-        compiler_params=pltpu.CompilerParams(vmem_limit_bytes=32 * 2**20),
-        cost_estimate=pl.CostEstimate(
-            flops=0, bytes_accessed=6 * shape[0] * shape[1], transcendentals=0
-        ),
-        name="widen",
+        out_shape=[jax.ShapeDtypeStruct(x, F32) for x in (down_shape, into_shape, into_shape)],
+        grid=(12,),
+        in_specs=[pl.BlockSpec((1, size, size), lambda t: (t % 2, t // 2, 0))],
+        out_specs=[pl.BlockSpec((size, size), spot(n)) for n in range(3)],
+        compiler_params=pltpu.CompilerParams(vmem_limit_bytes=48 * 2**20),
+        name="widen_three",
     )(sums)
 
 
@@ -696,8 +741,10 @@
     weights = (gate_weight, up_weight, down_weight)
 
     validity = valid_mask.astype(F32)
-    token_total = butterfly(jnp.sum(validity).reshape(1, 1), "dp")
-    scale = (rows * lax.axis_size("dp")) / token_total
+    token_total = jnp.sum(validity).reshape(1, 1)
+    hops = [(axis, 1 << k) for axis in ("dp", "row", "col") for k in range(10)]
+    hops = [(axis, step) for axis, step in hops if step < lax.axis_size(axis)]
+    token_hops = [h for h in hops if h[0] == "dp"]
     segs = local_order(segments)
     places = local_order(jnp.arange(rows, dtype=jnp.int32))
     valids = [v[:own, None] for v in local_order(validity)]
@@ -833,66 +880,80 @@
 
     part_a = joined(attention(0, first_norm(0, blocks[0])))
     operand = first_norm(1, blocks[1])
-    operand, part_a, low, mine, scale = tie(
-        (operand, part_a, part_a.astype(BF), low_first[0][:own], scale)
-    )
-    got_a, first_a = from_chips(low), cross(mine)
+    operand, part_a, low, token_total, core = tie(
+        (operand, part_a, part_a.astype(BF), token_total, 1 - row)
+    )
+    got_a = from_chips(low)
+    token_total = hop(token_total, *token_hops[0])
     pair = attention(1, operand)
-    pair, got_a, first_a = tie((pair, got_a, first_a))
     received = (
-        swap(take(gate_weight, 1 - row, units, 1)),
-        swap(take(up_weight, 1 - row, units, 1)),
-        swap(take(down_weight, 1 - row, units, 0)),
-    )
+        swap(take(gate_weight, core, units, 1)),
+        swap(take(up_weight, core, units, 1)),
+        swap(take(down_weight, core, units, 0)),
+    )
+    pair, got_a, token_total, received = tie((pair, got_a, token_total, received))
     part_b = joined(pair)
     two_a = second_norm(0, part_a, got_a)
-    two_a, part_b, low, mine, received = tie(
-        (two_a, part_b, part_b.astype(BF), low_first[1][:own], received)
-    )
-    got_b, first_b = from_chips(low), cross(mine)
+    two_a, part_b, low, mine, token_total = tie(
+        (two_a, part_b, part_b.astype(BF), two_a[:own], token_total)
+    )
+    token_total = hop(token_total, *token_hops[1])
+    got_b, cross_two_a = from_chips(low), cross(mine)
     raw = forward(two_a, received)
-    raw, got_b, first_b = tie((raw, got_b, first_b))
+    raw, got_b, cross_two_a, token_total = tie((raw, got_b, cross_two_a, token_total))
     part_a, targets_a = after_forward(0, raw)
     two_b = second_norm(1, part_b, got_b)
-    two_b, part_a, low, mine = tie((two_b, part_a, part_a.astype(BF), two_a[:own]))
-    got_a, cross_two_a = from_chips(low), cross(mine)
+    two_b, part_a, low, mine, token_total = tie(
+        (two_b, part_a, part_a.astype(BF), two_b[:own], token_total)
+    )
+    for step in token_hops[2:]:
+        token_total = hop(token_total, *step)
+    got_a, cross_two_b = from_chips(low), cross(mine)
     raw = forward(two_b, received)
-    raw, got_a, cross_two_a = tie((raw, got_a, cross_two_a))
+    raw, got_a, cross_two_b, token_total = tie((raw, got_a, cross_two_b, token_total))
+    scale = (rows * lax.axis_size("dp")) / token_total
     part_b, targets_b = after_forward(1, raw)
     low_a = loss_of(0, part_a, got_a, targets_a)
-    low_a, part_b, low, mine = tie((low_a, part_b, part_b.astype(BF), two_b[:own]))
-    got_b, cross_two_b = from_chips(low), cross(mine)
+    low_a, part_b, low, mine = tie((low_a, part_b, part_b.astype(BF), act_gives[0]))
+    got_b, cross_act_a = from_chips(low), cross(mine)
     raw = backward(0, low_a, received)
-    raw, got_b, cross_two_b = tie((raw, got_b, cross_two_b))
+    raw, got_b, cross_act_a = tie((raw, got_b, cross_act_a))
     ups_a, part_a = raw[:4], joined(raw[4:])
     low_b = loss_of(1, part_b, got_b, targets_b)
-    low_b, part_a, low, mine = tie((low_b, part_a, part_a.astype(BF), act_gives[0]))
-    got_a, cross_act_a = from_chips(low), cross(mine)
+    low_b, part_a, low, mine, error_sum = tie(
+        (
+            low_b,
+            part_a,
+            part_a.astype(BF),
+            act_gives[1],
+            (errors[0] + errors[1]).reshape(1, 1),
+        )
+    )
+    error_sum = hop(error_sum, *hops[0])
+    got_a, cross_act_b = from_chips(low), cross(mine)
     raw = backward(1, low_b, received)
-    raw, got_a, cross_act_a = tie((raw, got_a, cross_act_a))
+    raw, got_a, cross_act_b, error_sum = tie((raw, got_a, cross_act_b, error_sum))
     ups_b, part_b = raw[:4], joined(raw[4:])
     hidden_a = second_norm_back(0, part_a, got_a)
     hidden_a, part_b, low, mine = tie((hidden_a, part_b, part_b.astype(BF), low_a[:own]))
+    error_sum = hop(error_sum, *hops[1])
     got_b, cross_low_a = from_chips(low), cross(mine)
     parts = attention_back(0, hidden_a, [])
-    parts, got_b, cross_low_a = tie((parts, got_b, cross_low_a))
+    parts, got_b, cross_low_a, error_sum = tie((parts, got_b, cross_low_a, error_sum))
     hidden_b = second_norm_back(1, part_b, got_b)
-    hidden_b, parts, mine = tie((hidden_b, parts, low_b[:own]))
+    hidden_b, parts, mine, error_sum = tie((hidden_b, parts, low_b[:own], error_sum))
+    error_sum = hop(error_sum, *hops[2])
     cross_low_b = cross(mine)
     first_back, back_b = attention_back(
         1, hidden_b, [key_heads[0], value_heads[0], *tables[0], *parts[1:]]
     )
-    first_back, back_b, cross_low_b = tie((first_back, back_b, cross_low_b))
+    first_back, back_b, cross_low_b, error_sum = tie(
+        (first_back, back_b, cross_low_b, error_sum)
+    )
     backs = [jnp.concatenate([parts[0], first_back], axis=1), back_b]
     gate_gives = [u[1] for u in (ups_a, ups_b)]
     up_gives = [u[3] for u in (ups_a, ups_b)]
 
-    def half_columns(operand, which):
-        return jnp.concatenate(
-            [take(operand[:, i * wide : (i + 1) * wide], which, part_wide, 1) for i in range(3)],
-            axis=1,
-        )
-
     def split_rows(full):
         half = full.shape[0] // 2
         return full[:half], swap(full[half:])
@@ -907,67 +968,56 @@
     def product(lefts, rights):
         return contract_rows(lefts, rights).astype(BF)
 
-    back_gives = [half_columns(g, 1 - side) for g in backs]
     hiddens = together(attended, [hidden_a, hidden_b])
-    error_sum = (errors[0] + errors[1]).reshape(1, 1)
-    hiddens, act_give, backs, back_gives = tie((hiddens, act_gives[1], backs, back_gives))
-    cross_act_b = cross(act_give)
-    last_parts = [
-        sum_cores(contract_cols(g, qkv_own), contract_cols(g, qkv_got)) for g in backs
-    ]
-    grad_out = product(*hiddens)
-    last_parts, grad_out, cross_act_b, error_sum = tie(
-        (last_parts, grad_out, cross_act_b, error_sum)
-    )
+    firsts = together(low_first, backs)
+    backs, mine, gate_gives = tie((backs, gate_gives[0], gate_gives))
+    cross_gate_a = cross(mine)
+    for step in hops[3:]:
+        error_sum = hop(error_sum, *step)
+    ends = [jax.ShapeDtypeStruct((own, 2 * half_width), t) for t in (F32, BF)]
+    raw = in_vmem(last_kernel, "first_norm_back", ends * 2, [*backs, qkv_own, qkv_got])
+    raw, cross_gate_a, error_sum = tie((raw, cross_gate_a, error_sum))
+    last_parts = [joined(raw[:2]), joined(raw[2:])]
     downs = together(
         [*acts, cross_act_a, cross_act_b], [low_a, low_b, *from_cores(cross_low_a, cross_low_b)]
     )
-    downs, gate_gives = tie((downs, gate_gives))
-    cross_gates = [cross(g) for g in gate_gives]
+    downs, mine = tie((downs, gate_gives[1]))
+    cross_gate_b = cross(mine)
     grad_down = product(*downs)
-    error_sum = butterfly(error_sum, "row")
-    cross_gates, grad_down, error_sum = tie((cross_gates, grad_down, error_sum))
+    grad_down, cross_gate_b, up_gives = tie((grad_down, cross_gate_b, up_gives))
     down_pair = split_cols(grad_down)
+    cross_up_a = cross(up_gives[0])
+    grad_qkv = product(*firsts)
+    grad_qkv, cross_up_a, up_gives, hiddens = tie((grad_qkv, cross_up_a, up_gives, hiddens))
+    qkv_pair = split_rows(grad_qkv)
+    out_pair = split_cols(product(*hiddens))
     twos = [two_a, two_b, *from_cores(cross_two_a, cross_two_b)]
-    gates = together(twos, [ups_a[0], ups_b[0], *cross_gates])
-    out_give = take(grad_out, 1 - side, part_wide, 0)
-    gates, up_gives = tie((gates, up_gives))
-    cross_ups = [cross(g) for g in up_gives]
+    gates = together(twos, [ups_a[0], ups_b[0], cross_gate_a, cross_gate_b])
+    gates, mine, qkv_pair, out_pair = tie((gates, up_gives[1], qkv_pair, out_pair))
+    cross_up_b = cross(mine)
     grad_gate = product(*gates)
-    error_sum = butterfly(error_sum, "col")
-    grad_gate, cross_ups, error_sum = tie((grad_gate, cross_ups, error_sum))
+    grad_gate, cross_up_b = tie((grad_gate, cross_up_b))
     gate_pair = split_rows(grad_gate)
-    ups = together(twos, [ups_a[2], ups_b[2], *cross_ups])
-    ups, out_give, back_gives = tie((ups, out_give, back_gives))
-    grad_out_got = cross(out_give)
-    cross_backs = [cross(g) for g in back_gives]
-    grad_up = product(*ups)
-    error_sum = butterfly(error_sum, "dp")
-    grad_up, grad_out_got, cross_backs, error_sum = tie(
-        (grad_up, grad_out_got, cross_backs, error_sum)
-    )
-    up_pair = split_rows(grad_up)
-    out_pair = split_cols(add_low(take(grad_out, side, part_wide, 0), grad_out_got))
-    qkv_pair = split_rows(
-        product(
-            *together(
-                [*low_first, *from_cores(first_a, first_b)],
-                [*[half_columns(g, side) for g in backs], *cross_backs],
+    up_pair = split_rows(
+        product(*together(twos, [ups_a[2], ups_b[2], cross_up_a, cross_up_b]))
+    )
+
+    def halves(pair, which):
+        three = [
+            ordered(
+                first_row,
+                *(take(p[:, i * wide : (i + 1) * wide], which, part_wide, 1) for p in pair),
+                1,
             )
-        )
-    )
-    three = [
-        ordered(
-            first_row,
-            qkv_pair[0][:, i * part_wide : (i + 1) * part_wide],
-            qkv_pair[1][:, i * part_wide : (i + 1) * part_wide],
-            1,
-        )
-        for i in range(3)
-    ]
+            for i in range(3)
+        ]
+        return [pack(jnp.concatenate(three[:2], axis=1), half_width), pack(three[2], half_width)]
+
     pieces, spots, starts = [], [], []
     total = 0
-    for pair in (down_pair, gate_pair, up_pair, out_pair):
+    out_mine = [take(p, side, part_wide, 0) for p in out_pair]
+    out_give = [take(p, 1 - side, part_wide, 0) for p in out_pair]
+    for pair in (down_pair, gate_pair, up_pair, out_mine):
         packed = [pack(p, half_width) for p in pair]
         size = packed[0].shape[0]
         pieces += packed
@@ -977,39 +1027,20 @@
         ]
         starts.append((total, size))
         total += 2 * size
-    for item in (jnp.concatenate(three[:2], axis=1), three[2]):
-        packed = pack(item, half_width)
+    for packed in halves(qkv_pair, side):
         size = packed.shape[0]
         pieces.append(packed)
         spots.append(lambda r, total=total: total + 0 * r)
         starts.append((total, size))
         total += size
+    gives = [pack(p, half_width) for p in out_give] + halves(qkv_pair, 1 - side)
     last_gots = [from_chips(p) for p in last_parts]
-    sums = line_sum(pieces, spots, chunk=min(256, total // 8))
+    sums = line_sum(pieces, spots, gives, chunk=min(256, total // 8))
     sums, last_parts, last_gots = tie((sums, last_parts, last_gots))
 
-    if cols == 2:
-        tall = min(1024, starts[0][1])
-
-        def rows_of(start, size, step):
-            def spot(j, i):
-                s, rest = i // (2 * step), i % (2 * step)
-                return (rest // step, (start + s * size) // tall + rest % step, 0)
-
-            return spot
-
-        def columns_at(start):
-            return lambda j, i: (j % 2, (start + (j // 2) * half_width) // tall + i, 0)
-
-        grad_down = widen(
-            sums,
-            down_weight.shape,
-            (tall, half_width),
-            rows_of(*starts[0], part_units // tall),
-        )
-        grad_gate, grad_up = (
-            widen(sums, gate_weight.shape, (tall, part_units), columns_at(starts[n][0]))
-            for n in (1, 2)
+    if cols == 2 and part_units == half_width:
+        grad_down, grad_gate, grad_up = widen_three(
+            sums, down_weight.shape, gate_weight.shape, half_width
         )
         grad_query, grad_key, grad_value, grad_output = widen_four(
             sums, query_weight.shape, [starts[n][0] for n in (4, 5, 3)], part_wide

time: 1130 us -> 1030 us (0.912)
  starting transfers between devices: 104 us -> 43.3 us
  local copies, waits for them, and re-layouts: 104 us -> 73.3 us
  waiting for transfers between devices: 105 us -> 79.7 us
  Pallas kernels: 645 us -> 660 us
  matrix products: 61.1 us -> 47 us
  other arithmetic: 95.2 us -> 109 us
    ppermute x8, starting transfers between devices: 72.3 us -> 16.8 us  [hop(): lax.ppermute(operand, axis, [(i, i ^ step) for i in range(size)])]
    ppermute x15 -> x10, waiting for transfers between devices: 84.8 us -> 45.8 us  [cross(): return lax.ppermute(operand, 'dp', sides)]
    dot_general x4 -> x0, matrix products: 12.6 us -> none  [contract_cols(): lax.dot_general(left, right, (((1,), (1,)), ((), ())), preferred_element_...]
    unnamed x307 -> x245, local copies, waits for them, and re-layouts: 51.6 us -> 39 us
    pallas_call x4 -> x5, Pallas kernels: 53.3 us -> 65.5 us  [in_vmem(): pl.pallas_call(kernel, out_shape=out_shape, in_specs=[pl.BlockSpec(memory...]
    concatenate x6, other arithmetic: 5.32 us -> 17.3 us  [both_cores(): return jnp.concatenate([kept, swap(swap_halves(kept, 1))], axis=0)]
    ppermute x2, waiting for transfers between devices: 0.01 us -> 11.5 us  [gather_blocks(): got = lax.ppermute(operand, 'col', [(0, 1), (1, 0)])]
    dynamic_slice x21 -> x10, local copies, waits for them, and re-layouts: 23.6 us -> 17.9 us  [take(): return lax.dynamic_slice_in_dim(operand, index * size, size, axis)]
  transfers between devices with their start and end apart: 68 -> 62, of which waited for: 15 -> 12; matrix products, arithmetic and copies ran while one was open for 20% -> 15% of each run, Pallas kernels for 57% -> 63%
where the time goes in v3:
time: 1030 us; the launch traced here: 1020 us
  Pallas kernels  660 us (64%)
  other arithmetic  109 us (11%)
  waiting for transfers between devices  79.7 us (8%)
  local copies, waits for them, and re-layouts  73.3 us (7%)
  matrix products  47 us (5%)
  starting transfers between devices  43.3 us (4%)
  between operations  11.3 us (1%)
    pallas_call x1, Pallas kernels, line_sum(): pl.pallas_call(functools.partial(line_kernel, sizes, spots, len(gives), c...  455 us
    pallas_call x4, Pallas kernels, feed_forward(): pl.pallas_call(functools.partial(kernel, side_steps=side_steps), out_shap...  102 us
    pallas_call x5, Pallas kernels, in_vmem(): pl.pallas_call(kernel, out_shape=out_shape, in_specs=[pl.BlockSpec(memory...  65.5 us
    dot_general x5, matrix products, contract_rows(): lax.dot_general(left, right, (((0,), (0,)), ((), ())), preferred_element_...  47 us
    ppermute x10, waiting for transfers between devices, cross(): return lax.ppermute(operand, 'dp', sides)  45.8 us
    unnamed x245, local copies, waits for them, and re-layouts  39 us
    pallas_call x1, Pallas kernels, widen_three(): pl.pallas_call(kernel, out_shape=[jax.ShapeDtypeStruct(x, F32) for x in (...  27.5 us
  transfers between devices with their start and end apart: 62, of which 12 were waited for; matrix products, arithmetic and copies ran while one was open for 15% of the time, Pallas kernels for 63%

profile of v3, /device:TPU:0, one launch (start us, length us, event | category | flops | bytes accessed | tf_op | source)
XLA Modules:
  0.0 1023.9 jit_solution(12191358810961560852)
XLA Ops:
  3.0 3.0 collective-permute-start.2
  15.2 2.8 fusion.58
  17.9 11.5 %collective-permute-done = bf16[512,512]{1,0:T(8,128)(2,1)} collective-permute-done((bf16[512,512]{1,0:T(8,128)(2,1)}, bf16[512,512]{1,0:T(8,128)(2,1)}, u32[]{:S(2)}, u32[]{:S(2)}) %collective-permute-start) | collective-permute-done | bytes 524320 | tf_op jit(solution)/shard_map/ppermute | solution.py:700
  40.2 12.7 %attention.2 = (bf16[512,512]{1,0:T(8,128)(2,1)S(1)}, bf16[512,512]{1,0:T(8,128)(2,1)S(1)}, bf16[512,512]{1,0:T(8,128)(2,1)}, bf16[512,512]{1,0:T(8,128)(2,1)}, ...) custom-call(bf16[512,2048]{1,0:T(8,128)(2,1)} %fusion.5.x_ref, ...), custom_call_target="tpu_custom_call" | custom-call | flops 8000000000 | bytes 20000000 | tf_op jit(solution)/shard_map/attention/pallas_call | solution.py:423
  57.6 4.8 constant_dynamic-slice_fusion.6
  62.4 4.9 constant_dynamic-slice_fusion.7
  67.3 2.3 constant_dynamic-slice_fusion.8
  74.3 15.9 %attention.3 = (bf16[512,512]{1,0:T(8,128)(2,1)S(1)}, bf16[512,512]{1,0:T(8,128)(2,1)S(1)}, bf16[512,512]{1,0:T(8,128)(2,1)}, bf16[512,512]{1,0:T(8,128)(2,1)}, ...) custom-call(bf16[512,2048]{1,0:T(8,128)(2,1)} %fusion.7.x_ref, ...), custom_call_target="tpu_custom_call" | custom-call | flops 8000000000 | bytes 20000000 | tf_op jit(solution)/shard_map/attention/pallas_call | solution.py:423
  91.7 4.4 collective-permute-done.7
  100.3 2.9 collective-permute-done.12
  103.2 3.1 pad_maximum_fusion.7.x_ref
  108.0 3.2 collective-permute-start.16
  114.2 24.6 %feed_forward.2 = (f32[512,2048]{1,0:T(8,128)}, f32[512,2048]{1,0:T(8,128)}, bf16[512,1024]{1,0:T(8,128)(2,1)S(1)}, bf16[512,1024]{1,0:T(8,128)(2,1)}, f32[256,2048]{1,0:T(8,128)}, /*index=5*/bf16[256,2048]{1,0:T(8,128)(2,1)}) custom-call(s32[2]{0:T(128)S(1)} %pad_add_fusion.10.r_ref, bf16[512,2048]{1,0:T(8,128)(2,1)} %pad_maximum_fusion.7.x_ref, ...), custom_call_target="tpu_custom_call" | custom-call | flops 12884901888 | bytes 37748736 | tf_op jit(solution)/shard_map/feed_forward/pallas_call | solution.py:575
  148.1 3.2 pad_maximum_fusion.8.x_ref
  153.1 3.9 collective-permute-start.22
  158.1 24.2 %feed_forward.3 = (f32[512,2048]{1,0:T(8,128)}, f32[512,2048]{1,0:T(8,128)}, bf16[512,1024]{1,0:T(8,128)(2,1)S(1)}, bf16[512,1024]{1,0:T(8,128)(2,1)}, f32[256,2048]{1,0:T(8,128)}, /*index=5*/bf16[256,2048]{1,0:T(8,128)(2,1)}) custom-call(s32[2]{0:T(128)S(1)} %pad_add_fusion.10.r_ref, bf16[512,2048]{1,0:T(8,128)(2,1)} %pad_maximum_fusion.8.x_ref, ...), custom_call_target="tpu_custom_call" | custom-call | flops 12884901888 | bytes 37748736 | tf_op jit(solution)/shard_map/feed_forward/pallas_call | solution.py:575
  187.7 3.4 collective-permute-done.26
  192.2 3.2 pad_maximum_fusion.9.g_ref
  200.3 26.4 %feed_forward_back.2 = (bf16[512,1024]{1,0:T(8,128)(2,1)S(1)}, bf16[512,1024]{1,0:T(8,128)(2,1)}, bf16[512,1024]{1,0:T(8,128)(2,1)}, bf16[512,1024]{1,0:T(8,128)...) custom-call(s32[2]{0:T(128)S(1)} %pad_add_fusion.10.r_ref, bf16[512,2048]{1,0:T(8,128)(2,1)} %pad_maximum_fusion.9.g_ref, ...), custom_call_target="tpu_custom_call" | custom-call | flops 12884901888 | bytes 37748736 | tf_op jit(solution)/shard_map/feed_forward_back/pallas_call | solution.py:575
  231.8 2.6 multiply_reduce_fusion.5
  235.6 2.4 multiply_reduce_fusion.4
  239.2 3.3 pad_maximum_fusion.10.g_ref
  248.1 26.6 %feed_forward_back.3 = (bf16[512,1024]{1,0:T(8,128)(2,1)S(1)}, bf16[512,1024]{1,0:T(8,128)(2,1)}, bf16[512,1024]{1,0:T(8,128)(2,1)}, bf16[512,1024]{1,0:T(8,128)...) custom-call(s32[2]{0:T(128)S(1)} %pad_add_fusion.10.r_ref, bf16[512,2048]{1,0:T(8,128)(2,1)} %pad_maximum_fusion.10.g_ref, ...), custom_call_target="tpu_custom_call" | custom-call | flops 12884901888 | bytes 37748736 | tf_op jit(solution)/shard_map/feed_forward_back/pallas_call | solution.py:575
  277.3 2.2 fusion.67
  283.6 2.3 pad_maximum_fusion.29
  289.0 3.0 pad_maximum_fusion.11.g_ref
  292.1 2.7 fusion.66
  302.5 9.8 attention_back.2
  312.3 7.8 collective-permute-done.37
  323.0 2.2 fusion.65
  336.0 2.6 constant_dynamic-update-slice_fusion.3
  340.2 15.0 %attention_back.3 = (bf16[512,1024]{1,0:T(8,128)(2,1)}, bf16[512,1536]{1,0:T(8,128)(2,1)}) custom-call(bf16[512,2048]{1,0:T(8,128)(2,1)} %pad_maximum_fusion.12.g_ref, bf16[512,1024]{1,0:T(8,128)(2,1)} %get-tuple-element.455.out_own, bf16[512,1024]{1,0:T(8,128)(2,1)} %collective-permute-done.5.out_got, f32[512,128]{1,0:T(8,128)S(1)} %copy-done.11, ...), custom_call_target="tpu_custom_call" | custom-call | flops 8000000000 | bytes 20000000 | tf_op jit(solution)/shard_map/attention_back/pallas_call | solution.py:423
  355.8 3.1 collective-permute-done.41
  367.4 2.6 pad_maximum_fusion.2
  375.5 13.2 %convolution_convert_fusion.1 = bf16[1024,2048]{1,0:T(8,128)(2,1)} fusion(bf16[2048,1024]{1,0:T(8,128)(2,1)S(1)} %pad_maximum_fusion, bf16[2048,2048]{1,0:T(8,128)(2,1)} %slice_dynamic-update-slice_fusion.2), kind=kOutput, calls=%fused_computation.28 | convolution fusion | flops 8592031744 | bytes 16777216 | tf_op jit(solution)/shard_map/dot_general | solution.py:40
  388.7 29.7 %collective-permute-done.47 = bf16[512,1024]{1,0:T(8,128)(2,1)S(1)} collective-permute-done((bf16[512,1024]{1,0:T(8,128)(2,1)S(1)}, bf16[512,1024]{1,0:T(8,128)(2,1)S(1)}, u32[]{:S(2)}, u32[]{:S(2)}) %collective-permute-start.47) | collective-permute-done | bytes 1048608 | tf_op jit(solution)/shard_map/ppermute | solution.py:696
  418.9 7.6 convolution_convert_fusion
  427.6 12.0 %first_norm_back.1 = (f32[256,2048]{1,0:T(8,128)}, bf16[256,2048]{1,0:T(8,128)(2,1)S(1)}, f32[256,2048]{1,0:T(8,128)}, bf16[256,2048]{1,0:T(8,128)(2,1)}) custom-call(bf16[512,1536]{1,0:T(8,128)(2,1)} %copy-done.103, bf16[512,1536]{1,0:T(8,128)(2,1)} %get-tuple-element.299.b_ref, bf16[1024,1536]{1,0:T(8,128)(2,1)} %pad_maximum_fusion.3.own_ref, ...), custom_call_target="tpu_custom_call" | custom-call | flops 8000000000 | bytes 20000000 | tf_op jit(solution)/shard_map/first_norm_back/pallas_call | solution.py:423
  452.1 2.4 convolution_convert_fusion.3
  462.6 11.8 %convolution_convert_fusion.2 = bf16[2048,1024]{1,0:T(8,128)(2,1)S(1)} fusion(bf16[2048,2048]{1,0:T(8,128)(2,1)} %slice_dynamic-update-slice_fusion, bf16[2048,1024]{1,0:T(8,128)(2,1)S(1)} %pad_maximum_fusion.1), kind=kOutput, calls=%fused_computation.29 | convolution fusion | flops 8592031744 | bytes 16777216 | tf_op jit(solution)/shard_map/dot_general | solution.py:40
  474.3 11.7 %collective-permute-done.53 = bf16[512,1024]{1,0:T(8,128)(2,1)S(1)} collective-permute-done((bf16[512,1024]{1,0:T(8,128)(2,1)S(1)}, bf16[512,1024]{1,0:T(8,128)(2,1)S(1)}, u32[]{:S(2)}, u32[]{:S(2)}) %collective-permute-start.53) | collective-permute-done | bytes 1048608 | tf_op jit(solution)/shard_map/ppermute | solution.py:696
  487.8 12.1 %fusion.19 = bf16[2048,1024]{1,0:T(8,128)(2,1)S(1)} fusion(bf16[2048,2048]{1,0:T(8,128)(2,1)} %slice_dynamic-update-slice_fusion, bf16[512,1024]{1,0:T(8,128)(2,1)S(1)} %collective-permute-done.53, bf16[512,1024]{1,0:T(8,128)(2,1)} %collective-permute-done.50, bf16[512,1024]{1,0:T(8,128)(2,1)S(1)} %copy-done.111, bf16[512,1024]{1,0:T(8,128)(2,1)S(1)} %copy-done.110), kind=kOutput, calls=%fused_computation.27 | convolution fusion | flops 8608808960 | bytes 16777216 | tf_op jit(solution)/shard_map/dot_general | solution.py:40
  513.7 455.1 %line_sum.1.qk_a.qk_b.v_a.v_b.o_ref.in_ref = bf16[2,8192,1024]{2,1,0:T(8,128)(2,1)} custom-call(bf16[1024,1024]{1,0:T(8,128)(2,1)} %get-tuple-element.421.refs_0_, bf16[1024,1024]{1,0:T(8,128)(2,1)} %collective-permute-done.48.refs_1_, bf16[1024,1024]{1,0:T(8,128)(2,1)} %get-tuple-element.419.refs_2_, bf16[1024,1024]{1,0:T(8,128)(2,1)} %copy-done.82, ...), custom_call_target="tpu_custom_call" | custom-call | tf_op jit(solution)/shard_map/line_sum/pallas_call | solution.py:270
  968.9 2.6 fusion.47
  972.0 2.1 fusion.31
  977.9 2.1 fusion.38
  982.2 10.7 %widen_four.1 = (f32[1024,1024]{1,0:T(8,128)}, f32[1024,1024]{1,0:T(8,128)}, f32[1024,1024]{1,0:T(8,128)}, f32[1024,1024]{1,0:T(8,128)}) custom-call(bf16[2,8192,1024]{2,1,0:T(8,128)(2,1)} %line_sum.1.qk_a.qk_b.v_a.v_b.o_ref.in_ref, bf16[2,8192,1024]{2,1,0:T(8,128)(2,1)} %line_sum.1.qk_a.qk_b.v_a.v_b.o_ref.in_ref, ...), custom_call_target="tpu_custom_call" | custom-call | tf_op jit(solution)/shard_map/widen_four/pallas_call | solution.py:643
  992.9 27.5 %widen_three.1 = (f32[4096,1024]{1,0:T(8,128)}, f32[1024,4096]{1,0:T(8,128)}, f32[1024,4096]{1,0:T(8,128)}) custom-call(bf16[2,8192,1024]{2,1,0:T(8,128)(2,1)} %line_sum.1.qk_a.qk_b.v_a.v_b.o_ref.in_ref), custom_call_target="tpu_custom_call" | custom-call | tf_op jit(solution)/shard_map/widen_three/pallas_call | solution.py:608
  (503 shorter events, 163.7 us)
Async XLA Ops:
  3.0 28.0 %collective-permute-start.2 = (bf16[512,512]{1,0:T(8,128)(2,1)}, bf16[512,512]{1,0:T(8,128)(2,1)}, u32[]{:S(2)}, u32[]{:S(2)}) collective-permute-start(bf16[512,512]{1,0:T(8,128)(2,1)} %pad_maximum_fusion.31), channel_id=1, source_target_pairs={{0,1},{1,0},{2,3},{3,2},{4,5},{5,4},{6,7},{7,6},{8,9},{9,8},{10,11... | collective-permute-start | bytes 1572872 | tf_op jit(solution)/shard_map/ppermute | solution.py:700
  6.8 22.6 %collective-permute-start = (bf16[512,512]{1,0:T(8,128)(2,1)}, bf16[512,512]{1,0:T(8,128)(2,1)}, u32[]{:S(2)}, u32[]{:S(2)}) collective-permute-start(bf16[512,512]{1,0:T(8,128)(2,1)} %pad_maximum_fusion.30), channel_id=1, source_target_pairs={{0,1},{1,0},{2,3},{3,2},{4,5},{5,4},{6,7},{7,6},{8,9},{9,8},{10,11... | collective-permute-start | bytes 1572872 | tf_op jit(solution)/shard_map/ppermute | solution.py:700
  8.3 31.9 %collective-permute-start.5 = (bf16[512,1024]{1,0:T(8,128)(2,1)}, bf16[512,1024]{1,0:T(8,128)(2,1)}, u32[]{:S(2)}, u32[]{:S(2)}) collective-permute-start(bf16[512,1024]{1,0:T(8,128)(2,1)} %get-tuple-element.454), channel_id=1, source_target_pairs={{0,2},{2,0},{1,3},{3,1},{4,6},{6,4},{5,7},{7,5},{8,10},{10,8},{9,1... | collective-permute-start | bytes 3145736 | tf_op jit(solution)/shard_map/ppermute | solution.py:693
  14.3 25.9 %collective-permute-start.4 = (bf16[1024,1536]{1,0:T(8,128)(2,1)}, bf16[1024,1536]{1,0:T(8,128)(2,1)}, u32[]{:S(2)}, u32[]{:S(2)}) collective-permute-start(bf16[1024,1536]{1,0:T(8,128)(2,1)} %pad_maximum_fusion.4), channel_id=1, source_target_pairs={{0,2},{2,0},{1,3},{3,1},{4,6},{6,4},{5,7},{7,5},{8,10},{10,8},{9,1... | collective-permute-start | bytes 9437192 | tf_op jit(solution)/shard_map/ppermute | solution.py:693
  69.7 26.4 %collective-permute-start.9 = (bf16[1024,2048]{1,0:T(8,128)(2,1)}, bf16[1024,2048]{1,0:T(8,128)(2,1)}, u32[]{:S(2)}, u32[]{:S(2)}) collective-permute-start(bf16[1024,2048]{1,0:T(8,128)(2,1)} %constant_dynamic-slice_fusion.8), channel_id=1, source_target_pairs={{0,2},{2,0},{1,3},{3,1},{4,6},{6,4},{5,7},{7,5},{8,10},{10,8},{9,1... | collective-permute-start | bytes 12582920 | tf_op jit(solution)/shard_map/ppermute | solution.py:693
  69.9 26.1 %collective-permute-start.10 = (bf16[1024,2048]{1,0:T(8,128)(2,1)}, bf16[1024,2048]{1,0:T(8,128)(2,1)}, u32[]{:S(2)}, u32[]{:S(2)}) collective-permute-start(bf16[1024,2048]{1,0:T(8,128)(2,1)} %constant_dynamic-slice_fusion.7), channel_id=1, source_target_pairs={{0,2},{2,0},{1,3},{3,1},{4,6},{6,4},{5,7},{7,5},{8,10},{10,8},{9,1... | collective-permute-start | bytes 12582920 | tf_op jit(solution)/shard_map/ppermute | solution.py:693
  70.2 25.8 %collective-permute-start.11 = (bf16[2048,1024]{1,0:T(8,128)(2,1)}, bf16[2048,1024]{1,0:T(8,128)(2,1)}, u32[]{:S(2)}, u32[]{:S(2)}) collective-permute-start(bf16[2048,1024]{1,0:T(8,128)(2,1)} %constant_dynamic-slice_fusion.6), channel_id=1, source_target_pairs={{0,2},{2,0},{1,3},{3,1},{4,6},{6,4},{5,7},{7,5},{8,10},{10,8},{9,1... | collective-permute-start | bytes 12582920 | tf_op jit(solution)/shard_map/ppermute | solution.py:693
  70.6 25.4 %collective-permute-start.7 = (bf16[256,2048]{1,0:T(8,128)(2,1)S(1)}, bf16[256,2048]{1,0:T(8,128)(2,1)S(1)}, u32[]{:S(2)}, u32[]{:S(2)}) collective-permute-start(bf16[256,2048]{1,0:T(8,128)(2,1)S(1)} %get-tuple-element.194), channel_id=1, source_target_pairs={{0,1},{1,0},{2,3},{3,2},{4,5},{5,4},{6,7},{7,6},{8,9},{9,8},{10,11... | collective-permute-start | bytes 3145736 | tf_op jit(solution)/shard_map/ppermute | solution.py:706
  72.8 17.5 %collective-permute-start.8 = (f32[1,1]{1,0:T(1,128)}, f32[1,1]{1,0:T(1,128)}, u32[]{:S(2)}, u32[]{:S(2)}) collective-permute-start(f32[1,1]{1,0:T(1,128)} %bitcast.4), channel_id=1, source_target_pairs={{0,4},{4,0},{8,12},{12,8},{16,20},{20,16},{24,28},{28,24},{1,5},{5... | collective-permute-start | bytes 20 | tf_op jit(solution)/shard_map/ppermute | solution.py:316
  108.0 30.7 %collective-permute-start.16 = (f32[1,1]{1,0:T(1,128)}, f32[1,1]{1,0:T(1,128)}, u32[]{:S(2)}, u32[]{:S(2)}) collective-permute-start(f32[1,1]{1,0:T(1,128)} %add.216), channel_id=1, source_target_pairs={{0,8},{4,12},{8,0},{12,4},{16,24},{20,28},{24,16},{28,20},{1,9},{5... | collective-permute-start | bytes 20 | tf_op jit(solution)/shard_map/ppermute | solution.py:316
  111.2 28.3 %collective-permute-start.14 = (bf16[256,2048]{1,0:T(8,128)(2,1)S(1)}, bf16[256,2048]{1,0:T(8,128)(2,1)S(1)}, u32[]{:S(2)}, u32[]{:S(2)}) collective-permute-start(bf16[256,2048]{1,0:T(8,128)(2,1)S(1)} %get-tuple-element.212), channel_id=1, source_target_pairs={{0,1},{1,0},{2,3},{3,2},{4,5},{5,4},{6,7},{7,6},{8,9},{9,8},{10,11... | collective-permute-start | bytes 3145736 | tf_op jit(solution)/shard_map/ppermute | solution.py:706
  112.7 26.8 %collective-permute-start.15 = (bf16[256,2048]{1,0:T(8,128)(2,1)}, bf16[256,2048]{1,0:T(8,128)(2,1)S(1)}, u32[]{:S(2)}, u32[]{:S(2)}) collective-permute-start(bf16[256,2048]{1,0:T(8,128)(2,1)} %fusion.39), channel_id=1, source_target_pairs={{0,4},{4,0},{8,12},{12,8},{16,20},{20,16},{24,28},{28,24},{1,5},{5... | collective-permute-start | bytes 3145736 | tf_op jit(solution)/shard_map/ppermute | solution.py:696
  144.3 7.0 collective-permute-start.18
  153.1 29.2 %collective-permute-start.22 = (f32[1,1]{1,0:T(1,128)}, f32[1,1]{1,0:T(1,128)}, u32[]{:S(2)}, u32[]{:S(2)}) collective-permute-start(f32[1,1]{1,0:T(1,128)} %add.223), channel_id=1, source_target_pairs={{0,16},{4,20},{8,24},{12,28},{16,0},{20,4},{24,8},{28,12},{1,17},{... | collective-permute-start | bytes 20 | tf_op jit(solution)/shard_map/ppermute | solution.py:316
  157.1 25.9 %collective-permute-start.20 = (bf16[256,2048]{1,0:T(8,128)(2,1)S(1)}, bf16[256,2048]{1,0:T(8,128)(2,1)S(1)}, u32[]{:S(2)}, u32[]{:S(2)}) collective-permute-start(bf16[256,2048]{1,0:T(8,128)(2,1)S(1)} %get-tuple-element.227), channel_id=1, source_target_pairs={{0,1},{1,0},{2,3},{3,2},{4,5},{5,4},{6,7},{7,6},{8,9},{9,8},{10,11... | collective-permute-start | bytes 3145736 | tf_op jit(solution)/shard_map/ppermute | solution.py:706
  157.6 25.4 %collective-permute-start.21 = (bf16[256,2048]{1,0:T(8,128)(2,1)S(1)}, bf16[256,2048]{1,0:T(8,128)(2,1)S(1)}, u32[]{:S(2)}, u32[]{:S(2)}) collective-permute-start(bf16[256,2048]{1,0:T(8,128)(2,1)S(1)} %fusion.40), channel_id=1, source_target_pairs={{0,4},{4,0},{8,12},{12,8},{16,20},{20,16},{24,28},{28,24},{1,5},{5... | collective-permute-start | bytes 3145736 | tf_op jit(solution)/shard_map/ppermute | solution.py:696
  186.2 9.2 collective-permute-start.25
  197.2 29.5 %collective-permute-start.27 = (bf16[256,2048]{1,0:T(8,128)(2,1)S(1)}, bf16[256,2048]{1,0:T(8,128)(2,1)S(1)}, u32[]{:S(2)}, u32[]{:S(2)}) collective-permute-start(bf16[256,2048]{1,0:T(8,128)(2,1)S(1)} %get-tuple-element.245), channel_id=1, source_target_pairs={{0,1},{1,0},{2,3},{3,2},{4,5},{5,4},{6,7},{7,6},{8,9},{9,8},{10,11... | collective-permute-start | bytes 3145736 | tf_op jit(solution)/shard_map/ppermute | solution.py:706
  198.8 27.9 %collective-permute-start.28 = (bf16[512,1024]{1,0:T(8,128)(2,1)}, bf16[512,1024]{1,0:T(8,128)(2,1)S(1)}, u32[]{:S(2)}, u32[]{:S(2)}) collective-permute-start(bf16[512,1024]{1,0:T(8,128)(2,1)} %get-tuple-element.246), channel_id=1, source_target_pairs={{0,4},{4,0},{8,12},{12,8},{16,20},{20,16},{24,28},{28,24},{1,5},{5... | collective-permute-start | bytes 3145736 | tf_op jit(solution)/shard_map/ppermute | solution.py:696
  229.6 9.6 collective-permute-start.30
  231.7 10.8 %collective-permute-start.31 = (bf16[256,2048]{1,0:T(8,128)(2,1)}, bf16[256,2048]{1,0:T(8,128)(2,1)}, u32[]{:S(2)}, u32[]{:S(2)}) collective-permute-start(bf16[256,2048]{1,0:T(8,128)(2,1)} %get-tuple-element.249), channel_id=1, source_target_pairs={{0,2},{2,0},{1,3},{3,1},{4,6},{6,4},{5,7},{7,5},{8,10},{10,8},{9,1... | collective-permute-start | bytes 3145736 | tf_op jit(solution)/shard_map/ppermute | solution.py:693
  244.2 30.5 %collective-permute-start.34 = (f32[1,1]{1,0:T(1,128)}, f32[1,1]{1,0:T(1,128)}, u32[]{:S(2)}, u32[]{:S(2)}) collective-permute-start(f32[1,1]{1,0:T(1,128)} %bitcast.12), channel_id=1, source_target_pairs={{0,4},{4,0},{8,12},{12,8},{16,20},{20,16},{24,28},{28,24},{1,5},{5... | collective-permute-start | bytes 20 | tf_op jit(solution)/shard_map/ppermute | solution.py:316
  246.0 29.2 %collective-permute-start.32 = (bf16[256,2048]{1,0:T(8,128)(2,1)S(1)}, bf16[256,2048]{1,0:T(8,128)(2,1)S(1)}, u32[]{:S(2)}, u32[]{:S(2)}) collective-permute-start(bf16[256,2048]{1,0:T(8,128)(2,1)S(1)} %get-tuple-element.261), channel_id=1, source_target_pairs={{0,1},{1,0},{2,3},{3,2},{4,5},{5,4},{6,7},{7,6},{8,9},{9,8},{10,11... | collective-permute-start | bytes 3145736 | tf_op jit(solution)/shard_map/ppermute | solution.py:706
  246.6 28.7 %collective-permute-start.33 = (bf16[512,1024]{1,0:T(8,128)(2,1)}, bf16[512,1024]{1,0:T(8,128)(2,1)S(1)}, u32[]{:S(2)}, u32[]{:S(2)}) collective-permute-start(bf16[512,1024]{1,0:T(8,128)(2,1)} %get-tuple-element.262), channel_id=1, source_target_pairs={{0,4},{4,0},{8,12},{12,8},{16,20},{20,16},{24,28},{28,24},{1,5},{5... | collective-permute-start | bytes 3145736 | tf_op jit(solution)/shard_map/ppermute | solution.py:696
  280.8 7.7 collective-permute-start.35
  280.8 11.2 %collective-permute-start.36 = (bf16[256,2048]{1,0:T(8,128)(2,1)}, bf16[256,2048]{1,0:T(8,128)(2,1)}, u32[]{:S(2)}, u32[]{:S(2)}) collective-permute-start(bf16[256,2048]{1,0:T(8,128)(2,1)} %get-tuple-element.266), channel_id=1, source_target_pairs={{0,2},{2,0},{1,3},{3,1},{4,6},{6,4},{5,7},{7,5},{8,10},{10,8},{9,1... | collective-permute-start | bytes 3145736 | tf_op jit(solution)/shard_map/ppermute | solution.py:693
  294.8 25.3 %collective-permute-start.37 = (bf16[256,2048]{1,0:T(8,128)(2,1)}, bf16[256,2048]{1,0:T(8,128)(2,1)S(1)}, u32[]{:S(2)}, u32[]{:S(2)}) collective-permute-start(bf16[256,2048]{1,0:T(8,128)(2,1)} %get-tuple-element.274), channel_id=1, source_target_pairs={{0,1},{1,0},{2,3},{3,2},{4,5},{5,4},{6,7},{7,6},{8,9},{9,8},{10,11... | collective-permute-start | bytes 3145736 | tf_op jit(solution)/shard_map/ppermute | solution.py:706
  296.3 25.1 %collective-permute-start.38 = (bf16[256,2048]{1,0:T(8,128)(2,1)}, bf16[256,2048]{1,0:T(8,128)(2,1)}, u32[]{:S(2)}, u32[]{:S(2)}) collective-permute-start(bf16[256,2048]{1,0:T(8,128)(2,1)} %slice.328), channel_id=1, source_target_pairs={{0,4},{4,0},{8,12},{12,8},{16,20},{20,16},{24,28},{28,24},{1,5},{5... | collective-permute-start | bytes 3145736 | tf_op jit(solution)/shard_map/ppermute | solution.py:696
  298.3 61.2 %collective-permute-start.23 = (bf16[256,512]{1,0:T(8,128)(2,1)}, bf16[256,512]{1,0:T(8,128)(2,1)}, u32[]{:S(2)}, u32[]{:S(2)}) collective-permute-start(bf16[256,512]{1,0:T(8,128)(2,1)} %get-tuple-element.481), channel_id=1, source_target_pairs={{0,2},{2,0},{1,3},{3,1},{4,6},{6,4},{5,7},{7,5},{8,10},{10,8},{9,1... | collective-permute-start | bytes 786440 | tf_op jit(solution)/shard_map/ppermute | solution.py:693
  325.4 6.9 collective-permute-start.40
  328.9 34.1 %collective-permute-start.49 = (bf16[512,2048]{1,0:T(8,128)(2,1)}, bf16[512,2048]{1,0:T(8,128)(2,1)S(1)}, u32[]{:S(2)}, u32[]{:S(2)}) collective-permute-start(bf16[512,2048]{1,0:T(8,128)(2,1)} %pad_maximum_fusion.14), channel_id=1, source_target_pairs={{0,2},{2,0},{1,3},{3,1},{4,6},{6,4},{5,7},{7,5},{8,10},{10,8},{9,1... | collective-permute-start | bytes 6291464 | tf_op jit(solution)/shard_map/ppermute | solution.py:693
  333.9 25.0 %collective-permute-start.41 = (bf16[256,2048]{1,0:T(8,128)(2,1)}, bf16[256,2048]{1,0:T(8,128)(2,1)S(1)}, u32[]{:S(2)}, u32[]{:S(2)}) collective-permute-start(bf16[256,2048]{1,0:T(8,128)(2,1)} %slice.331), channel_id=1, source_target_pairs={{0,4},{4,0},{8,12},{12,8},{16,20},{20,16},{24,28},{28,24},{1,5},{5... | collective-permute-start | bytes 3145736 | tf_op jit(solution)/shard_map/ppermute | solution.py:696
  338.5 16.7 %collective-permute-start.42 = (f32[1,1]{1,0:T(1,128)}, f32[1,1]{1,0:T(1,128)}, u32[]{:S(2)}, u32[]{:S(2)}) collective-permute-start(f32[1,1]{1,0:T(1,128)} %add.247), channel_id=1, source_target_pairs={{0,16},{4,20},{8,24},{12,28},{16,0},{20,4},{24,8},{28,12},{1,17},{... | collective-permute-start | bytes 20 | tf_op jit(solution)/shard_map/ppermute | solution.py:316
  359.4 11.3 %collective-permute-start.46 = (bf16[512,2048]{1,0:T(8,128)(2,1)S(1)}, bf16[512,2048]{1,0:T(8,128)(2,1)S(1)}, u32[]{:S(2)}, u32[]{:S(2)}) collective-permute-start(bf16[512,2048]{1,0:T(8,128)(2,1)S(1)} %pad_maximum_fusion.13), channel_id=1, source_target_pairs={{0,2},{2,0},{1,3},{3,1},{4,6},{6,4},{5,7},{7,5},{8,10},{10,8},{9,1... | collective-permute-start | bytes 6291464 | tf_op jit(solution)/shard_map/ppermute | solution.py:693
  363.0 84.2 %collective-permute-start.29 = (bf16[256,512]{1,0:T(8,128)(2,1)S(1)}, bf16[256,512]{1,0:T(8,128)(2,1)S(1)}, u32[]{:S(2)}, u32[]{:S(2)}) collective-permute-start(bf16[256,512]{1,0:T(8,128)(2,1)S(1)} %copy-done.102), channel_id=1, source_target_pairs={{0,2},{2,0},{1,3},{3,1},{4,6},{6,4},{5,7},{7,5},{8,10},{10,8},{9,1... | collective-permute-start | bytes 786440 | tf_op jit(solution)/shard_map/ppermute | solution.py:693
  370.1 74.5 %collective-permute-start.43 = (bf16[512,1024]{1,0:T(8,128)(2,1)}, bf16[512,1024]{1,0:T(8,128)(2,1)S(1)}, u32[]{:S(2)}, u32[]{:S(2)}) collective-permute-start(bf16[512,1024]{1,0:T(8,128)(2,1)} %get-tuple-element.304), channel_id=1, source_target_pairs={{0,4},{4,0},{8,12},{12,8},{16,20},{20,16},{24,28},{28,24},{1,5},{5... | collective-permute-start | bytes 3145736 | tf_op jit(solution)/shard_map/ppermute | solution.py:696
  373.9 44.5 %collective-permute-start.47 = (bf16[512,1024]{1,0:T(8,128)(2,1)S(1)}, bf16[512,1024]{1,0:T(8,128)(2,1)S(1)}, u32[]{:S(2)}, u32[]{:S(2)}) collective-permute-start(bf16[512,1024]{1,0:T(8,128)(2,1)S(1)} %copy-done.113), channel_id=1, source_target_pairs={{0,4},{4,0},{8,12},{12,8},{16,20},{20,16},{24,28},{28,24},{1,5},{5... | collective-permute-start | bytes 3145736 | tf_op jit(solution)/shard_map/ppermute | solution.py:696
  418.4 26.3 %collective-permute-start.50 = (bf16[512,1024]{1,0:T(8,128)(2,1)}, bf16[512,1024]{1,0:T(8,128)(2,1)}, u32[]{:S(2)}, u32[]{:S(2)}) collective-permute-start(bf16[512,1024]{1,0:T(8,128)(2,1)} %get-tuple-element.326), channel_id=1, source_target_pairs={{0,4},{4,0},{8,12},{12,8},{16,20},{20,16},{24,28},{28,24},{1,5},{5... | collective-permute-start | bytes 3145736 | tf_op jit(solution)/shard_map/ppermute | solution.py:696
  426.6 13.1 %collective-permute-start.44 = (f32[1,1]{1,0:T(1,128)}, f32[1,1]{1,0:T(1,128)}, u32[]{:S(2)}, u32[]{:S(2)}) collective-permute-start(f32[1,1]{1,0:T(1,128)} %add.250), channel_id=1, source_target_pairs={{0,2},{2,0},{1,3},{3,1},{4,6},{6,4},{5,7},{7,5},{8,10},{10,8},{9,1... | collective-permute-start | bytes 20 | tf_op jit(solution)/shard_map/ppermute | solution.py:316
  446.0 14.4 %collective-permute-start.51 = (bf16[1024,1536]{1,0:T(8,128)(2,1)S(1)}, bf16[1024,1536]{1,0:T(8,128)(2,1)S(1)}, u32[]{:S(2)}, u32[]{:S(2)}) collective-permute-start(bf16[1024,1536]{1,0:T(8,128)(2,1)S(1)} %get-tuple-element.414), channel_id=1, source_target_pairs={{0,2},{2,0},{1,3},{3,1},{4,6},{6,4},{5,7},{7,5},{8,10},{10,8},{9,1... | collective-permute-start | bytes 9437192 | tf_op jit(solution)/shard_map/ppermute | solution.py:693
  450.6 518.2 %collective-permute-start.58 = (bf16[256,2048]{1,0:T(8,128)(2,1)}, bf16[256,2048]{1,0:T(8,128)(2,1)}, u32[]{:S(2)}, u32[]{:S(2)}) collective-permute-start(bf16[256,2048]{1,0:T(8,128)(2,1)} %get-tuple-element.372), channel_id=1, source_target_pairs={{0,1},{1,0},{2,3},{3,2},{4,5},{5,4},{6,7},{7,6},{8,9},{9,8},{10,11... | collective-permute-start | bytes 3145736 | tf_op jit(solution)/shard_map/ppermute | solution.py:706
  457.5 511.3 %collective-permute-start.59 = (bf16[256,2048]{1,0:T(8,128)(2,1)}, bf16[256,2048]{1,0:T(8,128)(2,1)}, u32[]{:S(2)}, u32[]{:S(2)}) collective-permute-start(bf16[256,2048]{1,0:T(8,128)(2,1)} %get-tuple-element.370), channel_id=1, source_target_pairs={{0,1},{1,0},{2,3},{3,2},{4,5},{5,4},{6,7},{7,6},{8,9},{9,8},{10,11... | collective-permute-start | bytes 3145736 | tf_op jit(solution)/shard_map/ppermute | solution.py:706
  459.8 51.8 %collective-permute-start.48 = (bf16[1024,1024]{1,0:T(8,128)(2,1)S(1)}, bf16[1024,1024]{1,0:T(8,128)(2,1)}, u32[]{:S(2)}, u32[]{:S(2)}) collective-permute-start(bf16[1024,1024]{1,0:T(8,128)(2,1)S(1)} %get-tuple-element.420), channel_id=1, source_target_pairs={{0,2},{2,0},{1,3},{3,1},{4,6},{6,4},{5,7},{7,5},{8,10},{10,8},{9,1... | collective-permute-start | bytes 6291464 | tf_op jit(solution)/shard_map/ppermute | solution.py:693
  461.0 25.0 %collective-permute-start.53 = (bf16[512,1024]{1,0:T(8,128)(2,1)S(1)}, bf16[512,1024]{1,0:T(8,128)(2,1)S(1)}, u32[]{:S(2)}, u32[]{:S(2)}) collective-permute-start(bf16[512,1024]{1,0:T(8,128)(2,1)S(1)} %copy-done.112), channel_id=1, source_target_pairs={{0,4},{4,0},{8,12},{12,8},{16,20},{20,16},{24,28},{28,24},{1,5},{5... | collective-permute-start | bytes 3145736 | tf_op jit(solution)/shard_map/ppermute | solution.py:696
  501.6 10.0 collective-permute-start.55
  501.6 10.0 collective-permute-start.54
  977.8 42.6 %collective-permute-start.60 = (f32[256,512]{1,0:T(8,128)S(1)}, f32[256,512]{1,0:T(8,128)S(1)}, u32[]{:S(2)}, u32[]{:S(2)}) collective-permute-start(f32[256,512]{1,0:T(8,128)S(1)} %constant_dynamic-slice_fusion.1), channel_id=1, source_target_pairs={{0,2},{2,0},{1,3},{3,1},{4,6},{6,4},{5,7},{7,5},{8,10},{10,8},{9,1... | collective-permute-start | bytes 1572872 | tf_op jit(solution)/shard_map/ppermute | solution.py:693
  980.3 40.3 %collective-permute-start.61 = (f32[256,512]{1,0:T(8,128)S(1)}, f32[256,512]{1,0:T(8,128)S(1)}, u32[]{:S(2)}, u32[]{:S(2)}) collective-permute-start(f32[256,512]{1,0:T(8,128)S(1)} %constant_dynamic-slice_fusion), channel_id=1, source_target_pairs={{0,2},{2,0},{1,3},{3,1},{4,6},{6,4},{5,7},{7,5},{8,10},{10,8},{9,1... | collective-permute-start | bytes 1572872 | tf_op jit(solution)/shard_map/ppermute | solution.py:693
  (131 other events, 2201.5 us)

commit v4 on v3

--- a/solution.py
+++ b/solution.py
@@ -365,9 +365,11 @@
 
 
 def attention_back_kernel(
-    g_ref, out_own, out_got, cos_ref, sin_ref, col_ref, row_ref, lse_ref, q_ref, k_ref, v_ref, *refs
+    own_rows, other_rows, out_own, out_got, cos_ref, sin_ref, col_ref, row_ref,
+    lse_ref, q_ref, k_ref, v_ref, *refs
 ):
     span, wide = q_ref.shape
+    g_ref = jnp.concatenate([own_rows[...], other_rows[...]], axis=0)
     half = g_ref.shape[1] // 2
     factor = 1.0 / math.sqrt(HEAD)
     cosine, sine_table = cos_ref[...], -sin_ref[...]
@@ -447,12 +449,18 @@
 
 
 def feed_forward_kernel(
-    r_ref, x_ref, gate_own, gate_got, up_own, up_got, down_own, down_got,
-    gate_out, up_out, act_keep, act_give, kept, sent, total, *, side_steps,
+    r_ref, own_rows, other_rows, gate_own, gate_got, up_own, up_got, down_own, down_got,
+    gate_out, up_out, act_keep, act_give, kept, sent, total, x_ref, *, side_steps,
 ):
     step, last = pl.program_id(0), pl.num_programs(0) - 1
     half = x_ref.shape[1] // 2
     own = kept.shape[0]
+
+    @pl.when(step == 0)
+    def _():
+        x_ref[:own] = own_rows[...]
+        x_ref[own:] = other_rows[...]
+
     near, far = x_ref[:, :half], x_ref[:, half:]
     gate = dot(near, gate_own[...]) + dot(far, gate_got[...])
     up = dot(near, up_own[...]) + dot(far, up_got[...])
@@ -489,12 +497,19 @@
 
 
 def feed_forward_back_kernel(
-    r_ref, g_ref, gate_ref, up_ref, gate_own, gate_got, up_own, up_got, down_own, down_got,
-    gate_keep, gate_give, up_keep, up_give, kept, sent, total, *, side_steps,
+    r_ref, own_rows, other_rows, gate_ref, up_ref,
+    gate_own, gate_got, up_own, up_got, down_own, down_got,
+    gate_keep, gate_give, up_keep, up_give, kept, sent, total, g_ref, *, side_steps,
 ):
     step, last = pl.program_id(0), pl.num_programs(0) - 1
     half = g_ref.shape[1] // 2
     own = kept.shape[0]
+
+    @pl.when(step == 0)
+    def _():
+        g_ref[:own] = own_rows[...]
+        g_ref[own:] = other_rows[...]
+
     grad = contract_cols(g_ref[:, :half], down_own[...]) + contract_cols(
         g_ref[:, half:], down_got[...]
     )
@@ -535,8 +550,8 @@
 
 
 def feed_forward(back, where, operand, saved, weights, got, units, tile):
-    span, width = operand.shape
-    half, own, steps = width // 2, span // 2, units // tile
+    own, width = operand[0].shape
+    half, span, steps = width // 2, 2 * own, units // tile
     side_steps = steps // 2
     gate, up, down = weights
     gate_got, up_got, down_got = got
@@ -547,7 +562,7 @@
     def other(i, r):
         return (0, jnp.clip(i - (1 - r[1]) * side_steps, 0, side_steps - 1))
 
-    whole = pl.BlockSpec((span, width), lambda i, r: (0, 0))
+    whole = pl.BlockSpec((own, width), lambda i, r: (0, 0))
     wide = pl.BlockSpec((span, tile), lambda i, r: (0, i))
     into_own = pl.BlockSpec((half, tile), lambda i, r: (0, r[0] * steps + i))
     into_got = pl.BlockSpec((half, tile), lambda i, r: (0, i))
@@ -564,12 +579,12 @@
     ]
     if back:
         kernel = feed_forward_back_kernel
-        in_specs = [whole, wide, wide] + weight_specs
+        in_specs = [whole, whole, wide, wide] + weight_specs
         out_specs = [keep, give, keep, give] + ends
         out_shape = [part] * 4 + end_shapes
     else:
         kernel = feed_forward_kernel
-        in_specs = [whole] + weight_specs
+        in_specs = [whole, whole] + weight_specs
         out_specs = [wide, wide, keep, give] + ends
         out_shape = [full] * 2 + [part] * 2 + end_shapes
     return pl.pallas_call(
@@ -580,7 +595,7 @@
             grid=(steps,),
             in_specs=in_specs,
             out_specs=out_specs,
-            scratch_shapes=[pltpu.VMEM((span, width), F32)],
+            scratch_shapes=[pltpu.VMEM((span, width), F32), pltpu.VMEM((span, width), BF)],
         ),
         compiler_params=pltpu.CompilerParams(vmem_limit_bytes=52 * 2**20),
         cost_estimate=pl.CostEstimate(
@@ -589,7 +604,7 @@
             transcendentals=span * units,
         ),
         name="feed_forward_back" if back else "feed_forward",
-    )(where, operand, *saved, gate, gate_got, up, up_got, down, down_got)
+    )(where, *operand, *saved, gate, gate_got, up, up_got, down, down_got)
 
 
 def widen_three(sums, down_shape, into_shape, size):
@@ -708,7 +723,7 @@
         return lax.psum(sent, "col") - sent
 
     def both_cores(kept):
-        return jnp.concatenate([kept, swap(swap_halves(kept, 1))], axis=0)
+        return [kept, swap(swap_halves(kept, 1))]
 
     def from_cores(first, second):
         other = swap(swap_halves(jnp.concatenate([first, second], axis=0), 1))
@@ -729,6 +744,14 @@
     for j in range(2):
         piece = tokens[j * span : (j + 1) * span]
         blocks.append(gather_blocks(ordered(first_row, piece[:own], piece[own:], 0)))
+
+    targets = []
+    for j in range(2):
+        piece = teacher[j * span : (j + 1) * span]
+        piece = ordered(first_row, piece[:own], piece[own:], 0)
+        targets.append((piece[:own], swap(piece[own:])))
+    slices = [take(w, 1 - row, units, 1) for w in (gate_weight, up_weight)]
+    blocks[0], slices, targets = tie((blocks[0], slices, targets))
 
     def columns_of(core):
         return jnp.concatenate(
@@ -808,9 +831,7 @@
         saved.append((gate_out, up_out))
         acts.append(act_keep)
         act_gives.append(act_give)
-        piece = teacher[j * span : (j + 1) * span]
-        piece = ordered(first_row, piece[:own], piece[own:], 0)
-        near, far = piece[:own].astype(F32), swap(piece[own:]).astype(F32)
+        near, far = (t.astype(F32) for t in targets[j])
         minus = [jnp.where(col == b, near, 0.0) for b in range(cols)]
         minus += [jnp.where(col == b, far, 0.0) for b in range(cols)]
         part = kept + swap(sent).astype(F32) - jnp.concatenate(minus, axis=1)
@@ -861,7 +882,7 @@
             "attention_back",
             shapes,
             [
-                operand,
+                *operand,
                 out_own,
                 out_got,
                 *tables[j],
@@ -880,22 +901,22 @@
 
     part_a = joined(attention(0, first_norm(0, blocks[0])))
     operand = first_norm(1, blocks[1])
-    operand, part_a, low, token_total, core = tie(
-        (operand, part_a, part_a.astype(BF), token_total, 1 - row)
+    operand, part_a, low, token_total, core, slices = tie(
+        (operand, part_a, part_a.astype(BF), token_total, 1 - row, slices)
     )
     got_a = from_chips(low)
     token_total = hop(token_total, *token_hops[0])
     pair = attention(1, operand)
     received = (
-        swap(take(gate_weight, core, units, 1)),
-        swap(take(up_weight, core, units, 1)),
+        swap(slices[0]),
+        swap(slices[1]),
         swap(take(down_weight, core, units, 0)),
     )
     pair, got_a, token_total, received = tie((pair, got_a, token_total, received))
     part_b = joined(pair)
     two_a = second_norm(0, part_a, got_a)
     two_a, part_b, low, mine, token_total = tie(
-        (two_a, part_b, part_b.astype(BF), two_a[:own], token_total)
+        (two_a, part_b, part_b.astype(BF), two_a[0], token_total)
     )
     token_total = hop(token_total, *token_hops[1])
     got_b, cross_two_a = from_chips(low), cross(mine)
@@ -904,7 +925,7 @@
     part_a, targets_a = after_forward(0, raw)
     two_b = second_norm(1, part_b, got_b)
     two_b, part_a, low, mine, token_total = tie(
-        (two_b, part_a, part_a.astype(BF), two_b[:own], token_total)
+        (two_b, part_a, part_a.astype(BF), two_b[0], token_total)
     )
     for step in token_hops[2:]:
         token_total = hop(token_total, *step)
@@ -935,13 +956,13 @@
     raw, got_a, cross_act_b, error_sum = tie((raw, got_a, cross_act_b, error_sum))
     ups_b, part_b = raw[:4], joined(raw[4:])
     hidden_a = second_norm_back(0, part_a, got_a)
-    hidden_a, part_b, low, mine = tie((hidden_a, part_b, part_b.astype(BF), low_a[:own]))
+    hidden_a, part_b, low, mine = tie((hidden_a, part_b, part_b.astype(BF), low_a[0]))
     error_sum = hop(error_sum, *hops[1])
     got_b, cross_low_a = from_chips(low), cross(mine)
     parts = attention_back(0, hidden_a, [])
     parts, got_b, cross_low_a, error_sum = tie((parts, got_b, cross_low_a, error_sum))
     hidden_b = second_norm_back(1, part_b, got_b)
-    hidden_b, parts, mine, error_sum = tie((hidden_b, parts, low_b[:own], error_sum))
+    hidden_b, parts, mine, error_sum = tie((hidden_b, parts, low_b[0], error_sum))
     error_sum = hop(error_sum, *hops[2])
     cross_low_b = cross(mine)
     first_back, back_b = attention_back(
@@ -968,7 +989,7 @@
     def product(lefts, rights):
         return contract_rows(lefts, rights).astype(BF)
 
-    hiddens = together(attended, [hidden_a, hidden_b])
+    hiddens = together(attended, [*hidden_a, *hidden_b])
     firsts = together(low_first, backs)
     backs, mine, gate_gives = tie((backs, gate_gives[0], gate_gives))
     cross_gate_a = cross(mine)
@@ -979,7 +1000,7 @@
     raw, cross_gate_a, error_sum = tie((raw, cross_gate_a, error_sum))
     last_parts = [joined(raw[:2]), joined(raw[2:])]
     downs = together(
-        [*acts, cross_act_a, cross_act_b], [low_a, low_b, *from_cores(cross_low_a, cross_low_b)]
+        [*acts, cross_act_a, cross_act_b], [*low_a, *low_b, *from_cores(cross_low_a, cross_low_b)]
     )
     downs, mine = tie((downs, gate_gives[1]))
     cross_gate_b = cross(mine)
@@ -991,7 +1012,7 @@
     grad_qkv, cross_up_a, up_gives, hiddens = tie((grad_qkv, cross_up_a, up_gives, hiddens))
     qkv_pair = split_rows(grad_qkv)
     out_pair = split_cols(product(*hiddens))
-    twos = [two_a, two_b, *from_cores(cross_two_a, cross_two_b)]
+    twos = [*two_a, *two_b, *from_cores(cross_two_a, cross_two_b)]
     gates = together(twos, [ups_a[0], ups_b[0], cross_gate_a, cross_gate_b])
     gates, mine, qkv_pair, out_pair = tie((gates, up_gives[1], qkv_pair, out_pair))
     cross_up_b = cross(mine)

time: 1030 us -> 1010 us (0.981)
  other arithmetic: 109 us -> 90.6 us
  local copies, waits for them, and re-layouts: 73.3 us -> 88.2 us
  waiting for transfers between devices: 79.7 us -> 66.4 us
    concatenate x6 -> x0, other arithmetic: 17.3 us -> none  [both_cores(): return jnp.concatenate([kept, swap(swap_halves(kept, 1))], axis=0)]
    ppermute x2, waiting for transfers between devices: 11.5 us -> 0.01 us  [gather_blocks(): got = lax.ppermute(operand, 'col', [(0, 1), (1, 0)])]
    unnamed x245 -> x294, local copies, waits for them, and re-layouts: 39 us -> 45.9 us
  transfers between devices with their start and end apart: 62 -> 62, of which waited for: 12 -> 9; matrix products, arithmetic and copies ran while one was open for 15% -> 17% of each run, Pallas kernels for 63% -> 64%
where the time goes in v4:
time: 1010 us
  Pallas kernels  660 us (65%)
  other arithmetic  90.6 us (9%)
  local copies, waits for them, and re-layouts  88.2 us (9%)
  waiting for transfers between devices  66.4 us (7%)
  matrix products  46.5 us (5%)
  starting transfers between devices  45.6 us (5%)
  between operations  11.6 us (1%)
    pallas_call x1, Pallas kernels, line_sum(): pl.pallas_call(functools.partial(line_kernel, sizes, spots, len(gives), c...  455 us
    pallas_call x4, Pallas kernels, feed_forward(): pl.pallas_call(functools.partial(kernel, side_steps=side_steps), out_shap...  101 us
    pallas_call x5, Pallas kernels, in_vmem(): pl.pallas_call(kernel, out_shape=out_shape, in_specs=[pl.BlockSpec(memory...  65.3 us
    ppermute x10, waiting for transfers between devices, cross(): return lax.ppermute(operand, 'dp', sides)  50.1 us
    dot_general x5, matrix products, contract_rows(): lax.dot_general(left, right, (((0,), (0,)), ((), ())), preferred_element_...  46.5 us
    unnamed x294, local copies, waits for them, and re-layouts  45.9 us
    pallas_call x1, Pallas kernels, widen_three(): pl.pallas_call(kernel, out_shape=[jax.ShapeDtypeStruct(x, F32) for x in (...  27.5 us
    dynamic_slice x10, local copies, waits for them, and re-layouts, take(): return lax.dynamic_slice_in_dim(operand, index * size, size, axis)  24.3 us
  transfers between devices with their start and end apart: 62, of which 9 were waited for; matrix products, arithmetic and copies ran while one was open for 17% of the time, Pallas kernels for 64%

profile of v4, /device:TPU:0, one launch (start us, length us, event | category | flops | bytes accessed | tf_op | source)
XLA Modules:
  0.0 1009.2 jit_solution(9977305575311869770)
XLA Ops:
  2.9 3.0 collective-permute-start
  8.1 3.1 constant_dynamic-slice_fusion.7
  11.9 2.8 fusion.56
  14.9 2.7 constant_dynamic-slice_fusion.11
  17.6 4.8 constant_dynamic-slice_fusion.16
  22.4 4.9 constant_dynamic-slice_fusion.15
  37.2 3.4 pad_maximum_fusion.3.own_ref
  47.0 12.7 %attention.2 = (bf16[512,512]{1,0:T(8,128)(2,1)S(1)}, bf16[512,512]{1,0:T(8,128)(2,1)S(1)}, bf16[512,512]{1,0:T(8,128)(2,1)}, bf16[512,512]{1,0:T(8,128)(2,1)}, ...) custom-call(bf16[512,2048]{1,0:T(8,128)(2,1)} %fusion.5.x_ref, ...), custom_call_target="tpu_custom_call" | custom-call | flops 8000000000 | bytes 20000000 | tf_op jit(solution)/shard_map/attention/pallas_call | solution.py:425
  62.6 2.2 fusion.74
  64.7 4.7 constant_dynamic-slice_fusion.6
  70.4 2.1 collective-permute-start.9
  74.5 15.9 %attention.3 = (bf16[512,512]{1,0:T(8,128)(2,1)S(1)}, bf16[512,512]{1,0:T(8,128)(2,1)S(1)}, bf16[512,512]{1,0:T(8,128)(2,1)}, bf16[512,512]{1,0:T(8,128)(2,1)}, ...) custom-call(bf16[512,2048]{1,0:T(8,128)(2,1)} %fusion.7.x_ref, ...), custom_call_target="tpu_custom_call" | custom-call | flops 8000000000 | bytes 20000000 | tf_op jit(solution)/shard_map/attention/pallas_call | solution.py:425
  91.7 4.6 collective-permute-done.9
  99.7 2.4 convert_select_fusion.5
  102.1 2.4 convert_select_fusion.1
  109.3 3.1 collective-permute-start.18
  115.4 24.5 %feed_forward.2 = (f32[512,2048]{1,0:T(8,128)}, f32[512,2048]{1,0:T(8,128)}, bf16[512,1024]{1,0:T(8,128)(2,1)S(1)}, bf16[512,1024]{1,0:T(8,128)(2,1)}, f32[256,2048]{1,0:T(8,128)}, /*index=5*/bf16[256,2048]{1,0:T(8,128)(2,1)}) custom-call(s32[2]{0:T(128)S(1)} %pad_add_fusion.10.r_ref, bf16[256,2048]{1,0:T(8,128)(2,1)} %copy-done.39, ...), custom_call_target="tpu_custom_call" | custom-call | flops 12884901888 | bytes 37748736 | tf_op jit(solution)/shard_map/feed_forward/pallas_call | solution.py:590
  150.9 3.9 collective-permute-start.23
  155.9 24.1 %feed_forward.3 = (f32[512,2048]{1,0:T(8,128)}, f32[512,2048]{1,0:T(8,128)}, bf16[512,1024]{1,0:T(8,128)(2,1)S(1)}, bf16[512,1024]{1,0:T(8,128)(2,1)}, f32[256,2048]{1,0:T(8,128)}, /*index=5*/bf16[256,2048]{1,0:T(8,128)(2,1)}) custom-call(s32[2]{0:T(128)S(1)} %pad_add_fusion.10.r_ref, bf16[256,2048]{1,0:T(8,128)(2,1)} %copy-done.37, ...), custom_call_target="tpu_custom_call" | custom-call | flops 12884901888 | bytes 37748736 | tf_op jit(solution)/shard_map/feed_forward/pallas_call | solution.py:590
  185.7 2.9 multiply_reduce_fusion.5
  192.3 26.3 %feed_forward_back.2 = (bf16[512,1024]{1,0:T(8,128)(2,1)S(1)}, bf16[512,1024]{1,0:T(8,128)(2,1)}, bf16[512,1024]{1,0:T(8,128)(2,1)}, bf16[512,1024]{1,0:T(8,128)...) custom-call(s32[2]{0:T(128)S(1)} %pad_add_fusion.10.r_ref, bf16[256,2048]{1,0:T(8,128)(2,1)} %copy-done.32, ...), custom_call_target="tpu_custom_call" | custom-call | flops 12884901888 | bytes 37748736 | tf_op jit(solution)/shard_map/feed_forward_back/pallas_call | solution.py:590
  223.6 2.4 multiply_reduce_fusion.4
  227.3 2.3 fusion.66
  233.5 26.3 %feed_forward_back.3 = (bf16[512,1024]{1,0:T(8,128)(2,1)S(1)}, bf16[512,1024]{1,0:T(8,128)(2,1)}, bf16[512,1024]{1,0:T(8,128)(2,1)}, bf16[512,1024]{1,0:T(8,128)...) custom-call(s32[2]{0:T(128)S(1)} %pad_add_fusion.10.r_ref, bf16[256,2048]{1,0:T(8,128)(2,1)} %copy-done.35, ...), custom_call_target="tpu_custom_call" | custom-call | flops 12884901888 | bytes 37748736 | tf_op jit(solution)/shard_map/feed_forward_back/pallas_call | solution.py:590
  263.4 3.5 fusion.65
  279.9 9.7 attention_back.2
  289.6 7.9 collective-permute-done.37
  300.6 3.5 fusion.63
  316.4 15.0 %attention_back.3 = (bf16[512,1024]{1,0:T(8,128)(2,1)}, bf16[512,1536]{1,0:T(8,128)(2,1)}) custom-call(bf16[256,2048]{1,0:T(8,128)(2,1)} %copy-done.43, bf16[256,2048]{1,0:T(8,128)(2,1)} %copy-done.115, bf16[512,1024]{1,0:T(8,128)(2,1)} %get-tuple-element.479.out_own, bf16[512,1024]{1,0:T(8,128)(2,1)} %collective-permute-done.7.out_got, ...), custom_call_target="tpu_custom_call" | custom-call | flops 8000000000 | bytes 20000000 | tf_op jit(solution)/shard_map/attention_back/pallas_call | solution.py:425
  332.1 3.1 collective-permute-done.41
  339.6 2.5 slice_dynamic-update-slice_fusion.1
  350.5 11.1 %convolution_convert_fusion.1 = bf16[1024,2048]{1,0:T(8,128)(2,1)} fusion(bf16[2048,1024]{1,0:T(8,128)(2,1)S(1)} %pad_maximum_fusion, bf16[2048,2048]{1,0:T(8,128)(2,1)S(1)} %slice_dynamic-update-slice_fusion.2), kind=kOutput, calls=%fused_computation.28 | convolution fusion | flops 8592031744 | bytes 16777216 | tf_op jit(solution)/shard_map/dot_general | solution.py:40
  361.5 33.8 %collective-permute-done.47 = bf16[512,1024]{1,0:T(8,128)(2,1)} collective-permute-done((bf16[512,1024]{1,0:T(8,128)(2,1)S(1)}, bf16[512,1024]{1,0:T(8,128)(2,1)}, u32[]{:S(2)}, u32[]{:S(2)}) %collective-permute-start.47) | collective-permute-done | bytes 1048608 | tf_op jit(solution)/shard_map/ppermute | solution.py:711
  395.9 9.0 convolution_convert_fusion
  405.8 12.0 %first_norm_back.1 = (f32[256,2048]{1,0:T(8,128)}, bf16[256,2048]{1,0:T(8,128)(2,1)S(1)}, f32[256,2048]{1,0:T(8,128)}, bf16[256,2048]{1,0:T(8,128)(2,1)}) custom-call(bf16[512,1536]{1,0:T(8,128)(2,1)} %copy-done.120, bf16[512,1536]{1,0:T(8,128)(2,1)} %get-tuple-element.329.b_ref, bf16[1024,1536]{1,0:T(8,128)(2,1)} %pad_maximum_fusion.3.own_ref, ...), custom_call_target="tpu_custom_call" | custom-call | flops 8000000000 | bytes 20000000 | tf_op jit(solution)/shard_map/first_norm_back/pallas_call | solution.py:425
  422.9 3.5 fusion.75
  426.8 2.5 slice_dynamic-update-slice_fusion
  431.5 2.0 fusion.62
  434.0 2.4 convolution_convert_fusion.3
  438.1 2.0 fusion.61
  446.8 11.8 %convolution_convert_fusion.2 = bf16[2048,1024]{1,0:T(8,128)(2,1)S(1)} fusion(bf16[2048,2048]{1,0:T(8,128)(2,1)} %slice_dynamic-update-slice_fusion, bf16[2048,1024]{1,0:T(8,128)(2,1)S(1)} %pad_maximum_fusion.1), kind=kOutput, calls=%fused_computation.29 | convolution fusion | flops 8592031744 | bytes 16777216 | tf_op jit(solution)/shard_map/dot_general | solution.py:40
  458.7 12.1 %collective-permute-done.53 = bf16[512,1024]{1,0:T(8,128)(2,1)S(1)} collective-permute-done((bf16[512,1024]{1,0:T(8,128)(2,1)S(1)}, bf16[512,1024]{1,0:T(8,128)(2,1)S(1)}, u32[]{:S(2)}, u32[]{:S(2)}) %collective-permute-start.53) | collective-permute-done | bytes 1048608 | tf_op jit(solution)/shard_map/ppermute | solution.py:711
  473.6 12.1 %fusion.19 = bf16[2048,1024]{1,0:T(8,128)(2,1)S(1)} fusion(bf16[2048,2048]{1,0:T(8,128)(2,1)} %slice_dynamic-update-slice_fusion, bf16[512,1024]{1,0:T(8,128)(2,1)} %copy-done.135, bf16[512,1024]{1,0:T(8,128)(2,1)} %collective-permute-done.50, bf16[512,1024]{1,0:T(8,128)(2,1)S(1)} %copy-done.129, bf16[512,1024]{1,0:T(8,128)(2,1)S(1)} %copy-done.128), kind=kOutput, calls=%fused_computation.27 | convolution fusion | flops 8608808960 | bytes 16777216 | tf_op jit(solution)/shard_map/dot_general | solution.py:40
  500.1 455.4 %line_sum.1.qk_a.qk_b.v_a.v_b.o_ref.in_ref = bf16[2,8192,1024]{2,1,0:T(8,128)(2,1)} custom-call(bf16[1024,1024]{1,0:T(8,128)(2,1)} %get-tuple-element.445.refs_0_, bf16[1024,1024]{1,0:T(8,128)(2,1)} %copy-done.86, bf16[1024,1024]{1,0:T(8,128)(2,1)} %get-tuple-element.443.refs_2_, bf16[1024,1024]{1,0:T(8,128)(2,1)} %copy-done.88, ...), custom_call_target="tpu_custom_call" | custom-call | tf_op jit(solution)/shard_map/line_sum/pallas_call | solution.py:270
  955.6 2.1 fusion.46
  957.7 2.1 fusion.31
  967.5 10.7 %widen_four.1 = (f32[1024,1024]{1,0:T(8,128)}, f32[1024,1024]{1,0:T(8,128)}, f32[1024,1024]{1,0:T(8,128)}, f32[1024,1024]{1,0:T(8,128)}) custom-call(bf16[2,8192,1024]{2,1,0:T(8,128)(2,1)} %line_sum.1.qk_a.qk_b.v_a.v_b.o_ref.in_ref, bf16[2,8192,1024]{2,1,0:T(8,128)(2,1)} %line_sum.1.qk_a.qk_b.v_a.v_b.o_ref.in_ref, ...), custom_call_target="tpu_custom_call" | custom-call | tf_op jit(solution)/shard_map/widen_four/pallas_call | solution.py:658
  978.2 27.5 %widen_three.1 = (f32[4096,1024]{1,0:T(8,128)}, f32[1024,4096]{1,0:T(8,128)}, f32[1024,4096]{1,0:T(8,128)}) custom-call(bf16[2,8192,1024]{2,1,0:T(8,128)(2,1)} %line_sum.1.qk_a.qk_b.v_a.v_b.o_ref.in_ref), custom_call_target="tpu_custom_call" | custom-call | tf_op jit(solution)/shard_map/widen_three/pallas_call | solution.py:623
  (543 shorter events, 152.6 us)
Async XLA Ops:
  2.9 28.2 %collective-permute-start = (bf16[512,512]{1,0:T(8,128)(2,1)}, bf16[512,512]{1,0:T(8,128)(2,1)}, u32[]{:S(2)}, u32[]{:S(2)}) collective-permute-start(bf16[512,512]{1,0:T(8,128)(2,1)} %pad_maximum_fusion.24), channel_id=1, source_target_pairs={{0,1},{1,0},{2,3},{3,2},{4,5},{5,4},{6,7},{7,6},{8,9},{9,8},{10,11... | collective-permute-start | bytes 1572872 | tf_op jit(solution)/shard_map/ppermute | solution.py:715
  6.7 27.5 %collective-permute-start.4 = (bf16[512,512]{1,0:T(8,128)(2,1)}, bf16[512,512]{1,0:T(8,128)(2,1)}, u32[]{:S(2)}, u32[]{:S(2)}) collective-permute-start(bf16[512,512]{1,0:T(8,128)(2,1)} %pad_maximum_fusion.25), channel_id=1, source_target_pairs={{0,1},{1,0},{2,3},{3,2},{4,5},{5,4},{6,7},{7,6},{8,9},{9,8},{10,11... | collective-permute-start | bytes 1572872 | tf_op jit(solution)/shard_map/ppermute | solution.py:715
  7.6 25.4 %collective-permute-start.2 = (bf16[256,512]{1,0:T(8,128)(2,1)}, bf16[256,512]{1,0:T(8,128)(2,1)}, u32[]{:S(2)}, u32[]{:S(2)}) collective-permute-start(bf16[256,512]{1,0:T(8,128)(2,1)} %get-tuple-element.522), channel_id=1, source_target_pairs={{0,2},{2,0},{1,3},{3,1},{4,6},{6,4},{5,7},{7,5},{8,10},{10,8},{9,1... | collective-permute-start | bytes 786440 | tf_op jit(solution)/shard_map/ppermute | solution.py:708
  7.6 25.3 %collective-permute-start.1 = (bf16[256,512]{1,0:T(8,128)(2,1)}, bf16[256,512]{1,0:T(8,128)(2,1)}, u32[]{:S(2)}, u32[]{:S(2)}) collective-permute-start(bf16[256,512]{1,0:T(8,128)(2,1)} %get-tuple-element.524), channel_id=1, source_target_pairs={{0,2},{2,0},{1,3},{3,1},{4,6},{6,4},{5,7},{7,5},{8,10},{10,8},{9,1... | collective-permute-start | bytes 786440 | tf_op jit(solution)/shard_map/ppermute | solution.py:708
  11.2 35.8 %collective-permute-start.7 = (bf16[512,1024]{1,0:T(8,128)(2,1)}, bf16[512,1024]{1,0:T(8,128)(2,1)}, u32[]{:S(2)}, u32[]{:S(2)}) collective-permute-start(bf16[512,1024]{1,0:T(8,128)(2,1)} %get-tuple-element.478), channel_id=1, source_target_pairs={{0,2},{2,0},{1,3},{3,1},{4,6},{6,4},{5,7},{7,5},{8,10},{10,8},{9,1... | collective-permute-start | bytes 3145736 | tf_op jit(solution)/shard_map/ppermute | solution.py:708
  31.1 15.9 %collective-permute-start.6 = (bf16[1024,1536]{1,0:T(8,128)(2,1)}, bf16[1024,1536]{1,0:T(8,128)(2,1)}, u32[]{:S(2)}, u32[]{:S(2)}) collective-permute-start(bf16[1024,1536]{1,0:T(8,128)(2,1)} %pad_maximum_fusion.4), channel_id=1, source_target_pairs={{0,2},{2,0},{1,3},{3,1},{4,6},{6,4},{5,7},{7,5},{8,10},{10,8},{9,1... | collective-permute-start | bytes 9437192 | tf_op jit(solution)/shard_map/ppermute | solution.py:708
  69.5 26.9 %collective-permute-start.13 = (bf16[2048,1024]{1,0:T(8,128)(2,1)}, bf16[2048,1024]{1,0:T(8,128)(2,1)}, u32[]{:S(2)}, u32[]{:S(2)}) collective-permute-start(bf16[2048,1024]{1,0:T(8,128)(2,1)} %constant_dynamic-slice_fusion.6), channel_id=1, source_target_pairs={{0,2},{2,0},{1,3},{3,1},{4,6},{6,4},{5,7},{7,5},{8,10},{10,8},{9,1... | collective-permute-start | bytes 12582920 | tf_op jit(solution)/shard_map/ppermute | solution.py:708
  69.7 26.6 %collective-permute-start.11 = (bf16[1024,2048]{1,0:T(8,128)(2,1)}, bf16[1024,2048]{1,0:T(8,128)(2,1)}, u32[]{:S(2)}, u32[]{:S(2)}) collective-permute-start(bf16[1024,2048]{1,0:T(8,128)(2,1)} %constant_dynamic-slice_fusion.16), channel_id=1, source_target_pairs={{0,2},{2,0},{1,3},{3,1},{4,6},{6,4},{5,7},{7,5},{8,10},{10,8},{9,1... | collective-permute-start | bytes 12582920 | tf_op jit(solution)/shard_map/ppermute | solution.py:708
  70.0 26.4 %collective-permute-start.12 = (bf16[1024,2048]{1,0:T(8,128)(2,1)}, bf16[1024,2048]{1,0:T(8,128)(2,1)}, u32[]{:S(2)}, u32[]{:S(2)}) collective-permute-start(bf16[1024,2048]{1,0:T(8,128)(2,1)} %constant_dynamic-slice_fusion.15), channel_id=1, source_target_pairs={{0,2},{2,0},{1,3},{3,1},{4,6},{6,4},{5,7},{7,5},{8,10},{10,8},{9,1... | collective-permute-start | bytes 12582920 | tf_op jit(solution)/shard_map/ppermute | solution.py:708
  70.4 25.9 %collective-permute-start.9 = (bf16[256,2048]{1,0:T(8,128)(2,1)}, bf16[256,2048]{1,0:T(8,128)(2,1)S(1)}, u32[]{:S(2)}, u32[]{:S(2)}) collective-permute-start(bf16[256,2048]{1,0:T(8,128)(2,1)} %get-tuple-element.212), channel_id=1, source_target_pairs={{0,1},{1,0},{2,3},{3,2},{4,5},{5,4},{6,7},{7,6},{8,9},{9,8},{10,11... | collective-permute-start | bytes 3145736 | tf_op jit(solution)/shard_map/ppermute | solution.py:721
  72.9 17.4 %collective-permute-start.10 = (f32[1,1]{1,0:T(1,128)}, f32[1,1]{1,0:T(1,128)}, u32[]{:S(2)}, u32[]{:S(2)}) collective-permute-start(f32[1,1]{1,0:T(1,128)} %bitcast.4), channel_id=1, source_target_pairs={{0,4},{4,0},{8,12},{12,8},{16,20},{20,16},{24,28},{28,24},{1,5},{5... | collective-permute-start | bytes 20 | tf_op jit(solution)/shard_map/ppermute | solution.py:316
  98.9 8.9 collective-permute-start.15
  99.1 10.2 %collective-permute-start.14 = (bf16[256,2048]{1,0:T(8,128)(2,1)S(1)}, bf16[256,2048]{1,0:T(8,128)(2,1)S(1)}, u32[]{:S(2)}, u32[]{:S(2)}) collective-permute-start(bf16[256,2048]{1,0:T(8,128)(2,1)S(1)} %pad_maximum_fusion.16), channel_id=1, source_target_pairs={{0,2},{2,0},{1,3},{3,1},{4,6},{6,4},{5,7},{7,5},{8,10},{10,8},{9,1... | collective-permute-start | bytes 3145736 | tf_op jit(solution)/shard_map/ppermute | solution.py:708
  109.3 30.7 %collective-permute-start.18 = (f32[1,1]{1,0:T(1,128)}, f32[1,1]{1,0:T(1,128)}, u32[]{:S(2)}, u32[]{:S(2)}) collective-permute-start(f32[1,1]{1,0:T(1,128)} %add.219), channel_id=1, source_target_pairs={{0,8},{4,12},{8,0},{12,4},{16,24},{20,28},{24,16},{28,20},{1,9},{5... | collective-permute-start | bytes 20 | tf_op jit(solution)/shard_map/ppermute | solution.py:316
  112.4 28.3 %collective-permute-start.16 = (bf16[256,2048]{1,0:T(8,128)(2,1)}, bf16[256,2048]{1,0:T(8,128)(2,1)S(1)}, u32[]{:S(2)}, u32[]{:S(2)}) collective-permute-start(bf16[256,2048]{1,0:T(8,128)(2,1)} %get-tuple-element.233), channel_id=1, source_target_pairs={{0,1},{1,0},{2,3},{3,2},{4,5},{5,4},{6,7},{7,6},{8,9},{9,8},{10,11... | collective-permute-start | bytes 3145736 | tf_op jit(solution)/shard_map/ppermute | solution.py:721
  113.9 26.8 %collective-permute-start.17 = (bf16[256,2048]{1,0:T(8,128)(2,1)S(1)}, bf16[256,2048]{1,0:T(8,128)(2,1)S(1)}, u32[]{:S(2)}, u32[]{:S(2)}) collective-permute-start(bf16[256,2048]{1,0:T(8,128)(2,1)S(1)} %fusion.39.own_rows), channel_id=1, source_target_pairs={{0,4},{4,0},{8,12},{12,8},{16,20},{20,16},{24,28},{28,24},{1,5},{5... | collective-permute-start | bytes 3145736 | tf_op jit(solution)/shard_map/ppermute | solution.py:711
  150.9 29.1 %collective-permute-start.23 = (f32[1,1]{1,0:T(1,128)}, f32[1,1]{1,0:T(1,128)}, u32[]{:S(2)}, u32[]{:S(2)}) collective-permute-start(f32[1,1]{1,0:T(1,128)} %add.226), channel_id=1, source_target_pairs={{0,16},{4,20},{8,24},{12,28},{16,0},{20,4},{24,8},{28,12},{1,17},{... | collective-permute-start | bytes 20 | tf_op jit(solution)/shard_map/ppermute | solution.py:316
  154.8 25.8 %collective-permute-start.21 = (bf16[256,2048]{1,0:T(8,128)(2,1)}, bf16[256,2048]{1,0:T(8,128)(2,1)S(1)}, u32[]{:S(2)}, u32[]{:S(2)}) collective-permute-start(bf16[256,2048]{1,0:T(8,128)(2,1)} %get-tuple-element.251), channel_id=1, source_target_pairs={{0,1},{1,0},{2,3},{3,2},{4,5},{5,4},{6,7},{7,6},{8,9},{9,8},{10,11... | collective-permute-start | bytes 3145736 | tf_op jit(solution)/shard_map/ppermute | solution.py:721
  155.3 25.3 %collective-permute-start.22 = (bf16[256,2048]{1,0:T(8,128)(2,1)S(1)}, bf16[256,2048]{1,0:T(8,128)(2,1)S(1)}, u32[]{:S(2)}, u32[]{:S(2)}) collective-permute-start(bf16[256,2048]{1,0:T(8,128)(2,1)S(1)} %fusion.40.own_rows), channel_id=1, source_target_pairs={{0,4},{4,0},{8,12},{12,8},{16,20},{20,16},{24,28},{28,24},{1,5},{5... | collective-permute-start | bytes 3145736 | tf_op jit(solution)/shard_map/ppermute | solution.py:711
  189.2 29.4 %collective-permute-start.27 = (bf16[256,2048]{1,0:T(8,128)(2,1)S(1)}, bf16[256,2048]{1,0:T(8,128)(2,1)S(1)}, u32[]{:S(2)}, u32[]{:S(2)}) collective-permute-start(bf16[256,2048]{1,0:T(8,128)(2,1)S(1)} %get-tuple-element.272), channel_id=1, source_target_pairs={{0,1},{1,0},{2,3},{3,2},{4,5},{5,4},{6,7},{7,6},{8,9},{9,8},{10,11... | collective-permute-start | bytes 3145736 | tf_op jit(solution)/shard_map/ppermute | solution.py:721
  190.8 27.8 %collective-permute-start.28 = (bf16[512,1024]{1,0:T(8,128)(2,1)}, bf16[512,1024]{1,0:T(8,128)(2,1)S(1)}, u32[]{:S(2)}, u32[]{:S(2)}) collective-permute-start(bf16[512,1024]{1,0:T(8,128)(2,1)} %get-tuple-element.273), channel_id=1, source_target_pairs={{0,4},{4,0},{8,12},{12,8},{16,20},{20,16},{24,28},{28,24},{1,5},{5... | collective-permute-start | bytes 3145736 | tf_op jit(solution)/shard_map/ppermute | solution.py:711
  218.7 8.6 collective-permute-start.31
  229.6 30.2 %collective-permute-start.34 = (f32[1,1]{1,0:T(1,128)}, f32[1,1]{1,0:T(1,128)}, u32[]{:S(2)}, u32[]{:S(2)}) collective-permute-start(f32[1,1]{1,0:T(1,128)} %bitcast.12), channel_id=1, source_target_pairs={{0,4},{4,0},{8,12},{12,8},{16,20},{20,16},{24,28},{28,24},{1,5},{5... | collective-permute-start | bytes 20 | tf_op jit(solution)/shard_map/ppermute | solution.py:316
  231.5 28.9 %collective-permute-start.32 = (bf16[256,2048]{1,0:T(8,128)(2,1)S(1)}, bf16[256,2048]{1,0:T(8,128)(2,1)S(1)}, u32[]{:S(2)}, u32[]{:S(2)}) collective-permute-start(bf16[256,2048]{1,0:T(8,128)(2,1)S(1)} %get-tuple-element.289), channel_id=1, source_target_pairs={{0,1},{1,0},{2,3},{3,2},{4,5},{5,4},{6,7},{7,6},{8,9},{9,8},{10,11... | collective-permute-start | bytes 3145736 | tf_op jit(solution)/shard_map/ppermute | solution.py:721
  232.0 28.4 %collective-permute-start.33 = (bf16[512,1024]{1,0:T(8,128)(2,1)}, bf16[512,1024]{1,0:T(8,128)(2,1)S(1)}, u32[]{:S(2)}, u32[]{:S(2)}) collective-permute-start(bf16[512,1024]{1,0:T(8,128)(2,1)} %get-tuple-element.290), channel_id=1, source_target_pairs={{0,4},{4,0},{8,12},{12,8},{16,20},{20,16},{24,28},{28,24},{1,5},{5... | collective-permute-start | bytes 3145736 | tf_op jit(solution)/shard_map/ppermute | solution.py:711
  272.1 25.4 %collective-permute-start.37 = (bf16[256,2048]{1,0:T(8,128)(2,1)}, bf16[256,2048]{1,0:T(8,128)(2,1)}, u32[]{:S(2)}, u32[]{:S(2)}) collective-permute-start(bf16[256,2048]{1,0:T(8,128)(2,1)} %get-tuple-element.303), channel_id=1, source_target_pairs={{0,1},{1,0},{2,3},{3,2},{4,5},{5,4},{6,7},{7,6},{8,9},{9,8},{10,11... | collective-permute-start | bytes 3145736 | tf_op jit(solution)/shard_map/ppermute | solution.py:721
  273.7 24.8 %collective-permute-start.38 = (bf16[256,2048]{1,0:T(8,128)(2,1)S(1)}, bf16[256,2048]{1,0:T(8,128)(2,1)}, u32[]{:S(2)}, u32[]{:S(2)}) collective-permute-start(bf16[256,2048]{1,0:T(8,128)(2,1)S(1)} %copy-done.33), channel_id=1, source_target_pairs={{0,4},{4,0},{8,12},{12,8},{16,20},{20,16},{24,28},{28,24},{1,5},{5... | collective-permute-start | bytes 3145736 | tf_op jit(solution)/shard_map/ppermute | solution.py:711
  306.2 30.1 %collective-permute-start.24 = (bf16[256,512]{1,0:T(8,128)(2,1)S(1)}, bf16[256,512]{1,0:T(8,128)(2,1)S(1)}, u32[]{:S(2)}, u32[]{:S(2)}) collective-permute-start(bf16[256,512]{1,0:T(8,128)(2,1)S(1)} %copy-done.119), channel_id=1, source_target_pairs={{0,2},{2,0},{1,3},{3,1},{4,6},{6,4},{5,7},{7,5},{8,10},{10,8},{9,1... | collective-permute-start | bytes 786440 | tf_op jit(solution)/shard_map/ppermute | solution.py:708
  307.8 31.7 %collective-permute-start.49 = (bf16[512,2048]{1,0:T(8,128)(2,1)}, bf16[512,2048]{1,0:T(8,128)(2,1)}, u32[]{:S(2)}, u32[]{:S(2)}) collective-permute-start(bf16[512,2048]{1,0:T(8,128)(2,1)} %pad_maximum_fusion.7), channel_id=1, source_target_pairs={{0,2},{2,0},{1,3},{3,1},{4,6},{6,4},{5,7},{7,5},{8,10},{10,8},{9,1... | collective-permute-start | bytes 6291464 | tf_op jit(solution)/shard_map/ppermute | solution.py:708
  309.5 25.6 %collective-permute-start.41 = (bf16[256,2048]{1,0:T(8,128)(2,1)S(1)}, bf16[256,2048]{1,0:T(8,128)(2,1)S(1)}, u32[]{:S(2)}, u32[]{:S(2)}) collective-permute-start(bf16[256,2048]{1,0:T(8,128)(2,1)S(1)} %copy-done.36), channel_id=1, source_target_pairs={{0,4},{4,0},{8,12},{12,8},{16,20},{20,16},{24,28},{28,24},{1,5},{5... | collective-permute-start | bytes 3145736 | tf_op jit(solution)/shard_map/ppermute | solution.py:711
  313.0 18.4 %collective-permute-start.42 = (f32[1,1]{1,0:T(1,128)}, f32[1,1]{1,0:T(1,128)}, u32[]{:S(2)}, u32[]{:S(2)}) collective-permute-start(f32[1,1]{1,0:T(1,128)} %add.250), channel_id=1, source_target_pairs={{0,16},{4,20},{8,24},{12,28},{16,0},{20,4},{24,8},{28,12},{1,17},{... | collective-permute-start | bytes 20 | tf_op jit(solution)/shard_map/ppermute | solution.py:316
  336.3 11.3 %collective-permute-start.46 = (bf16[512,2048]{1,0:T(8,128)(2,1)S(1)}, bf16[512,2048]{1,0:T(8,128)(2,1)S(1)}, u32[]{:S(2)}, u32[]{:S(2)}) collective-permute-start(bf16[512,2048]{1,0:T(8,128)(2,1)S(1)} %pad_maximum_fusion.6), channel_id=1, source_target_pairs={{0,2},{2,0},{1,3},{3,1},{4,6},{6,4},{5,7},{7,5},{8,10},{10,8},{9,1... | collective-permute-start | bytes 6291464 | tf_op jit(solution)/shard_map/ppermute | solution.py:708
  339.6 89.7 %collective-permute-start.29 = (bf16[256,512]{1,0:T(8,128)(2,1)}, bf16[256,512]{1,0:T(8,128)(2,1)}, u32[]{:S(2)}, u32[]{:S(2)}) collective-permute-start(bf16[256,512]{1,0:T(8,128)(2,1)} %get-tuple-element.503), channel_id=1, source_target_pairs={{0,2},{2,0},{1,3},{3,1},{4,6},{6,4},{5,7},{7,5},{8,10},{10,8},{9,1... | collective-permute-start | bytes 786440 | tf_op jit(solution)/shard_map/ppermute | solution.py:708
  347.0 75.8 %collective-permute-start.43 = (bf16[512,1024]{1,0:T(8,128)(2,1)}, bf16[512,1024]{1,0:T(8,128)(2,1)S(1)}, u32[]{:S(2)}, u32[]{:S(2)}) collective-permute-start(bf16[512,1024]{1,0:T(8,128)(2,1)} %get-tuple-element.334), channel_id=1, source_target_pairs={{0,4},{4,0},{8,12},{12,8},{16,20},{20,16},{24,28},{28,24},{1,5},{5... | collective-permute-start | bytes 3145736 | tf_op jit(solution)/shard_map/ppermute | solution.py:711
  349.9 45.5 %collective-permute-start.47 = (bf16[512,1024]{1,0:T(8,128)(2,1)S(1)}, bf16[512,1024]{1,0:T(8,128)(2,1)}, u32[]{:S(2)}, u32[]{:S(2)}) collective-permute-start(bf16[512,1024]{1,0:T(8,128)(2,1)S(1)} %copy-done.131), channel_id=1, source_target_pairs={{0,4},{4,0},{8,12},{12,8},{16,20},{20,16},{24,28},{28,24},{1,5},{5... | collective-permute-start | bytes 3145736 | tf_op jit(solution)/shard_map/ppermute | solution.py:711
  395.4 27.5 %collective-permute-start.50 = (bf16[512,1024]{1,0:T(8,128)(2,1)}, bf16[512,1024]{1,0:T(8,128)(2,1)}, u32[]{:S(2)}, u32[]{:S(2)}) collective-permute-start(bf16[512,1024]{1,0:T(8,128)(2,1)} %get-tuple-element.356), channel_id=1, source_target_pairs={{0,4},{4,0},{8,12},{12,8},{16,20},{20,16},{24,28},{28,24},{1,5},{5... | collective-permute-start | bytes 3145736 | tf_op jit(solution)/shard_map/ppermute | solution.py:711
  405.0 12.9 %collective-permute-start.44 = (f32[1,1]{1,0:T(1,128)}, f32[1,1]{1,0:T(1,128)}, u32[]{:S(2)}, u32[]{:S(2)}) collective-permute-start(f32[1,1]{1,0:T(1,128)} %add.253), channel_id=1, source_target_pairs={{0,2},{2,0},{1,3},{3,1},{4,6},{6,4},{5,7},{7,5},{8,10},{10,8},{9,1... | collective-permute-start | bytes 20 | tf_op jit(solution)/shard_map/ppermute | solution.py:316
  422.8 8.6 collective-permute-start.56
  426.5 18.7 %collective-permute-start.51 = (bf16[1024,1536]{1,0:T(8,128)(2,1)S(1)}, bf16[1024,1536]{1,0:T(8,128)(2,1)S(1)}, u32[]{:S(2)}, u32[]{:S(2)}) collective-permute-start(bf16[1024,1536]{1,0:T(8,128)(2,1)S(1)} %get-tuple-element.438), channel_id=1, source_target_pairs={{0,2},{2,0},{1,3},{3,1},{4,6},{6,4},{5,7},{7,5},{8,10},{10,8},{9,1... | collective-permute-start | bytes 9437192 | tf_op jit(solution)/shard_map/ppermute | solution.py:708
  433.5 522.0 %collective-permute-start.58 = (bf16[256,2048]{1,0:T(8,128)(2,1)}, bf16[256,2048]{1,0:T(8,128)(2,1)}, u32[]{:S(2)}, u32[]{:S(2)}) collective-permute-start(bf16[256,2048]{1,0:T(8,128)(2,1)} %get-tuple-element.402), channel_id=1, source_target_pairs={{0,1},{1,0},{2,3},{3,2},{4,5},{5,4},{6,7},{7,6},{8,9},{9,8},{10,11... | collective-permute-start | bytes 3145736 | tf_op jit(solution)/shard_map/ppermute | solution.py:721
  436.7 8.5 collective-permute-start.52
  440.1 515.4 %collective-permute-start.59 = (bf16[256,2048]{1,0:T(8,128)(2,1)}, bf16[256,2048]{1,0:T(8,128)(2,1)S(1)}, u32[]{:S(2)}, u32[]{:S(2)}) collective-permute-start(bf16[256,2048]{1,0:T(8,128)(2,1)} %get-tuple-element.400), channel_id=1, source_target_pairs={{0,1},{1,0},{2,3},{3,2},{4,5},{5,4},{6,7},{7,6},{8,9},{9,8},{10,11... | collective-permute-start | bytes 3145736 | tf_op jit(solution)/shard_map/ppermute | solution.py:721
  443.5 53.9 %collective-permute-start.48 = (bf16[1024,1024]{1,0:T(8,128)(2,1)S(1)}, bf16[1024,1024]{1,0:T(8,128)(2,1)S(1)}, u32[]{:S(2)}, u32[]{:S(2)}) collective-permute-start(bf16[1024,1024]{1,0:T(8,128)(2,1)S(1)} %get-tuple-element.444), channel_id=1, source_target_pairs={{0,2},{2,0},{1,3},{3,1},{4,6},{6,4},{5,7},{7,5},{8,10},{10,8},{9,1... | collective-permute-start | bytes 6291464 | tf_op jit(solution)/shard_map/ppermute | solution.py:708
  445.3 25.6 %collective-permute-start.53 = (bf16[512,1024]{1,0:T(8,128)(2,1)S(1)}, bf16[512,1024]{1,0:T(8,128)(2,1)S(1)}, u32[]{:S(2)}, u32[]{:S(2)}) collective-permute-start(bf16[512,1024]{1,0:T(8,128)(2,1)S(1)} %copy-done.130), channel_id=1, source_target_pairs={{0,4},{4,0},{8,12},{12,8},{16,20},{20,16},{24,28},{28,24},{1,5},{5... | collective-permute-start | bytes 3145736 | tf_op jit(solution)/shard_map/ppermute | solution.py:711
  487.4 9.9 collective-permute-start.55
  487.4 9.9 collective-permute-start.54
  962.8 43.0 %collective-permute-start.60 = (f32[256,512]{1,0:T(8,128)S(1)}, f32[256,512]{1,0:T(8,128)S(1)}, u32[]{:S(2)}, u32[]{:S(2)}) collective-permute-start(f32[256,512]{1,0:T(8,128)S(1)} %constant_dynamic-slice_fusion.1), channel_id=1, source_target_pairs={{0,2},{2,0},{1,3},{3,1},{4,6},{6,4},{5,7},{7,5},{8,10},{10,8},{9,1... | collective-permute-start | bytes 1572872 | tf_op jit(solution)/shard_map/ppermute | solution.py:708
  964.8 41.2 %collective-permute-start.61 = (f32[256,512]{1,0:T(8,128)S(1)}, f32[256,512]{1,0:T(8,128)S(1)}, u32[]{:S(2)}, u32[]{:S(2)}) collective-permute-start(f32[256,512]{1,0:T(8,128)S(1)} %constant_dynamic-slice_fusion), channel_id=1, source_target_pairs={{0,2},{2,0},{1,3},{3,1},{4,6},{6,4},{5,7},{7,5},{8,10},{10,8},{9,1... | collective-permute-start | bytes 1572872 | tf_op jit(solution)/shard_map/ppermute | solution.py:708
  (153 other events, 3080.1 us)

commit v5 on v4

--- a/solution.py
+++ b/solution.py
@@ -421,7 +421,7 @@
         sent[:, half:] = near[own:].astype(BF)
 
 
-def in_vmem(kernel, name, out_shape, operands):
+def in_vmem(kernel, name, out_shape, operands, flops=8 * 10**9):
     return pl.pallas_call(
         kernel,
         out_shape=out_shape,
@@ -429,7 +429,7 @@
         out_specs=[pl.BlockSpec(memory_space=pltpu.VMEM)] * len(out_shape),
         compiler_params=pltpu.CompilerParams(vmem_limit_bytes=52 * 2**20),
         cost_estimate=pl.CostEstimate(
-            flops=8 * 10**9, bytes_accessed=2 * 10**7, transcendentals=2 * 10**6
+            flops=flops, bytes_accessed=flops // 400, transcendentals=flops // 4000
         ),
         name=name,
     )(*operands)
@@ -991,33 +991,43 @@
 
     hiddens = together(attended, [*hidden_a, *hidden_b])
     firsts = together(low_first, backs)
-    backs, mine, gate_gives = tie((backs, gate_gives[0], gate_gives))
-    cross_gate_a = cross(mine)
+    downs = together(
+        [*acts, cross_act_a, cross_act_b], [*low_a, *low_b, *from_cores(cross_low_a, cross_low_b)]
+    )
+    downs, gate_gives, error_sum = tie((downs, gate_gives, error_sum))
+    cross_gate_a, cross_gate_b = (cross(g) for g in gate_gives)
     for step in hops[3:]:
         error_sum = hop(error_sum, *step)
+    grad_down = product(*downs)
+    grad_down, backs = tie((grad_down, backs))
     ends = [jax.ShapeDtypeStruct((own, 2 * half_width), t) for t in (F32, BF)]
-    raw = in_vmem(last_kernel, "first_norm_back", ends * 2, [*backs, qkv_own, qkv_got])
-    raw, cross_gate_a, error_sum = tie((raw, cross_gate_a, error_sum))
+    raw = in_vmem(
+        last_kernel, "first_norm_back", ends * 2, [*backs, qkv_own, qkv_got], flops=4000
+    )
+    raw, grad_down, cross_gate_a, cross_gate_b, up_gives, error_sum = tie(
+        (raw, grad_down, cross_gate_a, cross_gate_b, up_gives, error_sum)
+    )
     last_parts = [joined(raw[:2]), joined(raw[2:])]
-    downs = together(
-        [*acts, cross_act_a, cross_act_b], [*low_a, *low_b, *from_cores(cross_low_a, cross_low_b)]
-    )
-    downs, mine = tie((downs, gate_gives[1]))
-    cross_gate_b = cross(mine)
-    grad_down = product(*downs)
-    grad_down, cross_gate_b, up_gives = tie((grad_down, cross_gate_b, up_gives))
     down_pair = split_cols(grad_down)
-    cross_up_a = cross(up_gives[0])
+    firsts, up_gives = tie((firsts, up_gives))
+    cross_up_a, cross_up_b = (cross(g) for g in up_gives)
     grad_qkv = product(*firsts)
-    grad_qkv, cross_up_a, up_gives, hiddens = tie((grad_qkv, cross_up_a, up_gives, hiddens))
+    grad_qkv, hiddens, twos = tie(
+        (
+            grad_qkv,
+            hiddens,
+            ([*two_a, *two_b], [cross_two_a, cross_two_b], [ups_a[0], ups_b[0]]),
+        )
+    )
     qkv_pair = split_rows(grad_qkv)
     out_pair = split_cols(product(*hiddens))
-    twos = [*two_a, *two_b, *from_cores(cross_two_a, cross_two_b)]
-    gates = together(twos, [ups_a[0], ups_b[0], cross_gate_a, cross_gate_b])
-    gates, mine, qkv_pair, out_pair = tie((gates, up_gives[1], qkv_pair, out_pair))
-    cross_up_b = cross(mine)
+    gates = [*twos[2], cross_gate_a, cross_gate_b]
+    twos = [*twos[0], *from_cores(*twos[1])]
+    gates = together(twos, gates)
+    gates, qkv_pair, out_pair, cross_up_a, cross_up_b = tie(
+        (gates, qkv_pair, out_pair, cross_up_a, cross_up_b)
+    )
     grad_gate = product(*gates)
-    grad_gate, cross_up_b = tie((grad_gate, cross_up_b))
     gate_pair = split_rows(grad_gate)
     up_pair = split_rows(
         product(*together(twos, [ups_a[2], ups_b[2], cross_up_a, cross_up_b]))

time: 1010 us -> 1010 us (level)
  waiting for transfers between devices: 66.4 us -> 51.4 us
    ppermute x10, waiting for transfers between devices: 50.1 us -> 37.7 us  [cross(): return lax.ppermute(operand, 'dp', sides)]
    unnamed x294 -> x296, local copies, waits for them, and re-layouts: 45.9 us -> 49.7 us
  transfers between devices with their start and end apart: 62 -> 62, of which waited for: 9 -> 11; matrix products, arithmetic and copies ran while one was open for 17% -> 16% of each run, Pallas kernels for 64% -> 65%
where the time goes in v5:
time: 1010 us; the launch traced here: 1000 us
  Pallas kernels  661 us (65%)
  other arithmetic  97.3 us (10%)
  local copies, waits for them, and re-layouts  89.4 us (9%)
  waiting for transfers between devices  51.4 us (5%)
  starting transfers between devices  44.8 us (4%)
  matrix products  44.5 us (4%)
  between operations  11.4 us (1%)
    pallas_call x1, Pallas kernels, line_sum(): pl.pallas_call(functools.partial(line_kernel, sizes, spots, len(gives), c...  455 us
    pallas_call x4, Pallas kernels, feed_forward(): pl.pallas_call(functools.partial(kernel, side_steps=side_steps), out_shap...  101 us
    pallas_call x5, Pallas kernels, in_vmem(): pl.pallas_call(kernel, out_shape=out_shape, in_specs=[pl.BlockSpec(memory...  65.8 us
    unnamed x296, local copies, waits for them, and re-layouts  49.7 us
    dot_general x5, matrix products, contract_rows(): lax.dot_general(left, right, (((0,), (0,)), ((), ())), preferred_element_...  44.5 us
    ppermute x10, waiting for transfers between devices, cross(): return lax.ppermute(operand, 'dp', sides)  37.7 us
    pallas_call x1, Pallas kernels, widen_three(): pl.pallas_call(kernel, out_shape=[jax.ShapeDtypeStruct(x, F32) for x in (...  27.5 us
    dynamic_slice x10, local copies, waits for them, and re-layouts, take(): return lax.dynamic_slice_in_dim(operand, index * size, size, axis)  22.3 us
  transfers between devices with their start and end apart: 62, of which 11 were waited for; matrix products, arithmetic and copies ran while one was open for 16% of the time, Pallas kernels for 65%

profile of v5, /device:TPU:0, one launch (start us, length us, event | category | flops | bytes accessed | tf_op | source)
XLA Modules:
  0.0 999.6 jit_solution(8002483351142229400)
XLA Ops:
  2.9 3.0 collective-permute-start
  10.4 2.8 fusion.50
  13.3 2.7 constant_dynamic-slice_fusion.11
  16.0 4.8 constant_dynamic-slice_fusion.16
  20.8 4.9 constant_dynamic-slice_fusion.15
  35.6 3.1 pad_maximum_fusion.4.own_ref
  45.1 12.7 %attention.2 = (bf16[512,512]{1,0:T(8,128)(2,1)S(1)}, bf16[512,512]{1,0:T(8,128)(2,1)S(1)}, bf16[512,512]{1,0:T(8,128)(2,1)}, bf16[512,512]{1,0:T(8,128)(2,1)}, ...) custom-call(bf16[512,2048]{1,0:T(8,128)(2,1)} %fusion.5.x_ref, ...), custom_call_target="tpu_custom_call" | custom-call | flops 8000000000 | bytes 20000000 | tf_op jit(solution)/shard_map/attention/pallas_call | solution.py:425
  60.7 2.1 fusion.67
  62.8 4.7 constant_dynamic-slice_fusion.6
  68.5 2.1 collective-permute-start.9
  72.5 15.8 %attention.3 = (bf16[512,512]{1,0:T(8,128)(2,1)S(1)}, bf16[512,512]{1,0:T(8,128)(2,1)S(1)}, bf16[512,512]{1,0:T(8,128)(2,1)}, bf16[512,512]{1,0:T(8,128)(2,1)}, ...) custom-call(bf16[512,2048]{1,0:T(8,128)(2,1)} %fusion.7.x_ref, ...), custom_call_target="tpu_custom_call" | custom-call | flops 8000000000 | bytes 20000000 | tf_op jit(solution)/shard_map/attention/pallas_call | solution.py:425
  89.7 4.7 collective-permute-done.9
  103.2 3.1 collective-permute-start.18
  109.3 24.5 %feed_forward.2 = (f32[512,2048]{1,0:T(8,128)}, f32[512,2048]{1,0:T(8,128)}, bf16[512,1024]{1,0:T(8,128)(2,1)S(1)}, bf16[512,1024]{1,0:T(8,128)(2,1)}, f32[256,2048]{1,0:T(8,128)}, /*index=5*/bf16[256,2048]{1,0:T(8,128)(2,1)}) custom-call(s32[2]{0:T(128)S(1)} %pad_add_fusion.10.r_ref, bf16[256,2048]{1,0:T(8,128)(2,1)} %fusion.33.own_rows, ...), custom_call_target="tpu_custom_call" | custom-call | flops 12884901888 | bytes 37748736 | tf_op jit(solution)/shard_map/feed_forward/pallas_call | solution.py:590
  140.4 2.2 convert_select_fusion.1
  144.3 3.9 collective-permute-start.23
  149.3 24.1 %feed_forward.3 = (f32[512,2048]{1,0:T(8,128)}, f32[512,2048]{1,0:T(8,128)}, bf16[512,1024]{1,0:T(8,128)(2,1)S(1)}, bf16[512,1024]{1,0:T(8,128)(2,1)}, f32[256,2048]{1,0:T(8,128)}, /*index=5*/bf16[256,2048]{1,0:T(8,128)(2,1)}) custom-call(s32[2]{0:T(128)S(1)} %pad_add_fusion.10.r_ref, bf16[256,2048]{1,0:T(8,128)(2,1)} %copy-done.38, ...), custom_call_target="tpu_custom_call" | custom-call | flops 12884901888 | bytes 37748736 | tf_op jit(solution)/shard_map/feed_forward/pallas_call | solution.py:590
  175.4 2.9 multiply_convert_fusion.1
  180.7 2.9 multiply_reduce_fusion.5
  187.3 26.4 %feed_forward_back.2 = (bf16[512,1024]{1,0:T(8,128)(2,1)S(1)}, bf16[512,1024]{1,0:T(8,128)(2,1)}, bf16[512,1024]{1,0:T(8,128)(2,1)}, bf16[512,1024]{1,0:T(8,128)...) custom-call(s32[2]{0:T(128)S(1)} %pad_add_fusion.10.r_ref, bf16[256,2048]{1,0:T(8,128)(2,1)} %get-tuple-element.317.own_rows, ...), custom_call_target="tpu_custom_call" | custom-call | flops 12884901888 | bytes 37748736 | tf_op jit(solution)/shard_map/feed_forward_back/pallas_call | solution.py:590
  220.2 2.4 multiply_reduce_fusion.4
  223.7 2.3 fusion.59
  230.0 26.4 %feed_forward_back.3 = (bf16[512,1024]{1,0:T(8,128)(2,1)S(1)}, bf16[512,1024]{1,0:T(8,128)(2,1)}, bf16[512,1024]{1,0:T(8,128)(2,1)}, bf16[512,1024]{1,0:T(8,128)...) custom-call(s32[2]{0:T(128)S(1)} %pad_add_fusion.10.r_ref, bf16[256,2048]{1,0:T(8,128)(2,1)} %copy-done.34, ...), custom_call_target="tpu_custom_call" | custom-call | flops 12884901888 | bytes 37748736 | tf_op jit(solution)/shard_map/feed_forward_back/pallas_call | solution.py:590
  260.0 2.2 fusion.58
  264.1 2.1 fusion.57
  278.9 9.8 attention_back.2
  288.7 3.8 collective-permute-done.37
  295.8 3.5 fusion.56
  301.9 2.6 pad_maximum_fusion.1
  313.5 15.0 %attention_back.3 = (bf16[512,1024]{1,0:T(8,128)(2,1)}, bf16[512,1536]{1,0:T(8,128)(2,1)}) custom-call(bf16[256,2048]{1,0:T(8,128)(2,1)} %copy-done.42, bf16[256,2048]{1,0:T(8,128)(2,1)} %copy-done.115, bf16[512,1024]{1,0:T(8,128)(2,1)} %get-tuple-element.499.out_own, bf16[512,1024]{1,0:T(8,128)(2,1)} %collective-permute-done.7.out_got, ...), custom_call_target="tpu_custom_call" | custom-call | flops 8000000000 | bytes 20000000 | tf_op jit(solution)/shard_map/attention_back/pallas_call | solution.py:425
  329.1 2.6 collective-permute-done.41
  340.7 2.3 pad_maximum_fusion.2
  350.3 11.0 %convolution_convert_fusion.1 = bf16[1024,2048]{1,0:T(8,128)(2,1)} fusion(bf16[2048,1024]{1,0:T(8,128)(2,1)S(1)} %pad_maximum_fusion, bf16[2048,2048]{1,0:T(8,128)(2,1)S(1)} %slice_dynamic-update-slice_fusion.2), kind=kOutput, calls=%fused_computation.26 | convolution fusion | flops 8592031744 | bytes 16777216 | tf_op jit(solution)/shard_map/dot_general | solution.py:40
  362.3 12.5 %first_norm_back.1 = (f32[256,2048]{1,0:T(8,128)}, bf16[256,2048]{1,0:T(8,128)(2,1)S(1)}, f32[256,2048]{1,0:T(8,128)}, bf16[256,2048]{1,0:T(8,128)(2,1)}) custom-call(bf16[512,1536]{1,0:T(8,128)(2,1)} %copy-done.44, bf16[512,1536]{1,0:T(8,128)(2,1)} %get-tuple-element.348.b_ref, bf16[1024,1536]{1,0:T(8,128)(2,1)} %pad_maximum_fusion.4.own_ref, ...), custom_call_target="tpu_custom_call" | custom-call | flops 4000 | bytes 10 | tf_op jit(solution)/shard_map/first_norm_back/pallas_call | solution.py:425
  379.7 16.5 %collective-permute-done.45 = bf16[512,1024]{1,0:T(8,128)(2,1)S(1)} collective-permute-done((bf16[512,1024]{1,0:T(8,128)(2,1)}, bf16[512,1024]{1,0:T(8,128)(2,1)S(1)}, u32[]{:S(2)}, u32[]{:S(2)}) %collective-permute-start.45) | collective-permute-done | bytes 1048608 | tf_op jit(solution)/shard_map/ppermute | solution.py:711
  396.3 7.6 convolution_convert_fusion
  408.8 3.4 copy-done.126
  415.6 2.4 convolution_convert_fusion.3
  420.8 2.5 fusion.71
  424.9 3.3 fusion.55
  433.8 17.3 %collective-permute-done.53 = bf16[512,1024]{1,0:T(8,128)(2,1)S(1)} collective-permute-done((bf16[512,1024]{1,0:T(8,128)(2,1)S(1)}, bf16[512,1024]{1,0:T(8,128)(2,1)S(1)}, u32[]{:S(2)}, u32[]{:S(2)}) %collective-permute-start.53) | collective-permute-done | bytes 1048608 | tf_op jit(solution)/shard_map/ppermute | solution.py:711
  451.6 11.4 %convolution_convert_fusion.2 = bf16[2048,1024]{1,0:T(8,128)(2,1)S(1)} fusion(bf16[2048,2048]{1,0:T(8,128)(2,1)} %slice_dynamic-update-slice_fusion, bf16[2048,1024]{1,0:T(8,128)(2,1)S(1)} %pad_maximum_fusion.3), kind=kOutput, calls=%fused_computation.27 | convolution fusion | flops 8592031744 | bytes 16777216 | tf_op jit(solution)/shard_map/dot_general | solution.py:40
  465.0 12.1 %fusion.16 = bf16[2048,1024]{1,0:T(8,128)(2,1)S(1)} fusion(bf16[2048,2048]{1,0:T(8,128)(2,1)} %slice_dynamic-update-slice_fusion, bf16[512,1024]{1,0:T(8,128)(2,1)S(1)} %collective-permute-done.53, bf16[512,1024]{1,0:T(8,128)(2,1)} %collective-permute-done.52, bf16[512,1024]{1,0:T(8,128)(2,1)S(1)} %copy-done.134, bf16[512,1024]{1,0:T(8,128)(2,1)S(1)} %copy-done.133), kind=kOutput, calls=%fused_computation.25 | convolution fusion | flops 8608808960 | bytes 16777216 | tf_op jit(solution)/shard_map/dot_general | solution.py:40
  490.7 455.4 %line_sum.1.qk_a.qk_b.v_a.v_b.o_ref.in_ref = bf16[2,8192,1024]{2,1,0:T(8,128)(2,1)} custom-call(bf16[1024,1024]{1,0:T(8,128)(2,1)} %get-tuple-element.465.refs_0_, bf16[1024,1024]{1,0:T(8,128)(2,1)} %collective-permute-done.48.refs_1_, bf16[1024,1024]{1,0:T(8,128)(2,1)} %get-tuple-element.463.refs_2_, bf16[1024,1024]{1,0:T(8,128)(2,1)} %copy-done.88, ...), custom_call_target="tpu_custom_call" | custom-call | tf_op jit(solution)/shard_map/line_sum/pallas_call | solution.py:270
  946.2 2.7 fusion.40
  949.3 2.1 fusion.25
  957.8 10.7 %widen_four.1 = (f32[1024,1024]{1,0:T(8,128)}, f32[1024,1024]{1,0:T(8,128)}, f32[1024,1024]{1,0:T(8,128)}, f32[1024,1024]{1,0:T(8,128)}) custom-call(bf16[2,8192,1024]{2,1,0:T(8,128)(2,1)} %line_sum.1.qk_a.qk_b.v_a.v_b.o_ref.in_ref, bf16[2,8192,1024]{2,1,0:T(8,128)(2,1)} %line_sum.1.qk_a.qk_b.v_a.v_b.o_ref.in_ref, ...), custom_call_target="tpu_custom_call" | custom-call | tf_op jit(solution)/shard_map/widen_four/pallas_call | solution.py:658
  968.5 27.5 %widen_three.1 = (f32[4096,1024]{1,0:T(8,128)}, f32[1024,4096]{1,0:T(8,128)}, f32[1024,4096]{1,0:T(8,128)}) custom-call(bf16[2,8192,1024]{2,1,0:T(8,128)(2,1)} %line_sum.1.qk_a.qk_b.v_a.v_b.o_ref.in_ref), custom_call_target="tpu_custom_call" | custom-call | tf_op jit(solution)/shard_map/widen_three/pallas_call | solution.py:623
  (547 shorter events, 161.4 us)
Async XLA Ops:
  2.9 26.3 %collective-permute-start = (bf16[512,512]{1,0:T(8,128)(2,1)}, bf16[512,512]{1,0:T(8,128)(2,1)}, u32[]{:S(2)}, u32[]{:S(2)}) collective-permute-start(bf16[512,512]{1,0:T(8,128)(2,1)} %pad_maximum_fusion.26), channel_id=1, source_target_pairs={{0,1},{1,0},{2,3},{3,2},{4,5},{5,4},{6,7},{7,6},{8,9},{9,8},{10,11... | collective-permute-start | bytes 1572872 | tf_op jit(solution)/shard_map/ppermute | solution.py:715
  6.7 25.8 %collective-permute-start.4 = (bf16[512,512]{1,0:T(8,128)(2,1)}, bf16[512,512]{1,0:T(8,128)(2,1)}, u32[]{:S(2)}, u32[]{:S(2)}) collective-permute-start(bf16[512,512]{1,0:T(8,128)(2,1)} %pad_maximum_fusion.27), channel_id=1, source_target_pairs={{0,1},{1,0},{2,3},{3,2},{4,5},{5,4},{6,7},{7,6},{8,9},{9,8},{10,11... | collective-permute-start | bytes 1572872 | tf_op jit(solution)/shard_map/ppermute | solution.py:715
  7.7 23.5 %collective-permute-start.2 = (bf16[256,512]{1,0:T(8,128)(2,1)}, bf16[256,512]{1,0:T(8,128)(2,1)}, u32[]{:S(2)}, u32[]{:S(2)}) collective-permute-start(bf16[256,512]{1,0:T(8,128)(2,1)} %get-tuple-element.542), channel_id=1, source_target_pairs={{0,2},{2,0},{1,3},{3,1},{4,6},{6,4},{5,7},{7,5},{8,10},{10,8},{9,1... | collective-permute-start | bytes 786440 | tf_op jit(solution)/shard_map/ppermute | solution.py:708
  7.7 23.5 %collective-permute-start.1 = (bf16[256,512]{1,0:T(8,128)(2,1)}, bf16[256,512]{1,0:T(8,128)(2,1)}, u32[]{:S(2)}, u32[]{:S(2)}) collective-permute-start(bf16[256,512]{1,0:T(8,128)(2,1)} %get-tuple-element.544), channel_id=1, source_target_pairs={{0,2},{2,0},{1,3},{3,1},{4,6},{6,4},{5,7},{7,5},{8,10},{10,8},{9,1... | collective-permute-start | bytes 786440 | tf_op jit(solution)/shard_map/ppermute | solution.py:708
  9.7 35.4 %collective-permute-start.7 = (bf16[512,1024]{1,0:T(8,128)(2,1)}, bf16[512,1024]{1,0:T(8,128)(2,1)}, u32[]{:S(2)}, u32[]{:S(2)}) collective-permute-start(bf16[512,1024]{1,0:T(8,128)(2,1)} %get-tuple-element.498), channel_id=1, source_target_pairs={{0,2},{2,0},{1,3},{3,1},{4,6},{6,4},{5,7},{7,5},{8,10},{10,8},{9,1... | collective-permute-start | bytes 3145736 | tf_op jit(solution)/shard_map/ppermute | solution.py:708
  29.2 15.9 %collective-permute-start.6 = (bf16[1024,1536]{1,0:T(8,128)(2,1)}, bf16[1024,1536]{1,0:T(8,128)(2,1)}, u32[]{:S(2)}, u32[]{:S(2)}) collective-permute-start(bf16[1024,1536]{1,0:T(8,128)(2,1)} %pad_maximum_fusion.5), channel_id=1, source_target_pairs={{0,2},{2,0},{1,3},{3,1},{4,6},{6,4},{5,7},{7,5},{8,10},{10,8},{9,1... | collective-permute-start | bytes 9437192 | tf_op jit(solution)/shard_map/ppermute | solution.py:708
  67.5 26.8 %collective-permute-start.13 = (bf16[2048,1024]{1,0:T(8,128)(2,1)}, bf16[2048,1024]{1,0:T(8,128)(2,1)}, u32[]{:S(2)}, u32[]{:S(2)}) collective-permute-start(bf16[2048,1024]{1,0:T(8,128)(2,1)} %constant_dynamic-slice_fusion.6), channel_id=1, source_target_pairs={{0,2},{2,0},{1,3},{3,1},{4,6},{6,4},{5,7},{7,5},{8,10},{10,8},{9,1... | collective-permute-start | bytes 12582920 | tf_op jit(solution)/shard_map/ppermute | solution.py:708
  67.8 26.6 %collective-permute-start.11 = (bf16[1024,2048]{1,0:T(8,128)(2,1)}, bf16[1024,2048]{1,0:T(8,128)(2,1)}, u32[]{:S(2)}, u32[]{:S(2)}) collective-permute-start(bf16[1024,2048]{1,0:T(8,128)(2,1)} %constant_dynamic-slice_fusion.16), channel_id=1, source_target_pairs={{0,2},{2,0},{1,3},{3,1},{4,6},{6,4},{5,7},{7,5},{8,10},{10,8},{9,1... | collective-permute-start | bytes 12582920 | tf_op jit(solution)/shard_map/ppermute | solution.py:708
  68.0 26.3 %collective-permute-start.12 = (bf16[1024,2048]{1,0:T(8,128)(2,1)}, bf16[1024,2048]{1,0:T(8,128)(2,1)}, u32[]{:S(2)}, u32[]{:S(2)}) collective-permute-start(bf16[1024,2048]{1,0:T(8,128)(2,1)} %constant_dynamic-slice_fusion.15), channel_id=1, source_target_pairs={{0,2},{2,0},{1,3},{3,1},{4,6},{6,4},{5,7},{7,5},{8,10},{10,8},{9,1... | collective-permute-start | bytes 12582920 | tf_op jit(solution)/shard_map/ppermute | solution.py:708
  68.5 25.9 %collective-permute-start.9 = (bf16[256,2048]{1,0:T(8,128)(2,1)}, bf16[256,2048]{1,0:T(8,128)(2,1)S(1)}, u32[]{:S(2)}, u32[]{:S(2)}) collective-permute-start(bf16[256,2048]{1,0:T(8,128)(2,1)} %get-tuple-element.222), channel_id=1, source_target_pairs={{0,1},{1,0},{2,3},{3,2},{4,5},{5,4},{6,7},{7,6},{8,9},{9,8},{10,11... | collective-permute-start | bytes 3145736 | tf_op jit(solution)/shard_map/ppermute | solution.py:721
  70.9 17.4 %collective-permute-start.10 = (f32[1,1]{1,0:T(1,128)}, f32[1,1]{1,0:T(1,128)}, u32[]{:S(2)}, u32[]{:S(2)}) collective-permute-start(f32[1,1]{1,0:T(1,128)} %bitcast.4), channel_id=1, source_target_pairs={{0,4},{4,0},{8,12},{12,8},{16,20},{20,16},{24,28},{28,24},{1,5},{5... | collective-permute-start | bytes 20 | tf_op jit(solution)/shard_map/ppermute | solution.py:316
  103.2 30.7 %collective-permute-start.18 = (f32[1,1]{1,0:T(1,128)}, f32[1,1]{1,0:T(1,128)}, u32[]{:S(2)}, u32[]{:S(2)}) collective-permute-start(f32[1,1]{1,0:T(1,128)} %add.219), channel_id=1, source_target_pairs={{0,8},{4,12},{8,0},{12,4},{16,24},{20,28},{24,16},{28,20},{1,9},{5... | collective-permute-start | bytes 20 | tf_op jit(solution)/shard_map/ppermute | solution.py:316
  106.3 28.2 %collective-permute-start.16 = (bf16[256,2048]{1,0:T(8,128)(2,1)S(1)}, bf16[256,2048]{1,0:T(8,128)(2,1)S(1)}, u32[]{:S(2)}, u32[]{:S(2)}) collective-permute-start(bf16[256,2048]{1,0:T(8,128)(2,1)S(1)} %get-tuple-element.243), channel_id=1, source_target_pairs={{0,1},{1,0},{2,3},{3,2},{4,5},{5,4},{6,7},{7,6},{8,9},{9,8},{10,11... | collective-permute-start | bytes 3145736 | tf_op jit(solution)/shard_map/ppermute | solution.py:721
  107.8 26.7 %collective-permute-start.17 = (bf16[256,2048]{1,0:T(8,128)(2,1)}, bf16[256,2048]{1,0:T(8,128)(2,1)S(1)}, u32[]{:S(2)}, u32[]{:S(2)}) collective-permute-start(bf16[256,2048]{1,0:T(8,128)(2,1)} %fusion.33.own_rows), channel_id=1, source_target_pairs={{0,4},{4,0},{8,12},{12,8},{16,20},{20,16},{24,28},{28,24},{1,5},{5... | collective-permute-start | bytes 3145736 | tf_op jit(solution)/shard_map/ppermute | solution.py:711
  144.3 29.1 %collective-permute-start.23 = (f32[1,1]{1,0:T(1,128)}, f32[1,1]{1,0:T(1,128)}, u32[]{:S(2)}, u32[]{:S(2)}) collective-permute-start(f32[1,1]{1,0:T(1,128)} %add.226), channel_id=1, source_target_pairs={{0,16},{4,20},{8,24},{12,28},{16,0},{20,4},{24,8},{28,12},{1,17},{... | collective-permute-start | bytes 20 | tf_op jit(solution)/shard_map/ppermute | solution.py:316
  148.2 25.8 %collective-permute-start.21 = (bf16[256,2048]{1,0:T(8,128)(2,1)}, bf16[256,2048]{1,0:T(8,128)(2,1)S(1)}, u32[]{:S(2)}, u32[]{:S(2)}) collective-permute-start(bf16[256,2048]{1,0:T(8,128)(2,1)} %get-tuple-element.261), channel_id=1, source_target_pairs={{0,1},{1,0},{2,3},{3,2},{4,5},{5,4},{6,7},{7,6},{8,9},{9,8},{10,11... | collective-permute-start | bytes 3145736 | tf_op jit(solution)/shard_map/ppermute | solution.py:721
  148.7 25.3 %collective-permute-start.22 = (bf16[256,2048]{1,0:T(8,128)(2,1)S(1)}, bf16[256,2048]{1,0:T(8,128)(2,1)S(1)}, u32[]{:S(2)}, u32[]{:S(2)}) collective-permute-start(bf16[256,2048]{1,0:T(8,128)(2,1)S(1)} %fusion.34.own_rows), channel_id=1, source_target_pairs={{0,4},{4,0},{8,12},{12,8},{16,20},{20,16},{24,28},{28,24},{1,5},{5... | collective-permute-start | bytes 3145736 | tf_op jit(solution)/shard_map/ppermute | solution.py:711
  174.1 9.5 collective-permute-start.26
  184.2 29.4 %collective-permute-start.27 = (bf16[256,2048]{1,0:T(8,128)(2,1)S(1)}, bf16[256,2048]{1,0:T(8,128)(2,1)S(1)}, u32[]{:S(2)}, u32[]{:S(2)}) collective-permute-start(bf16[256,2048]{1,0:T(8,128)(2,1)S(1)} %get-tuple-element.282), channel_id=1, source_target_pairs={{0,1},{1,0},{2,3},{3,2},{4,5},{5,4},{6,7},{7,6},{8,9},{9,8},{10,11... | collective-permute-start | bytes 3145736 | tf_op jit(solution)/shard_map/ppermute | solution.py:721
  185.8 27.9 %collective-permute-start.28 = (bf16[512,1024]{1,0:T(8,128)(2,1)}, bf16[512,1024]{1,0:T(8,128)(2,1)S(1)}, u32[]{:S(2)}, u32[]{:S(2)}) collective-permute-start(bf16[512,1024]{1,0:T(8,128)(2,1)} %get-tuple-element.283), channel_id=1, source_target_pairs={{0,4},{4,0},{8,12},{12,8},{16,20},{20,16},{24,28},{28,24},{1,5},{5... | collective-permute-start | bytes 3145736 | tf_op jit(solution)/shard_map/ppermute | solution.py:711
  213.7 10.0 %collective-permute-start.31 = (bf16[256,2048]{1,0:T(8,128)(2,1)}, bf16[256,2048]{1,0:T(8,128)(2,1)}, u32[]{:S(2)}, u32[]{:S(2)}) collective-permute-start(bf16[256,2048]{1,0:T(8,128)(2,1)} %get-tuple-element.289), channel_id=1, source_target_pairs={{0,2},{2,0},{1,3},{3,1},{4,6},{6,4},{5,7},{7,5},{8,10},{10,8},{9,1... | collective-permute-start | bytes 3145736 | tf_op jit(solution)/shard_map/ppermute | solution.py:708
  218.2 7.8 collective-permute-start.30
  226.1 30.3 %collective-permute-start.34 = (f32[1,1]{1,0:T(1,128)}, f32[1,1]{1,0:T(1,128)}, u32[]{:S(2)}, u32[]{:S(2)}) collective-permute-start(f32[1,1]{1,0:T(1,128)} %bitcast.12), channel_id=1, source_target_pairs={{0,4},{4,0},{8,12},{12,8},{16,20},{20,16},{24,28},{28,24},{1,5},{5... | collective-permute-start | bytes 20 | tf_op jit(solution)/shard_map/ppermute | solution.py:316
  228.0 29.1 %collective-permute-start.32 = (bf16[256,2048]{1,0:T(8,128)(2,1)S(1)}, bf16[256,2048]{1,0:T(8,128)(2,1)S(1)}, u32[]{:S(2)}, u32[]{:S(2)}) collective-permute-start(bf16[256,2048]{1,0:T(8,128)(2,1)S(1)} %get-tuple-element.301), channel_id=1, source_target_pairs={{0,1},{1,0},{2,3},{3,2},{4,5},{5,4},{6,7},{7,6},{8,9},{9,8},{10,11... | collective-permute-start | bytes 3145736 | tf_op jit(solution)/shard_map/ppermute | solution.py:721
  228.5 28.6 %collective-permute-start.33 = (bf16[512,1024]{1,0:T(8,128)(2,1)}, bf16[512,1024]{1,0:T(8,128)(2,1)S(1)}, u32[]{:S(2)}, u32[]{:S(2)}) collective-permute-start(bf16[512,1024]{1,0:T(8,128)(2,1)} %get-tuple-element.302), channel_id=1, source_target_pairs={{0,4},{4,0},{8,12},{12,8},{16,20},{20,16},{24,28},{28,24},{1,5},{5... | collective-permute-start | bytes 3145736 | tf_op jit(solution)/shard_map/ppermute | solution.py:711
  267.3 25.2 %collective-permute-start.37 = (bf16[256,2048]{1,0:T(8,128)(2,1)}, bf16[256,2048]{1,0:T(8,128)(2,1)}, u32[]{:S(2)}, u32[]{:S(2)}) collective-permute-start(bf16[256,2048]{1,0:T(8,128)(2,1)} %get-tuple-element.316), channel_id=1, source_target_pairs={{0,1},{1,0},{2,3},{3,2},{4,5},{5,4},{6,7},{7,6},{8,9},{9,8},{10,11... | collective-permute-start | bytes 3145736 | tf_op jit(solution)/shard_map/ppermute | solution.py:721
  268.8 24.9 %collective-permute-start.38 = (bf16[256,2048]{1,0:T(8,128)(2,1)}, bf16[256,2048]{1,0:T(8,128)(2,1)}, u32[]{:S(2)}, u32[]{:S(2)}) collective-permute-start(bf16[256,2048]{1,0:T(8,128)(2,1)} %get-tuple-element.317.own_rows), channel_id=1, source_target_pairs={{0,4},{4,0},{8,12},{12,8},{16,20},{20,16},{24,28},{28,24},{1,5},{5... | collective-permute-start | bytes 3145736 | tf_op jit(solution)/shard_map/ppermute | solution.py:711
  304.5 31.1 %collective-permute-start.24 = (bf16[256,512]{1,0:T(8,128)(2,1)S(1)}, bf16[256,512]{1,0:T(8,128)(2,1)S(1)}, u32[]{:S(2)}, u32[]{:S(2)}) collective-permute-start(bf16[256,512]{1,0:T(8,128)(2,1)S(1)} %copy-done.123), channel_id=1, source_target_pairs={{0,2},{2,0},{1,3},{3,1},{4,6},{6,4},{5,7},{7,5},{8,10},{10,8},{9,1... | collective-permute-start | bytes 786440 | tf_op jit(solution)/shard_map/ppermute | solution.py:708
  306.5 25.3 %collective-permute-start.41 = (bf16[256,2048]{1,0:T(8,128)(2,1)S(1)}, bf16[256,2048]{1,0:T(8,128)(2,1)S(1)}, u32[]{:S(2)}, u32[]{:S(2)}) collective-permute-start(bf16[256,2048]{1,0:T(8,128)(2,1)S(1)} %copy-done.35), channel_id=1, source_target_pairs={{0,4},{4,0},{8,12},{12,8},{16,20},{20,16},{24,28},{28,24},{1,5},{5... | collective-permute-start | bytes 3145736 | tf_op jit(solution)/shard_map/ppermute | solution.py:711
  310.1 18.4 %collective-permute-start.42 = (f32[1,1]{1,0:T(1,128)}, f32[1,1]{1,0:T(1,128)}, u32[]{:S(2)}, u32[]{:S(2)}) collective-permute-start(f32[1,1]{1,0:T(1,128)} %add.250), channel_id=1, source_target_pairs={{0,16},{4,20},{8,24},{12,28},{16,0},{20,4},{24,8},{28,12},{1,17},{... | collective-permute-start | bytes 20 | tf_op jit(solution)/shard_map/ppermute | solution.py:316
  332.9 13.8 %collective-permute-start.43 = (bf16[512,2048]{1,0:T(8,128)(2,1)S(1)}, bf16[512,2048]{1,0:T(8,128)(2,1)S(1)}, u32[]{:S(2)}, u32[]{:S(2)}) collective-permute-start(bf16[512,2048]{1,0:T(8,128)(2,1)S(1)} %pad_maximum_fusion.8), channel_id=1, source_target_pairs={{0,2},{2,0},{1,3},{3,1},{4,6},{6,4},{5,7},{7,5},{8,10},{10,8},{9,1... | collective-permute-start | bytes 6291464 | tf_op jit(solution)/shard_map/ppermute | solution.py:708
  348.2 31.5 %collective-permute-start.44 = (bf16[512,1024]{1,0:T(8,128)(2,1)}, bf16[512,1024]{1,0:T(8,128)(2,1)S(1)}, u32[]{:S(2)}, u32[]{:S(2)}) collective-permute-start(bf16[512,1024]{1,0:T(8,128)(2,1)} %get-tuple-element.354), channel_id=1, source_target_pairs={{0,4},{4,0},{8,12},{12,8},{16,20},{20,16},{24,28},{28,24},{1,5},{5... | collective-permute-start | bytes 3145736 | tf_op jit(solution)/shard_map/ppermute | solution.py:711
  348.8 47.4 %collective-permute-start.45 = (bf16[512,1024]{1,0:T(8,128)(2,1)}, bf16[512,1024]{1,0:T(8,128)(2,1)S(1)}, u32[]{:S(2)}, u32[]{:S(2)}) collective-permute-start(bf16[512,1024]{1,0:T(8,128)(2,1)} %get-tuple-element.355), channel_id=1, source_target_pairs={{0,4},{4,0},{8,12},{12,8},{16,20},{20,16},{24,28},{28,24},{1,5},{5... | collective-permute-start | bytes 3145736 | tf_op jit(solution)/shard_map/ppermute | solution.py:711
  361.3 13.4 %collective-permute-start.46 = (f32[1,1]{1,0:T(1,128)}, f32[1,1]{1,0:T(1,128)}, u32[]{:S(2)}, u32[]{:S(2)}) collective-permute-start(f32[1,1]{1,0:T(1,128)} %add.253), channel_id=1, source_target_pairs={{0,2},{2,0},{1,3},{3,1},{4,6},{6,4},{5,7},{7,5},{8,10},{10,8},{9,1... | collective-permute-start | bytes 20 | tf_op jit(solution)/shard_map/ppermute | solution.py:316
  403.9 29.4 %collective-permute-start.52 = (bf16[512,1024]{1,0:T(8,128)(2,1)}, bf16[512,1024]{1,0:T(8,128)(2,1)}, u32[]{:S(2)}, u32[]{:S(2)}) collective-permute-start(bf16[512,1024]{1,0:T(8,128)(2,1)} %get-tuple-element.384), channel_id=1, source_target_pairs={{0,4},{4,0},{8,12},{12,8},{16,20},{20,16},{24,28},{28,24},{1,5},{5... | collective-permute-start | bytes 3145736 | tf_op jit(solution)/shard_map/ppermute | solution.py:711
  404.5 18.8 %collective-permute-start.56 = (bf16[256,2048]{1,0:T(8,128)(2,1)S(1)}, bf16[256,2048]{1,0:T(8,128)(2,1)}, u32[]{:S(2)}, u32[]{:S(2)}) collective-permute-start(bf16[256,2048]{1,0:T(8,128)(2,1)S(1)} %get-tuple-element.397), channel_id=1, source_target_pairs={{0,2},{2,0},{1,3},{3,1},{4,6},{6,4},{5,7},{7,5},{8,10},{10,8},{9,1... | collective-permute-start | bytes 3145736 | tf_op jit(solution)/shard_map/ppermute | solution.py:708
  404.5 23.6 %collective-permute-start.57 = (bf16[256,2048]{1,0:T(8,128)(2,1)}, bf16[256,2048]{1,0:T(8,128)(2,1)S(1)}, u32[]{:S(2)}, u32[]{:S(2)}) collective-permute-start(bf16[256,2048]{1,0:T(8,128)(2,1)} %get-tuple-element.399), channel_id=1, source_target_pairs={{0,2},{2,0},{1,3},{3,1},{4,6},{6,4},{5,7},{7,5},{8,10},{10,8},{9,1... | collective-permute-start | bytes 3145736 | tf_op jit(solution)/shard_map/ppermute | solution.py:708
  405.5 46.2 %collective-permute-start.50 = (bf16[1024,1536]{1,0:T(8,128)(2,1)S(1)}, bf16[1024,1536]{1,0:T(8,128)(2,1)S(1)}, u32[]{:S(2)}, u32[]{:S(2)}) collective-permute-start(bf16[1024,1536]{1,0:T(8,128)(2,1)S(1)} %get-tuple-element.458), channel_id=1, source_target_pairs={{0,2},{2,0},{1,3},{3,1},{4,6},{6,4},{5,7},{7,5},{8,10},{10,8},{9,1... | collective-permute-start | bytes 9437192 | tf_op jit(solution)/shard_map/ppermute | solution.py:708
  414.0 15.6 %collective-permute-start.49 = (bf16[512,2048]{1,0:T(8,128)(2,1)}, bf16[512,2048]{1,0:T(8,128)(2,1)S(1)}, u32[]{:S(2)}, u32[]{:S(2)}) collective-permute-start(bf16[512,2048]{1,0:T(8,128)(2,1)} %pad_maximum_fusion.9), channel_id=1, source_target_pairs={{0,2},{2,0},{1,3},{3,1},{4,6},{6,4},{5,7},{7,5},{8,10},{10,8},{9,1... | collective-permute-start | bytes 6291464 | tf_op jit(solution)/shard_map/ppermute | solution.py:708
  423.3 27.8 %collective-permute-start.53 = (bf16[512,1024]{1,0:T(8,128)(2,1)S(1)}, bf16[512,1024]{1,0:T(8,128)(2,1)S(1)}, u32[]{:S(2)}, u32[]{:S(2)}) collective-permute-start(bf16[512,1024]{1,0:T(8,128)(2,1)S(1)} %copy-done.135), channel_id=1, source_target_pairs={{0,4},{4,0},{8,12},{12,8},{16,20},{20,16},{24,28},{28,24},{1,5},{5... | collective-permute-start | bytes 3145736 | tf_op jit(solution)/shard_map/ppermute | solution.py:711
  428.2 23.5 %collective-permute-start.51 = (bf16[512,1024]{1,0:T(8,128)(2,1)S(1)}, bf16[512,1024]{1,0:T(8,128)(2,1)S(1)}, u32[]{:S(2)}, u32[]{:S(2)}) collective-permute-start(bf16[512,1024]{1,0:T(8,128)(2,1)S(1)} %get-tuple-element.488), channel_id=1, source_target_pairs={{0,2},{2,0},{1,3},{3,1},{4,6},{6,4},{5,7},{7,5},{8,10},{10,8},{9,1... | collective-permute-start | bytes 3145736 | tf_op jit(solution)/shard_map/ppermute | solution.py:708
  429.6 59.1 %collective-permute-start.48 = (bf16[1024,1024]{1,0:T(8,128)(2,1)}, bf16[1024,1024]{1,0:T(8,128)(2,1)}, u32[]{:S(2)}, u32[]{:S(2)}) collective-permute-start(bf16[1024,1024]{1,0:T(8,128)(2,1)} %get-tuple-element.464), channel_id=1, source_target_pairs={{0,2},{2,0},{1,3},{3,1},{4,6},{6,4},{5,7},{7,5},{8,10},{10,8},{9,1... | collective-permute-start | bytes 6291464 | tf_op jit(solution)/shard_map/ppermute | solution.py:708
  433.3 512.8 %collective-permute-start.58 = (bf16[256,2048]{1,0:T(8,128)(2,1)}, bf16[256,2048]{1,0:T(8,128)(2,1)}, u32[]{:S(2)}, u32[]{:S(2)}) collective-permute-start(bf16[256,2048]{1,0:T(8,128)(2,1)} %get-tuple-element.422), channel_id=1, source_target_pairs={{0,1},{1,0},{2,3},{3,2},{4,5},{5,4},{6,7},{7,6},{8,9},{9,8},{10,11... | collective-permute-start | bytes 3145736 | tf_op jit(solution)/shard_map/ppermute | solution.py:721
  451.1 495.0 %collective-permute-start.59 = (bf16[256,2048]{1,0:T(8,128)(2,1)}, bf16[256,2048]{1,0:T(8,128)(2,1)S(1)}, u32[]{:S(2)}, u32[]{:S(2)}) collective-permute-start(bf16[256,2048]{1,0:T(8,128)(2,1)} %get-tuple-element.420), channel_id=1, source_target_pairs={{0,1},{1,0},{2,3},{3,2},{4,5},{5,4},{6,7},{7,6},{8,9},{9,8},{10,11... | collective-permute-start | bytes 3145736 | tf_op jit(solution)/shard_map/ppermute | solution.py:721
  478.8 9.9 collective-permute-start.55
  478.8 9.9 collective-permute-start.54
  953.7 42.3 %collective-permute-start.60 = (f32[256,512]{1,0:T(8,128)S(1)}, f32[256,512]{1,0:T(8,128)S(1)}, u32[]{:S(2)}, u32[]{:S(2)}) collective-permute-start(f32[256,512]{1,0:T(8,128)S(1)} %constant_dynamic-slice_fusion.1), channel_id=1, source_target_pairs={{0,2},{2,0},{1,3},{3,1},{4,6},{6,4},{5,7},{7,5},{8,10},{10,8},{9,1... | collective-permute-start | bytes 1572872 | tf_op jit(solution)/shard_map/ppermute | solution.py:708
  955.7 40.5 %collective-permute-start.61 = (f32[256,512]{1,0:T(8,128)S(1)}, f32[256,512]{1,0:T(8,128)S(1)}, u32[]{:S(2)}, u32[]{:S(2)}) collective-permute-start(f32[256,512]{1,0:T(8,128)S(1)} %constant_dynamic-slice_fusion), channel_id=1, source_target_pairs={{0,2},{2,0},{1,3},{3,1},{4,6},{6,4},{5,7},{7,5},{8,10},{10,8},{9,1... | collective-permute-start | bytes 1572872 | tf_op jit(solution)/shard_map/ppermute | solution.py:708
  (154 other events, 2253.4 us)

commit v6 on v5

--- a/solution.py
+++ b/solution.py
@@ -957,13 +957,11 @@
     ups_b, part_b = raw[:4], joined(raw[4:])
     hidden_a = second_norm_back(0, part_a, got_a)
     hidden_a, part_b, low, mine = tie((hidden_a, part_b, part_b.astype(BF), low_a[0]))
-    error_sum = hop(error_sum, *hops[1])
     got_b, cross_low_a = from_chips(low), cross(mine)
     parts = attention_back(0, hidden_a, [])
     parts, got_b, cross_low_a, error_sum = tie((parts, got_b, cross_low_a, error_sum))
     hidden_b = second_norm_back(1, part_b, got_b)
     hidden_b, parts, mine, error_sum = tie((hidden_b, parts, low_b[0], error_sum))
-    error_sum = hop(error_sum, *hops[2])
     cross_low_b = cross(mine)
     first_back, back_b = attention_back(
         1, hidden_b, [key_heads[0], value_heads[0], *tables[0], *parts[1:]]
@@ -996,7 +994,7 @@
     )
     downs, gate_gives, error_sum = tie((downs, gate_gives, error_sum))
     cross_gate_a, cross_gate_b = (cross(g) for g in gate_gives)
-    for step in hops[3:]:
+    for step in hops[1:]:
         error_sum = hop(error_sum, *step)
     grad_down = product(*downs)
     grad_down, backs = tie((grad_down, backs))

time: 1010 us -> 1010 us (level)
  transfers between devices with their start and end apart: 62 -> 62, of which waited for: 11 -> 12; matrix products, arithmetic and copies ran while one was open for 16% -> 16% of each run, Pallas kernels for 65% -> 65%
where the time goes in v6:
time: 1010 us; the launch traced here: 1000 us
  Pallas kernels  661 us (65%)
  other arithmetic  97.3 us (10%)
  local copies, waits for them, and re-layouts  91.1 us (9%)
  waiting for transfers between devices  49.7 us (5%)
  starting transfers between devices  44.9 us (4%)
  matrix products  44.5 us (4%)
  between operations  11.3 us (1%)
    pallas_call x1, Pallas kernels, line_sum(): pl.pallas_call(functools.partial(line_kernel, sizes, spots, len(gives), c...  455 us
    pallas_call x4, Pallas kernels, feed_forward(): pl.pallas_call(functools.partial(kernel, side_steps=side_steps), out_shap...  101 us
    pallas_call x5, Pallas kernels, in_vmem(): pl.pallas_call(kernel, out_shape=out_shape, in_specs=[pl.BlockSpec(memory...  65.8 us
    unnamed x296, local copies, waits for them, and re-layouts  51.4 us
    dot_general x5, matrix products, contract_rows(): lax.dot_general(left, right, (((0,), (0,)), ((), ())), preferred_element_...  44.5 us
    ppermute x10, waiting for transfers between devices, cross(): return lax.ppermute(operand, 'dp', sides)  30.4 us
    pallas_call x1, Pallas kernels, widen_three(): pl.pallas_call(kernel, out_shape=[jax.ShapeDtypeStruct(x, F32) for x in (...  27.5 us
    dynamic_slice x10, local copies, waits for them, and re-layouts, take(): return lax.dynamic_slice_in_dim(operand, index * size, size, axis)  22.3 us
  transfers between devices with their start and end apart: 62, of which 12 were waited for; matrix products, arithmetic and copies ran while one was open for 16% of the time, Pallas kernels for 65%

profile of v6, /device:TPU:0, one launch (start us, length us, event | category | flops | bytes accessed | tf_op | source)
XLA Modules:
  0.0 999.6 jit_solution(10822553770402694256)
XLA Ops:
  2.9 3.0 collective-permute-start
  10.4 2.8 fusion.50
  13.3 2.7 constant_dynamic-slice_fusion.11
  16.0 4.8 constant_dynamic-slice_fusion.16
  20.8 4.9 constant_dynamic-slice_fusion.15
  35.6 3.1 pad_maximum_fusion.4.own_ref
  45.1 12.7 %attention.2 = (bf16[512,512]{1,0:T(8,128)(2,1)S(1)}, bf16[512,512]{1,0:T(8,128)(2,1)S(1)}, bf16[512,512]{1,0:T(8,128)(2,1)}, bf16[512,512]{1,0:T(8,128)(2,1)}, ...) custom-call(bf16[512,2048]{1,0:T(8,128)(2,1)} %fusion.5.x_ref, ...), custom_call_target="tpu_custom_call" | custom-call | flops 8000000000 | bytes 20000000 | tf_op jit(solution)/shard_map/attention/pallas_call | solution.py:425
  60.7 2.1 fusion.67
  62.8 4.7 constant_dynamic-slice_fusion.6
  72.5 15.8 %attention.3 = (bf16[512,512]{1,0:T(8,128)(2,1)S(1)}, bf16[512,512]{1,0:T(8,128)(2,1)S(1)}, bf16[512,512]{1,0:T(8,128)(2,1)}, bf16[512,512]{1,0:T(8,128)(2,1)}, ...) custom-call(bf16[512,2048]{1,0:T(8,128)(2,1)} %fusion.7.x_ref, ...), custom_call_target="tpu_custom_call" | custom-call | flops 8000000000 | bytes 20000000 | tf_op jit(solution)/shard_map/attention/pallas_call | solution.py:425
  89.7 4.7 collective-permute-done.9
  103.2 3.1 collective-permute-start.18
  109.3 24.5 %feed_forward.2 = (f32[512,2048]{1,0:T(8,128)}, f32[512,2048]{1,0:T(8,128)}, bf16[512,1024]{1,0:T(8,128)(2,1)S(1)}, bf16[512,1024]{1,0:T(8,128)(2,1)}, f32[256,2048]{1,0:T(8,128)}, /*index=5*/bf16[256,2048]{1,0:T(8,128)(2,1)}) custom-call(s32[2]{0:T(128)S(1)} %pad_add_fusion.10.r_ref, bf16[256,2048]{1,0:T(8,128)(2,1)} %fusion.33.own_rows, ...), custom_call_target="tpu_custom_call" | custom-call | flops 12884901888 | bytes 37748736 | tf_op jit(solution)/shard_map/feed_forward/pallas_call | solution.py:590
  140.4 2.2 convert_select_fusion.1
  144.3 3.9 collective-permute-start.23
  149.3 24.1 %feed_forward.3 = (f32[512,2048]{1,0:T(8,128)}, f32[512,2048]{1,0:T(8,128)}, bf16[512,1024]{1,0:T(8,128)(2,1)S(1)}, bf16[512,1024]{1,0:T(8,128)(2,1)}, f32[256,2048]{1,0:T(8,128)}, /*index=5*/bf16[256,2048]{1,0:T(8,128)(2,1)}) custom-call(s32[2]{0:T(128)S(1)} %pad_add_fusion.10.r_ref, bf16[256,2048]{1,0:T(8,128)(2,1)} %copy-done.38, ...), custom_call_target="tpu_custom_call" | custom-call | flops 12884901888 | bytes 37748736 | tf_op jit(solution)/shard_map/feed_forward/pallas_call | solution.py:590
  175.4 2.9 multiply_convert_fusion.1
  180.7 2.9 multiply_reduce_fusion.5
  187.3 26.4 %feed_forward_back.2 = (bf16[512,1024]{1,0:T(8,128)(2,1)S(1)}, bf16[512,1024]{1,0:T(8,128)(2,1)}, bf16[512,1024]{1,0:T(8,128)(2,1)}, bf16[512,1024]{1,0:T(8,128)...) custom-call(s32[2]{0:T(128)S(1)} %pad_add_fusion.10.r_ref, bf16[256,2048]{1,0:T(8,128)(2,1)} %get-tuple-element.317.own_rows, ...), custom_call_target="tpu_custom_call" | custom-call | flops 12884901888 | bytes 37748736 | tf_op jit(solution)/shard_map/feed_forward_back/pallas_call | solution.py:590
  220.2 2.4 multiply_reduce_fusion.4
  223.7 2.3 fusion.59
  230.0 26.4 %feed_forward_back.3 = (bf16[512,1024]{1,0:T(8,128)(2,1)S(1)}, bf16[512,1024]{1,0:T(8,128)(2,1)}, bf16[512,1024]{1,0:T(8,128)(2,1)}, bf16[512,1024]{1,0:T(8,128)...) custom-call(s32[2]{0:T(128)S(1)} %pad_add_fusion.10.r_ref, bf16[256,2048]{1,0:T(8,128)(2,1)} %copy-done.34, ...), custom_call_target="tpu_custom_call" | custom-call | flops 12884901888 | bytes 37748736 | tf_op jit(solution)/shard_map/feed_forward_back/pallas_call | solution.py:590
  260.0 2.2 fusion.58
  264.1 2.1 fusion.57
  274.6 9.8 attention_back.2
  284.4 8.1 collective-permute-done.37
  295.8 3.5 fusion.56
  301.9 2.6 pad_maximum_fusion.1
  310.1 3.4 copy-done.125
  313.5 15.0 %attention_back.3 = (bf16[512,1024]{1,0:T(8,128)(2,1)}, bf16[512,1536]{1,0:T(8,128)(2,1)}) custom-call(bf16[256,2048]{1,0:T(8,128)(2,1)} %copy-done.42, bf16[256,2048]{1,0:T(8,128)(2,1)} %copy-done.119, bf16[512,1024]{1,0:T(8,128)(2,1)} %get-tuple-element.499.out_own, bf16[512,1024]{1,0:T(8,128)(2,1)} %collective-permute-done.7.out_got, ...), custom_call_target="tpu_custom_call" | custom-call | flops 8000000000 | bytes 20000000 | tf_op jit(solution)/shard_map/attention_back/pallas_call | solution.py:425
  328.5 3.2 collective-permute-done.40
  340.7 2.3 pad_maximum_fusion.2
  350.3 11.0 %convolution_convert_fusion.1 = bf16[1024,2048]{1,0:T(8,128)(2,1)} fusion(bf16[2048,1024]{1,0:T(8,128)(2,1)S(1)} %pad_maximum_fusion, bf16[2048,2048]{1,0:T(8,128)(2,1)S(1)} %slice_dynamic-update-slice_fusion.2), kind=kOutput, calls=%fused_computation.26 | convolution fusion | flops 8592031744 | bytes 16777216 | tf_op jit(solution)/shard_map/dot_general | solution.py:40
  363.0 12.4 %first_norm_back.1 = (f32[256,2048]{1,0:T(8,128)}, bf16[256,2048]{1,0:T(8,128)(2,1)S(1)}, f32[256,2048]{1,0:T(8,128)}, bf16[256,2048]{1,0:T(8,128)(2,1)}) custom-call(bf16[512,1536]{1,0:T(8,128)(2,1)} %copy-done.44, bf16[512,1536]{1,0:T(8,128)(2,1)} %get-tuple-element.348.b_ref, bf16[1024,1536]{1,0:T(8,128)(2,1)} %pad_maximum_fusion.4.own_ref, ...), custom_call_target="tpu_custom_call" | custom-call | flops 4000 | bytes 10 | tf_op jit(solution)/shard_map/first_norm_back/pallas_call | solution.py:425
  377.8 2.9 collective-permute-done.45
  387.6 8.6 collective-permute-done.43
  396.3 7.6 convolution_convert_fusion
  408.8 3.4 copy-done.126
  415.6 2.4 convolution_convert_fusion.3
  420.8 2.5 fusion.71
  424.9 3.3 fusion.55
  433.8 17.3 %collective-permute-done.53 = bf16[512,1024]{1,0:T(8,128)(2,1)S(1)} collective-permute-done((bf16[512,1024]{1,0:T(8,128)(2,1)S(1)}, bf16[512,1024]{1,0:T(8,128)(2,1)S(1)}, u32[]{:S(2)}, u32[]{:S(2)}) %collective-permute-start.53) | collective-permute-done | bytes 1048608 | tf_op jit(solution)/shard_map/ppermute | solution.py:711
  451.6 11.4 %convolution_convert_fusion.2 = bf16[2048,1024]{1,0:T(8,128)(2,1)S(1)} fusion(bf16[2048,2048]{1,0:T(8,128)(2,1)} %slice_dynamic-update-slice_fusion, bf16[2048,1024]{1,0:T(8,128)(2,1)S(1)} %pad_maximum_fusion.3), kind=kOutput, calls=%fused_computation.27 | convolution fusion | flops 8592031744 | bytes 16777216 | tf_op jit(solution)/shard_map/dot_general | solution.py:40
  465.0 12.1 %fusion.16 = bf16[2048,1024]{1,0:T(8,128)(2,1)S(1)} fusion(bf16[2048,2048]{1,0:T(8,128)(2,1)} %slice_dynamic-update-slice_fusion, bf16[512,1024]{1,0:T(8,128)(2,1)S(1)} %collective-permute-done.53, bf16[512,1024]{1,0:T(8,128)(2,1)} %collective-permute-done.52, bf16[512,1024]{1,0:T(8,128)(2,1)S(1)} %copy-done.134, bf16[512,1024]{1,0:T(8,128)(2,1)S(1)} %copy-done.133), kind=kOutput, calls=%fused_computation.25 | convolution fusion | flops 8608808960 | bytes 16777216 | tf_op jit(solution)/shard_map/dot_general | solution.py:40
  490.7 455.4 %line_sum.1.qk_a.qk_b.v_a.v_b.o_ref.in_ref = bf16[2,8192,1024]{2,1,0:T(8,128)(2,1)} custom-call(bf16[1024,1024]{1,0:T(8,128)(2,1)} %get-tuple-element.465.refs_0_, bf16[1024,1024]{1,0:T(8,128)(2,1)} %collective-permute-done.48.refs_1_, bf16[1024,1024]{1,0:T(8,128)(2,1)} %get-tuple-element.463.refs_2_, bf16[1024,1024]{1,0:T(8,128)(2,1)} %copy-done.88, ...), custom_call_target="tpu_custom_call" | custom-call | tf_op jit(solution)/shard_map/line_sum/pallas_call | solution.py:270
  946.2 2.7 fusion.40
  957.8 10.7 %widen_four.1 = (f32[1024,1024]{1,0:T(8,128)}, f32[1024,1024]{1,0:T(8,128)}, f32[1024,1024]{1,0:T(8,128)}, f32[1024,1024]{1,0:T(8,128)}) custom-call(bf16[2,8192,1024]{2,1,0:T(8,128)(2,1)} %line_sum.1.qk_a.qk_b.v_a.v_b.o_ref.in_ref, bf16[2,8192,1024]{2,1,0:T(8,128)(2,1)} %line_sum.1.qk_a.qk_b.v_a.v_b.o_ref.in_ref, ...), custom_call_target="tpu_custom_call" | custom-call | tf_op jit(solution)/shard_map/widen_four/pallas_call | solution.py:658
  968.5 27.5 %widen_three.1 = (f32[4096,1024]{1,0:T(8,128)}, f32[1024,4096]{1,0:T(8,128)}, f32[1024,4096]{1,0:T(8,128)}) custom-call(bf16[2,8192,1024]{2,1,0:T(8,128)(2,1)} %line_sum.1.qk_a.qk_b.v_a.v_b.o_ref.in_ref), custom_call_target="tpu_custom_call" | custom-call | tf_op jit(solution)/shard_map/widen_three/pallas_call | solution.py:623
  (547 shorter events, 162.4 us)
Async XLA Ops:
  2.9 26.3 %collective-permute-start = (bf16[512,512]{1,0:T(8,128)(2,1)}, bf16[512,512]{1,0:T(8,128)(2,1)}, u32[]{:S(2)}, u32[]{:S(2)}) collective-permute-start(bf16[512,512]{1,0:T(8,128)(2,1)} %pad_maximum_fusion.26), channel_id=1, source_target_pairs={{0,1},{1,0},{2,3},{3,2},{4,5},{5,4},{6,7},{7,6},{8,9},{9,8},{10,11... | collective-permute-start | bytes 1572872 | tf_op jit(solution)/shard_map/ppermute | solution.py:715
  6.7 25.8 %collective-permute-start.4 = (bf16[512,512]{1,0:T(8,128)(2,1)}, bf16[512,512]{1,0:T(8,128)(2,1)}, u32[]{:S(2)}, u32[]{:S(2)}) collective-permute-start(bf16[512,512]{1,0:T(8,128)(2,1)} %pad_maximum_fusion.27), channel_id=1, source_target_pairs={{0,1},{1,0},{2,3},{3,2},{4,5},{5,4},{6,7},{7,6},{8,9},{9,8},{10,11... | collective-permute-start | bytes 1572872 | tf_op jit(solution)/shard_map/ppermute | solution.py:715
  7.7 23.5 %collective-permute-start.2 = (bf16[256,512]{1,0:T(8,128)(2,1)}, bf16[256,512]{1,0:T(8,128)(2,1)}, u32[]{:S(2)}, u32[]{:S(2)}) collective-permute-start(bf16[256,512]{1,0:T(8,128)(2,1)} %get-tuple-element.542), channel_id=1, source_target_pairs={{0,2},{2,0},{1,3},{3,1},{4,6},{6,4},{5,7},{7,5},{8,10},{10,8},{9,1... | collective-permute-start | bytes 786440 | tf_op jit(solution)/shard_map/ppermute | solution.py:708
  7.7 23.5 %collective-permute-start.1 = (bf16[256,512]{1,0:T(8,128)(2,1)}, bf16[256,512]{1,0:T(8,128)(2,1)}, u32[]{:S(2)}, u32[]{:S(2)}) collective-permute-start(bf16[256,512]{1,0:T(8,128)(2,1)} %get-tuple-element.544), channel_id=1, source_target_pairs={{0,2},{2,0},{1,3},{3,1},{4,6},{6,4},{5,7},{7,5},{8,10},{10,8},{9,1... | collective-permute-start | bytes 786440 | tf_op jit(solution)/shard_map/ppermute | solution.py:708
  9.7 35.4 %collective-permute-start.7 = (bf16[512,1024]{1,0:T(8,128)(2,1)}, bf16[512,1024]{1,0:T(8,128)(2,1)}, u32[]{:S(2)}, u32[]{:S(2)}) collective-permute-start(bf16[512,1024]{1,0:T(8,128)(2,1)} %get-tuple-element.498), channel_id=1, source_target_pairs={{0,2},{2,0},{1,3},{3,1},{4,6},{6,4},{5,7},{7,5},{8,10},{10,8},{9,1... | collective-permute-start | bytes 3145736 | tf_op jit(solution)/shard_map/ppermute | solution.py:708
  29.2 15.9 %collective-permute-start.6 = (bf16[1024,1536]{1,0:T(8,128)(2,1)}, bf16[1024,1536]{1,0:T(8,128)(2,1)}, u32[]{:S(2)}, u32[]{:S(2)}) collective-permute-start(bf16[1024,1536]{1,0:T(8,128)(2,1)} %pad_maximum_fusion.5), channel_id=1, source_target_pairs={{0,2},{2,0},{1,3},{3,1},{4,6},{6,4},{5,7},{7,5},{8,10},{10,8},{9,1... | collective-permute-start | bytes 9437192 | tf_op jit(solution)/shard_map/ppermute | solution.py:708
  32.4 6.3 collective-permute-start.3
  67.5 26.8 %collective-permute-start.13 = (bf16[2048,1024]{1,0:T(8,128)(2,1)}, bf16[2048,1024]{1,0:T(8,128)(2,1)}, u32[]{:S(2)}, u32[]{:S(2)}) collective-permute-start(bf16[2048,1024]{1,0:T(8,128)(2,1)} %constant_dynamic-slice_fusion.6), channel_id=1, source_target_pairs={{0,2},{2,0},{1,3},{3,1},{4,6},{6,4},{5,7},{7,5},{8,10},{10,8},{9,1... | collective-permute-start | bytes 12582920 | tf_op jit(solution)/shard_map/ppermute | solution.py:708
  67.8 26.6 %collective-permute-start.11 = (bf16[1024,2048]{1,0:T(8,128)(2,1)}, bf16[1024,2048]{1,0:T(8,128)(2,1)}, u32[]{:S(2)}, u32[]{:S(2)}) collective-permute-start(bf16[1024,2048]{1,0:T(8,128)(2,1)} %constant_dynamic-slice_fusion.16), channel_id=1, source_target_pairs={{0,2},{2,0},{1,3},{3,1},{4,6},{6,4},{5,7},{7,5},{8,10},{10,8},{9,1... | collective-permute-start | bytes 12582920 | tf_op jit(solution)/shard_map/ppermute | solution.py:708
  68.0 26.3 %collective-permute-start.12 = (bf16[1024,2048]{1,0:T(8,128)(2,1)}, bf16[1024,2048]{1,0:T(8,128)(2,1)}, u32[]{:S(2)}, u32[]{:S(2)}) collective-permute-start(bf16[1024,2048]{1,0:T(8,128)(2,1)} %constant_dynamic-slice_fusion.15), channel_id=1, source_target_pairs={{0,2},{2,0},{1,3},{3,1},{4,6},{6,4},{5,7},{7,5},{8,10},{10,8},{9,1... | collective-permute-start | bytes 12582920 | tf_op jit(solution)/shard_map/ppermute | solution.py:708
  68.5 25.9 %collective-permute-start.9 = (bf16[256,2048]{1,0:T(8,128)(2,1)}, bf16[256,2048]{1,0:T(8,128)(2,1)S(1)}, u32[]{:S(2)}, u32[]{:S(2)}) collective-permute-start(bf16[256,2048]{1,0:T(8,128)(2,1)} %get-tuple-element.222), channel_id=1, source_target_pairs={{0,1},{1,0},{2,3},{3,2},{4,5},{5,4},{6,7},{7,6},{8,9},{9,8},{10,11... | collective-permute-start | bytes 3145736 | tf_op jit(solution)/shard_map/ppermute | solution.py:721
  70.9 17.4 %collective-permute-start.10 = (f32[1,1]{1,0:T(1,128)}, f32[1,1]{1,0:T(1,128)}, u32[]{:S(2)}, u32[]{:S(2)}) collective-permute-start(f32[1,1]{1,0:T(1,128)} %bitcast.4), channel_id=1, source_target_pairs={{0,4},{4,0},{8,12},{12,8},{16,20},{20,16},{24,28},{28,24},{1,5},{5... | collective-permute-start | bytes 20 | tf_op jit(solution)/shard_map/ppermute | solution.py:316
  103.2 30.7 %collective-permute-start.18 = (f32[1,1]{1,0:T(1,128)}, f32[1,1]{1,0:T(1,128)}, u32[]{:S(2)}, u32[]{:S(2)}) collective-permute-start(f32[1,1]{1,0:T(1,128)} %add.219), channel_id=1, source_target_pairs={{0,8},{4,12},{8,0},{12,4},{16,24},{20,28},{24,16},{28,20},{1,9},{5... | collective-permute-start | bytes 20 | tf_op jit(solution)/shard_map/ppermute | solution.py:316
  106.3 28.2 %collective-permute-start.16 = (bf16[256,2048]{1,0:T(8,128)(2,1)S(1)}, bf16[256,2048]{1,0:T(8,128)(2,1)S(1)}, u32[]{:S(2)}, u32[]{:S(2)}) collective-permute-start(bf16[256,2048]{1,0:T(8,128)(2,1)S(1)} %get-tuple-element.243), channel_id=1, source_target_pairs={{0,1},{1,0},{2,3},{3,2},{4,5},{5,4},{6,7},{7,6},{8,9},{9,8},{10,11... | collective-permute-start | bytes 3145736 | tf_op jit(solution)/shard_map/ppermute | solution.py:721
  107.8 26.7 %collective-permute-start.17 = (bf16[256,2048]{1,0:T(8,128)(2,1)}, bf16[256,2048]{1,0:T(8,128)(2,1)S(1)}, u32[]{:S(2)}, u32[]{:S(2)}) collective-permute-start(bf16[256,2048]{1,0:T(8,128)(2,1)} %fusion.33.own_rows), channel_id=1, source_target_pairs={{0,4},{4,0},{8,12},{12,8},{16,20},{20,16},{24,28},{28,24},{1,5},{5... | collective-permute-start | bytes 3145736 | tf_op jit(solution)/shard_map/ppermute | solution.py:711
  144.3 29.1 %collective-permute-start.23 = (f32[1,1]{1,0:T(1,128)}, f32[1,1]{1,0:T(1,128)}, u32[]{:S(2)}, u32[]{:S(2)}) collective-permute-start(f32[1,1]{1,0:T(1,128)} %add.226), channel_id=1, source_target_pairs={{0,16},{4,20},{8,24},{12,28},{16,0},{20,4},{24,8},{28,12},{1,17},{... | collective-permute-start | bytes 20 | tf_op jit(solution)/shard_map/ppermute | solution.py:316
  148.2 25.8 %collective-permute-start.21 = (bf16[256,2048]{1,0:T(8,128)(2,1)}, bf16[256,2048]{1,0:T(8,128)(2,1)S(1)}, u32[]{:S(2)}, u32[]{:S(2)}) collective-permute-start(bf16[256,2048]{1,0:T(8,128)(2,1)} %get-tuple-element.261), channel_id=1, source_target_pairs={{0,1},{1,0},{2,3},{3,2},{4,5},{5,4},{6,7},{7,6},{8,9},{9,8},{10,11... | collective-permute-start | bytes 3145736 | tf_op jit(solution)/shard_map/ppermute | solution.py:721
  148.7 25.3 %collective-permute-start.22 = (bf16[256,2048]{1,0:T(8,128)(2,1)S(1)}, bf16[256,2048]{1,0:T(8,128)(2,1)S(1)}, u32[]{:S(2)}, u32[]{:S(2)}) collective-permute-start(bf16[256,2048]{1,0:T(8,128)(2,1)S(1)} %fusion.34.own_rows), channel_id=1, source_target_pairs={{0,4},{4,0},{8,12},{12,8},{16,20},{20,16},{24,28},{28,24},{1,5},{5... | collective-permute-start | bytes 3145736 | tf_op jit(solution)/shard_map/ppermute | solution.py:711
  174.1 9.5 collective-permute-start.26
  184.2 29.4 %collective-permute-start.27 = (bf16[256,2048]{1,0:T(8,128)(2,1)S(1)}, bf16[256,2048]{1,0:T(8,128)(2,1)S(1)}, u32[]{:S(2)}, u32[]{:S(2)}) collective-permute-start(bf16[256,2048]{1,0:T(8,128)(2,1)S(1)} %get-tuple-element.282), channel_id=1, source_target_pairs={{0,1},{1,0},{2,3},{3,2},{4,5},{5,4},{6,7},{7,6},{8,9},{9,8},{10,11... | collective-permute-start | bytes 3145736 | tf_op jit(solution)/shard_map/ppermute | solution.py:721
  185.8 27.9 %collective-permute-start.28 = (bf16[512,1024]{1,0:T(8,128)(2,1)}, bf16[512,1024]{1,0:T(8,128)(2,1)S(1)}, u32[]{:S(2)}, u32[]{:S(2)}) collective-permute-start(bf16[512,1024]{1,0:T(8,128)(2,1)} %get-tuple-element.283), channel_id=1, source_target_pairs={{0,4},{4,0},{8,12},{12,8},{16,20},{20,16},{24,28},{28,24},{1,5},{5... | collective-permute-start | bytes 3145736 | tf_op jit(solution)/shard_map/ppermute | solution.py:711
  213.7 10.0 %collective-permute-start.31 = (bf16[256,2048]{1,0:T(8,128)(2,1)}, bf16[256,2048]{1,0:T(8,128)(2,1)}, u32[]{:S(2)}, u32[]{:S(2)}) collective-permute-start(bf16[256,2048]{1,0:T(8,128)(2,1)} %get-tuple-element.289), channel_id=1, source_target_pairs={{0,2},{2,0},{1,3},{3,1},{4,6},{6,4},{5,7},{7,5},{8,10},{10,8},{9,1... | collective-permute-start | bytes 3145736 | tf_op jit(solution)/shard_map/ppermute | solution.py:708
  218.2 7.8 collective-permute-start.30
  226.1 30.3 %collective-permute-start.34 = (f32[1,1]{1,0:T(1,128)}, f32[1,1]{1,0:T(1,128)}, u32[]{:S(2)}, u32[]{:S(2)}) collective-permute-start(f32[1,1]{1,0:T(1,128)} %bitcast.12), channel_id=1, source_target_pairs={{0,4},{4,0},{8,12},{12,8},{16,20},{20,16},{24,28},{28,24},{1,5},{5... | collective-permute-start | bytes 20 | tf_op jit(solution)/shard_map/ppermute | solution.py:316
  228.0 29.1 %collective-permute-start.32 = (bf16[256,2048]{1,0:T(8,128)(2,1)S(1)}, bf16[256,2048]{1,0:T(8,128)(2,1)S(1)}, u32[]{:S(2)}, u32[]{:S(2)}) collective-permute-start(bf16[256,2048]{1,0:T(8,128)(2,1)S(1)} %get-tuple-element.301), channel_id=1, source_target_pairs={{0,1},{1,0},{2,3},{3,2},{4,5},{5,4},{6,7},{7,6},{8,9},{9,8},{10,11... | collective-permute-start | bytes 3145736 | tf_op jit(solution)/shard_map/ppermute | solution.py:721
  228.5 28.6 %collective-permute-start.33 = (bf16[512,1024]{1,0:T(8,128)(2,1)}, bf16[512,1024]{1,0:T(8,128)(2,1)S(1)}, u32[]{:S(2)}, u32[]{:S(2)}) collective-permute-start(bf16[512,1024]{1,0:T(8,128)(2,1)} %get-tuple-element.302), channel_id=1, source_target_pairs={{0,4},{4,0},{8,12},{12,8},{16,20},{20,16},{24,28},{28,24},{1,5},{5... | collective-permute-start | bytes 3145736 | tf_op jit(solution)/shard_map/ppermute | solution.py:711
  267.3 25.2 %collective-permute-start.37 = (bf16[256,2048]{1,0:T(8,128)(2,1)}, bf16[256,2048]{1,0:T(8,128)(2,1)}, u32[]{:S(2)}, u32[]{:S(2)}) collective-permute-start(bf16[256,2048]{1,0:T(8,128)(2,1)} %get-tuple-element.316), channel_id=1, source_target_pairs={{0,1},{1,0},{2,3},{3,2},{4,5},{5,4},{6,7},{7,6},{8,9},{9,8},{10,11... | collective-permute-start | bytes 3145736 | tf_op jit(solution)/shard_map/ppermute | solution.py:721
  268.8 24.9 %collective-permute-start.38 = (bf16[256,2048]{1,0:T(8,128)(2,1)}, bf16[256,2048]{1,0:T(8,128)(2,1)}, u32[]{:S(2)}, u32[]{:S(2)}) collective-permute-start(bf16[256,2048]{1,0:T(8,128)(2,1)} %get-tuple-element.317.own_rows), channel_id=1, source_target_pairs={{0,4},{4,0},{8,12},{12,8},{16,20},{20,16},{24,28},{28,24},{1,5},{5... | collective-permute-start | bytes 3145736 | tf_op jit(solution)/shard_map/ppermute | solution.py:711
  304.5 31.1 %collective-permute-start.24 = (bf16[256,512]{1,0:T(8,128)(2,1)S(1)}, bf16[256,512]{1,0:T(8,128)(2,1)S(1)}, u32[]{:S(2)}, u32[]{:S(2)}) collective-permute-start(bf16[256,512]{1,0:T(8,128)(2,1)S(1)} %copy-done.123), channel_id=1, source_target_pairs={{0,2},{2,0},{1,3},{3,1},{4,6},{6,4},{5,7},{7,5},{8,10},{10,8},{9,1... | collective-permute-start | bytes 786440 | tf_op jit(solution)/shard_map/ppermute | solution.py:708
  306.5 25.3 %collective-permute-start.40 = (bf16[256,2048]{1,0:T(8,128)(2,1)S(1)}, bf16[256,2048]{1,0:T(8,128)(2,1)S(1)}, u32[]{:S(2)}, u32[]{:S(2)}) collective-permute-start(bf16[256,2048]{1,0:T(8,128)(2,1)S(1)} %copy-done.35), channel_id=1, source_target_pairs={{0,4},{4,0},{8,12},{12,8},{16,20},{20,16},{24,28},{28,24},{1,5},{5... | collective-permute-start | bytes 3145736 | tf_op jit(solution)/shard_map/ppermute | solution.py:711
  332.9 13.8 %collective-permute-start.41 = (bf16[512,2048]{1,0:T(8,128)(2,1)S(1)}, bf16[512,2048]{1,0:T(8,128)(2,1)S(1)}, u32[]{:S(2)}, u32[]{:S(2)}) collective-permute-start(bf16[512,2048]{1,0:T(8,128)(2,1)S(1)} %pad_maximum_fusion.8), channel_id=1, source_target_pairs={{0,2},{2,0},{1,3},{3,1},{4,6},{6,4},{5,7},{7,5},{8,10},{10,8},{9,1... | collective-permute-start | bytes 6291464 | tf_op jit(solution)/shard_map/ppermute | solution.py:708
  348.2 39.4 %collective-permute-start.42 = (bf16[512,1024]{1,0:T(8,128)(2,1)}, bf16[512,1024]{1,0:T(8,128)(2,1)S(1)}, u32[]{:S(2)}, u32[]{:S(2)}) collective-permute-start(bf16[512,1024]{1,0:T(8,128)(2,1)} %get-tuple-element.354), channel_id=1, source_target_pairs={{0,4},{4,0},{8,12},{12,8},{16,20},{20,16},{24,28},{28,24},{1,5},{5... | collective-permute-start | bytes 3145736 | tf_op jit(solution)/shard_map/ppermute | solution.py:711
  348.8 47.4 %collective-permute-start.43 = (bf16[512,1024]{1,0:T(8,128)(2,1)}, bf16[512,1024]{1,0:T(8,128)(2,1)S(1)}, u32[]{:S(2)}, u32[]{:S(2)}) collective-permute-start(bf16[512,1024]{1,0:T(8,128)(2,1)} %get-tuple-element.355), channel_id=1, source_target_pairs={{0,4},{4,0},{8,12},{12,8},{16,20},{20,16},{24,28},{28,24},{1,5},{5... | collective-permute-start | bytes 3145736 | tf_op jit(solution)/shard_map/ppermute | solution.py:711
  361.3 14.2 %collective-permute-start.44 = (f32[1,1]{1,0:T(1,128)}, f32[1,1]{1,0:T(1,128)}, u32[]{:S(2)}, u32[]{:S(2)}) collective-permute-start(f32[1,1]{1,0:T(1,128)} %add.246), channel_id=1, source_target_pairs={{0,8},{4,12},{8,0},{12,4},{16,24},{20,28},{24,16},{28,20},{1,9},{5... | collective-permute-start | bytes 20 | tf_op jit(solution)/shard_map/ppermute | solution.py:316
  403.9 29.4 %collective-permute-start.52 = (bf16[512,1024]{1,0:T(8,128)(2,1)}, bf16[512,1024]{1,0:T(8,128)(2,1)}, u32[]{:S(2)}, u32[]{:S(2)}) collective-permute-start(bf16[512,1024]{1,0:T(8,128)(2,1)} %get-tuple-element.384), channel_id=1, source_target_pairs={{0,4},{4,0},{8,12},{12,8},{16,20},{20,16},{24,28},{28,24},{1,5},{5... | collective-permute-start | bytes 3145736 | tf_op jit(solution)/shard_map/ppermute | solution.py:711
  404.5 18.8 %collective-permute-start.56 = (bf16[256,2048]{1,0:T(8,128)(2,1)S(1)}, bf16[256,2048]{1,0:T(8,128)(2,1)}, u32[]{:S(2)}, u32[]{:S(2)}) collective-permute-start(bf16[256,2048]{1,0:T(8,128)(2,1)S(1)} %get-tuple-element.397), channel_id=1, source_target_pairs={{0,2},{2,0},{1,3},{3,1},{4,6},{6,4},{5,7},{7,5},{8,10},{10,8},{9,1... | collective-permute-start | bytes 3145736 | tf_op jit(solution)/shard_map/ppermute | solution.py:708
  404.5 23.6 %collective-permute-start.57 = (bf16[256,2048]{1,0:T(8,128)(2,1)}, bf16[256,2048]{1,0:T(8,128)(2,1)S(1)}, u32[]{:S(2)}, u32[]{:S(2)}) collective-permute-start(bf16[256,2048]{1,0:T(8,128)(2,1)} %get-tuple-element.399), channel_id=1, source_target_pairs={{0,2},{2,0},{1,3},{3,1},{4,6},{6,4},{5,7},{7,5},{8,10},{10,8},{9,1... | collective-permute-start | bytes 3145736 | tf_op jit(solution)/shard_map/ppermute | solution.py:708
  405.5 46.2 %collective-permute-start.50 = (bf16[1024,1536]{1,0:T(8,128)(2,1)S(1)}, bf16[1024,1536]{1,0:T(8,128)(2,1)S(1)}, u32[]{:S(2)}, u32[]{:S(2)}) collective-permute-start(bf16[1024,1536]{1,0:T(8,128)(2,1)S(1)} %get-tuple-element.458), channel_id=1, source_target_pairs={{0,2},{2,0},{1,3},{3,1},{4,6},{6,4},{5,7},{7,5},{8,10},{10,8},{9,1... | collective-permute-start | bytes 9437192 | tf_op jit(solution)/shard_map/ppermute | solution.py:708
  414.0 15.6 %collective-permute-start.49 = (bf16[512,2048]{1,0:T(8,128)(2,1)}, bf16[512,2048]{1,0:T(8,128)(2,1)S(1)}, u32[]{:S(2)}, u32[]{:S(2)}) collective-permute-start(bf16[512,2048]{1,0:T(8,128)(2,1)} %pad_maximum_fusion.9), channel_id=1, source_target_pairs={{0,2},{2,0},{1,3},{3,1},{4,6},{6,4},{5,7},{7,5},{8,10},{10,8},{9,1... | collective-permute-start | bytes 6291464 | tf_op jit(solution)/shard_map/ppermute | solution.py:708
  423.3 27.8 %collective-permute-start.53 = (bf16[512,1024]{1,0:T(8,128)(2,1)S(1)}, bf16[512,1024]{1,0:T(8,128)(2,1)S(1)}, u32[]{:S(2)}, u32[]{:S(2)}) collective-permute-start(bf16[512,1024]{1,0:T(8,128)(2,1)S(1)} %copy-done.135), channel_id=1, source_target_pairs={{0,4},{4,0},{8,12},{12,8},{16,20},{20,16},{24,28},{28,24},{1,5},{5... | collective-permute-start | bytes 3145736 | tf_op jit(solution)/shard_map/ppermute | solution.py:711
  428.2 23.5 %collective-permute-start.51 = (bf16[512,1024]{1,0:T(8,128)(2,1)S(1)}, bf16[512,1024]{1,0:T(8,128)(2,1)S(1)}, u32[]{:S(2)}, u32[]{:S(2)}) collective-permute-start(bf16[512,1024]{1,0:T(8,128)(2,1)S(1)} %get-tuple-element.488), channel_id=1, source_target_pairs={{0,2},{2,0},{1,3},{3,1},{4,6},{6,4},{5,7},{7,5},{8,10},{10,8},{9,1... | collective-permute-start | bytes 3145736 | tf_op jit(solution)/shard_map/ppermute | solution.py:708
  429.6 59.1 %collective-permute-start.48 = (bf16[1024,1024]{1,0:T(8,128)(2,1)}, bf16[1024,1024]{1,0:T(8,128)(2,1)}, u32[]{:S(2)}, u32[]{:S(2)}) collective-permute-start(bf16[1024,1024]{1,0:T(8,128)(2,1)} %get-tuple-element.464), channel_id=1, source_target_pairs={{0,2},{2,0},{1,3},{3,1},{4,6},{6,4},{5,7},{7,5},{8,10},{10,8},{9,1... | collective-permute-start | bytes 6291464 | tf_op jit(solution)/shard_map/ppermute | solution.py:708
  433.3 512.8 %collective-permute-start.58 = (bf16[256,2048]{1,0:T(8,128)(2,1)}, bf16[256,2048]{1,0:T(8,128)(2,1)}, u32[]{:S(2)}, u32[]{:S(2)}) collective-permute-start(bf16[256,2048]{1,0:T(8,128)(2,1)} %get-tuple-element.422), channel_id=1, source_target_pairs={{0,1},{1,0},{2,3},{3,2},{4,5},{5,4},{6,7},{7,6},{8,9},{9,8},{10,11... | collective-permute-start | bytes 3145736 | tf_op jit(solution)/shard_map/ppermute | solution.py:721
  451.1 495.0 %collective-permute-start.59 = (bf16[256,2048]{1,0:T(8,128)(2,1)}, bf16[256,2048]{1,0:T(8,128)(2,1)S(1)}, u32[]{:S(2)}, u32[]{:S(2)}) collective-permute-start(bf16[256,2048]{1,0:T(8,128)(2,1)} %get-tuple-element.420), channel_id=1, source_target_pairs={{0,1},{1,0},{2,3},{3,2},{4,5},{5,4},{6,7},{7,6},{8,9},{9,8},{10,11... | collective-permute-start | bytes 3145736 | tf_op jit(solution)/shard_map/ppermute | solution.py:721
  478.8 9.9 collective-permute-start.55
  478.8 9.9 collective-permute-start.54
  953.7 42.3 %collective-permute-start.60 = (f32[256,512]{1,0:T(8,128)S(1)}, f32[256,512]{1,0:T(8,128)S(1)}, u32[]{:S(2)}, u32[]{:S(2)}) collective-permute-start(f32[256,512]{1,0:T(8,128)S(1)} %constant_dynamic-slice_fusion.1), channel_id=1, source_target_pairs={{0,2},{2,0},{1,3},{3,1},{4,6},{6,4},{5,7},{7,5},{8,10},{10,8},{9,1... | collective-permute-start | bytes 1572872 | tf_op jit(solution)/shard_map/ppermute | solution.py:708
  955.7 40.5 %collective-permute-start.61 = (f32[256,512]{1,0:T(8,128)S(1)}, f32[256,512]{1,0:T(8,128)S(1)}, u32[]{:S(2)}, u32[]{:S(2)}) collective-permute-start(f32[256,512]{1,0:T(8,128)S(1)} %constant_dynamic-slice_fusion), channel_id=1, source_target_pairs={{0,2},{2,0},{1,3},{3,1},{4,6},{6,4},{5,7},{7,5},{8,10},{10,8},{9,1... | collective-permute-start | bytes 1572872 | tf_op jit(solution)/shard_map/ppermute | solution.py:708
  (154 other events, 2250.0 us)
